TPU v7x, 256 devices: a whole 4x4x8 slice. The times are simulated.
256 devices in a mesh: owner: 64 (over z, y, core), view: 4 (over x).
Axes of the slice: x: 4, y: 4, z: 8, core: 2. Of those that a mesh axis runs over, the one named last changes fastest.
Arguments:
- geometry: float32 [4, 5, 2097152], P('view', None, 'owner'), may hold values from -2 to 40, as said below
- appearance: float32 [4, 2097152], P(None, 'owner'), may hold values from -6 to 6, as said below
- list_owner: int32 [4, 262144, 1], P('view', 'owner'), may hold values from 0 to 63; in each aligned block of 4096 rows (0 to 4095, 4096 to 8191, ..., all dimensions but the last counted through in order) at most 128 rows name the same one
- list_local: int32 [4, 262144], P('view', 'owner'), may hold values from 0 to 32767
- counts: int32 [4, 1024], P('view', 'owner'), may hold values from 1 to 256, 131072 in all within a row
- cotangent: float32 [4, 1024, 3, 256], P('view', 'owner'), may hold values from -6 to 6
Outputs:
- geo_grad: float32 [4, 5, 2097152], P('view', None, 'owner')
- look_grad: float32 [4, 2097152], P(None, 'owner')
Inputs may be any that keep to these rules, and one draw needn't show every extreme that they name: `list_owner`: within the slots of one device's tiles (4096 slots in a row of one view), no owner is named more than 128 times, a bound that some block reaches. `geometry`: rows 0 and 1 lie in [0, 1], rows 2 and 4 in [4, 40], row 3 in [-2, 2]. `appearance`: rows 0 to 2 lie in [-6, 6], row 3 in [-6, -1.5].
All inputs are finite; a program needn't handle non-finite values. No bound on the sum of `counts` on one device may be relied on, other than what follows from the above.
Results may differ from a plain program's by a relative error of at most 0.0003.
Values sent between devices are 32-bit elements; how exact they have to be, the bound alone decides.
No kernel may reach another device: no remote copies, remote signals or barrier semaphores. Data moves between devices by JAX's collectives and lax.ppermute only.
A program may use at most 192 MiB of HBM per device.

v0:
```python
import jax
import jax.numpy as jnp
from jax import lax
from jax.sharding import PartitionSpec as P

K = 256
TS = 16


def render(entries, alive, pixel_x, pixel_y):
    offset_x = pixel_x[:, None] - entries[0][None, :]
    offset_y = pixel_y[:, None] - entries[1][None, :]
    falloff = 0.5 * (
        entries[2][None, :] * offset_x * offset_x
        + 2.0 * entries[3][None, :] * offset_x * offset_y
        + entries[4][None, :] * offset_y * offset_y
    )
    alphas = 0.99 * jax.nn.sigmoid(entries[8])[None, :] * jnp.exp(-falloff) * alive[None, :]
    log_keep = jnp.log1p(-alphas)
    prefix_sum = jnp.cumsum(log_keep, axis=1) - log_keep
    weight = jnp.exp(prefix_sum) * alphas
    return jnp.dot(entries[5:8], weight.T, precision=lax.Precision.HIGHEST)


def shards(geometry, appearance, list_owner, list_local, counts, cotangent):
    owners = lax.axis_size("owner")
    slots_dev = list_local.shape[1]
    capacity = 2 * slots_dev // owners
    tiles_dev = counts.shape[1]
    target_owner = list_owner[0, :, 0]
    local_ids = list_local[0]
    slot_iota = jnp.arange(K, dtype=jnp.int32)
    alive = (slot_iota[None, :] < counts[0][:, None]).astype(jnp.float32)
    used = jnp.ones((slots_dev,), jnp.int32)
    one_hot = (target_owner[:, None] == jnp.arange(owners, dtype=jnp.int32)[None, :]).astype(
        jnp.int32
    ) * used[:, None]
    slot_index = jnp.sum((jnp.cumsum(one_hot, axis=0) - one_hot) * one_hot, axis=1)
    slot_index = jnp.where(used > 0, slot_index, capacity)
    requests = (
        jnp.zeros((owners, capacity), jnp.int32)
        .at[target_owner, slot_index]
        .set(local_ids, mode="drop")
    )
    own_table = jnp.concatenate([geometry[0], appearance], 0)
    received_ids = lax.all_to_all(requests, "owner", split_axis=0, concat_axis=0, tiled=True)
    picked = own_table[:, received_ids]
    fetched = lax.all_to_all(picked, "owner", split_axis=1, concat_axis=1, tiled=True)
    asked_ids = received_ids[None]
    fetch_index = jnp.minimum(slot_index, capacity - 1)
    entries = fetched[:, target_owner, fetch_index] * used.astype(jnp.float32)[None, :]
    entries = jnp.transpose(entries.reshape(9, tiles_dev, K), (1, 0, 2))
    pixel = jnp.arange(TS * TS, dtype=jnp.int32)
    pixel_x = ((pixel % TS).astype(jnp.float32) + 0.5) / TS
    pixel_y = ((pixel // TS).astype(jnp.float32) + 0.5) / TS

    def tile_grad(packed):
        colors, pullback = jax.vjp(
            lambda values: render(values, packed[1], pixel_x, pixel_y), packed[0]
        )
        return pullback(packed[2])[0]

    gradients = lax.map(tile_grad, (entries, alive, cotangent[0]))
    flattened = jnp.transpose(gradients, (1, 0, 2)).reshape(9, slots_dev)
    outgoing = (
        jnp.zeros((9, owners, capacity), jnp.float32)
        .at[:, target_owner, slot_index]
        .set(flattened, mode="drop")
    )
    returned = lax.all_to_all(outgoing, "owner", split_axis=1, concat_axis=1, tiled=True)
    totals = (
        jnp.zeros((9, own_table.shape[1]), jnp.float32)
        .at[:, asked_ids.reshape(-1)]
        .add(returned.reshape(9, -1))
    )
    geo_grad = totals[:5][None]
    look_grad = lax.psum(totals[5:], "view")
    return (geo_grad, look_grad)


def solution(mesh):
    placed = (
        P("view", None, "owner"),
        P(None, "owner"),
        P("view", "owner", None),
        P("view", "owner"),
        P("view", "owner"),
        P("view", "owner", None, None),
    )
    return jax.shard_map(
        shards,
        mesh=mesh,
        in_specs=placed,
        out_specs=(P("view", None, "owner"), P(None, "owner")),
        check_vma=False,
    )
```

profile of v0, /device:TPU:1, one launch (start us, length us, event | category | flops | bytes accessed | tf_op | source)
XLA Modules:
  0.0 732.3 jit_solution(5033152807431286066)
XLA Ops:
  8.1 18.4 %reduce-window.20 = s32[64,32,128]{2,1,0:T(8,128)S(1)} reduce-window(s32[64,32,128]{2,1,0:T(8,128)S(1)} %fusion.62, s32[]{:T(128)} %constant.78.clone.1), window={size=1x1x128 pad=0_0x0_0x127_0}, to_apply=%region_0.0 | reduce-window | flops 33292288 | bytes 2097156 | tf_op jit(solution)/shard_map/reduce-window.4
  29.2 16.3 %scatter_custom_fusion.1 = s32[8192]{0:T(1024)} fusion(s32[4096]{0:T(1024)S(1)} %broadcast_select_fusion, s32[4096]{0:T(1024)} %bitcast.259, s32[]{:T(128)} %constant.78.clone.1), kind=kCustom, calls=%fused_computation.135 | custom fusion | bytes 33280
  45.4 13.2 %all-to-all-start = ((s32[64,1,128]{2,1,0:T(1,128)}), s32[64,1,128]{2,1,0:T(1,128)S(1)}, u32[]{:S(2)}, u32[]{:S(2)}) async-start(s32[64,1,128]{2,1,0:T(1,128)} %bitcast.8), calls=%async_computation | async-start | bytes 65536 | tf_op jit(solution)/shard_map/all_to_all | solution.py:46
  59.3 8.8 %copy.81 = f32[9,32768]{0,1:T(8,128)} copy(f32[9,32768]{1,0:T(8,128)S(1)} %pad_maximum_fusion) | data formatting | bytes 2359296 | tf_op jit(solution)/shard_map/concatenate | solution.py:45
  68.2 33.5 %gather_fusion = f32[8192,9]{1,0:T(8,128)} fusion(f32[9,32768]{0,1:T(8,128)} %copy.81, s32[8192]{0:T(1024)S(1)} %fusion.64), kind=kCustom, calls=%fused_computation | custom fusion | bytes 622592 | tf_op jit(solution)/shard_map/gather | solution.py:47
  101.7 3.6 copy.82
  105.2 10.3 %all-to-all-start.1 = ((f32[9,64,128]{2,0,1:T(8,128)}), f32[9,64,128]{2,0,1:T(8,128)S(1)}, u32[]{:S(2)}, u32[]{:S(2)}) async-start(f32[9,64,128]{2,0,1:T(8,128)} %bitcast.15), calls=%async_computation.1 | async-start | bytes 1048576 | tf_op jit(solution)/shard_map/all_to_all | solution.py:48
  115.7 17.6 %all-to-all-done.1 = f32[9,64,128]{2,0,1:T(8,128)S(1)} async-done(((f32[9,64,128]{2,0,1:T(8,128)}), f32[9,64,128]{2,0,1:T(8,128)S(1)}, u32[]{:S(2)}, u32[]{:S(2)}) %all-to-all-start.1) | async-done | bytes 294944 | tf_op jit(solution)/shard_map/all_to_all | solution.py:48
  133.2 2.6 copy.83
  135.9 40.5 %gather_fusion.1 = f32[4096,9]{1,0:T(8,128)S(1)} fusion(f32[9,64,128]{0,2,1:T(8,128)} %copy.83, s32[4096]{0:T(1024)S(1)} %bitcast.201), kind=kCustom, calls=%fused_computation.1 | custom fusion | bytes 327680 | tf_op jit(solution)/shard_map/gather | solution.py:51
  177.0 125.4 %while.12 = (s32[]{:T(128)}, f32[16,9,256]{2,1,0:T(8,128)S(1)}, f32[16,3,256]{2,1,0:T(4,128)S(1)}, f32[16,9,256]{2,1,0:T(8,128)S(1)}, f32[16,256]{1,0:T(8,128)S(...) while((s32[]{:T(128)}, f32[16,9,256]{2,1,0:T(8,128)S(1)}, ...), condition=%wide.region_15.16_spmd.clone.clone, body=%wide.region_4.15_spmd.clone.clone.sunk | while | flops 28988424 | bytes 6737149 | solution.py:63
  177.8 1.0 fusion.87
  178.9 1.4 exponential_multiply_fusion.2
  180.9 2.3 fusion.88
  185.6 1.0 fusion.87
  186.7 1.4 exponential_multiply_fusion.2
  188.8 2.3 fusion.88
  193.5 1.0 fusion.87
  194.6 1.4 exponential_multiply_fusion.2
  196.6 2.3 fusion.88
  201.3 1.0 fusion.87
  202.4 1.4 exponential_multiply_fusion.2
  204.4 2.3 fusion.88
  209.2 1.0 fusion.87
  210.3 1.4 exponential_multiply_fusion.2
  212.3 2.3 fusion.88
  217.0 1.0 fusion.87
  218.1 1.4 exponential_multiply_fusion.2
  220.1 2.3 fusion.88
  224.8 1.0 fusion.87
  225.9 1.4 exponential_multiply_fusion.2
  228.0 2.3 fusion.88
  232.7 1.0 fusion.87
  233.8 1.4 exponential_multiply_fusion.2
  235.8 2.3 fusion.88
  240.5 1.0 fusion.87
  241.6 1.4 exponential_multiply_fusion.2
  243.6 2.3 fusion.88
  248.4 1.0 fusion.87
  249.5 1.4 exponential_multiply_fusion.2
  251.5 2.3 fusion.88
  257.3 1.4 exponential_multiply_fusion.2
  259.3 2.3 fusion.88
  265.1 1.4 exponential_multiply_fusion.2
  267.2 2.3 fusion.88
  273.0 1.4 exponential_multiply_fusion.2
  275.0 2.3 fusion.88
  280.8 1.4 exponential_multiply_fusion.2
  282.8 2.3 fusion.88
  288.7 1.4 exponential_multiply_fusion.2
  290.7 2.3 fusion.88
  296.5 1.4 exponential_multiply_fusion.2
  298.5 2.3 fusion.88
  303.3 12.8 %scatter_custom_fusion.2 = f32[9,8192]{0,1:T(8,128)} fusion(s32[4096]{0:T(1024)S(1)} %broadcast_select_fusion, f32[4096,9]{1,0:T(8,128)S(1)} %copy.86, f32[]{:T(128)} %constant.77.clone.1), kind=kCustom, calls=%fused_computation.110 | custom fusion | bytes 294916
  316.1 3.6 copy.87
  319.6 5.8 all-to-all-start.2
  325.7 17.4 %all-to-all-done.2 = f32[9,64,128]{2,0,1:T(8,128)S(1)} async-done(((f32[9,64,128]{2,0,1:T(8,128)}), f32[9,64,128]{2,0,1:T(8,128)S(1)}, u32[]{:S(2)}, u32[]{:S(2)}) %all-to-all-start.2) | async-done | bytes 294944 | tf_op jit(solution)/shard_map/all_to_all | solution.py:70
  343.6 2.6 copy.89
  346.2 57.5 %scatter_custom_fusion = f32[9,32768]{0,1:T(8,128)} fusion(s32[8192]{0:T(1024)S(1)} %bitcast.257, f32[8192,9]{1,0:T(8,128)} %copy.89, f32[]{:T(128)} %constant.77.clone.1), kind=kCustom, calls=%fused_computation.107 | custom fusion | flops 73728 | bytes 1180160 | tf_op jit(solution)/shard_map/scatter-add | solution.py:74
  403.7 12.7 %slice.93 = f32[4,32768]{0,1:T(8,128)} slice(f32[9,32768]{0,1:T(8,128)} %scatter_custom_fusion), slice={[5:9], [0:32768]} | slice | bytes 1048576 | tf_op jit(solution)/shard_map/slice | solution.py:77
  416.5 11.8 %slice_bitcast_fusion.2 = f32[1,5,32768]{1,2,0:T(8,128)} fusion(f32[9,32768]{0,1:T(8,128)} %scatter_custom_fusion), kind=kLoop, calls=%fused_computation.106 | loop fusion | bytes 1310720 | tf_op jit(solution)/shard_map/broadcast_in_dim | solution.py:76
  428.2 10.8 %copy.90 = f32[1,5,32768]{2,0,1:T(1,128)} copy(f32[1,5,32768]{1,2,0:T(8,128)} %slice_bitcast_fusion.2) | data formatting | bytes 1310720
  439.0 276.6 %all-reduce.9.cloned.1.call-done = f32[4,32768]{0,1:T(8,128)} async-done(((f32[4,32768]{0,1:T(8,128)}), f32[4,32768]{0,1:T(8,128)}) %all-reduce.9.cloned.1.call-update) | async-done | bytes 524304 | tf_op jit(solution)/shard_map/psum | solution.py:77
  715.6 9.8 %copy.91 = f32[4,32768]{1,0:T(4,128)} copy(f32[4,32768]{0,1:T(8,128)} %all-reduce.9.cloned.1.call-done) | data formatting | bytes 1048576
  (544 shorter events, 60.9 us)
Async XLA Ops:
  7.2 20.7 %copy-start.2 = (s32[1,4096,1]{1,2,0:T(1,128)S(1)}, s32[1,4096,1]{1,2,0:T(1,128)}, u32[]{:S(2)}) copy-start(s32[1,4096,1]{1,2,0:T(1,128)} %param.10) | copy-start | bytes 49156
  8.1 20.8 %copy-start.5 = (s32[2]{0:T(128)S(1)}, s32[2]{0:T(128)}, u32[]{:S(2)}) copy-start(s32[2]{0:T(128)} %constant.109) | copy-start | bytes 28
  8.1 20.9 %copy-start.4 = (s32[2]{0:T(128)S(1)}, s32[2]{0:T(128)}, u32[]{:S(2)}) copy-start(s32[2]{0:T(128)} %constant.112) | copy-start | bytes 28
  8.1 50.5 %copy-start = (f32[1,5,32768]{2,0,1:T(1,128)S(1)}, f32[1,5,32768]{2,0,1:T(1,128)}, u32[]{:S(2)}) copy-start(f32[1,5,32768]{2,0,1:T(1,128)} %param.8) | copy-start | bytes 1966084
  26.6 32.5 %copy-start.1 = (f32[4,32768]{1,0:T(4,128)S(1)}, f32[4,32768]{1,0:T(4,128)}, u32[]{:S(2)}) copy-start(f32[4,32768]{1,0:T(4,128)} %param.9) | copy-start | bytes 1572868
  45.4 22.7 %all-to-all-start = ((s32[64,1,128]{2,1,0:T(1,128)}), s32[64,1,128]{2,1,0:T(1,128)S(1)}, u32[]{:S(2)}, u32[]{:S(2)}) async-start(s32[64,1,128]{2,1,0:T(1,128)} %bitcast.8), calls=%async_computation | async-start | bytes 65536 | tf_op jit(solution)/shard_map/all_to_all | solution.py:46
  68.2 47.4 %copy-start.3 = (f32[1,16,3,256]{3,1,2,0:T(8,128)S(1)}, f32[1,16,3,256]{3,1,2,0:T(8,128)}, u32[]{:S(2)}) copy-start(f32[1,16,3,256]{3,1,2,0:T(8,128)} %param.13) | copy-start | bytes 147460
  68.2 47.4 %copy-start.6 = (s32[1,16]{1,0:T(1,128)S(1)}, s32[1,16]{1,0:T(1,128)}, u32[]{:S(2)}) copy-start(s32[1,16]{1,0:T(1,128)} %param.12) | copy-start | bytes 196
  105.2 28.0 %all-to-all-start.1 = ((f32[9,64,128]{2,0,1:T(8,128)}), f32[9,64,128]{2,0,1:T(8,128)S(1)}, u32[]{:S(2)}, u32[]{:S(2)}) async-start(f32[9,64,128]{2,0,1:T(8,128)} %bitcast.15), calls=%async_computation.1 | async-start | bytes 1048576 | tf_op jit(solution)/shard_map/all_to_all | solution.py:48
  319.6 23.5 %all-to-all-start.2 = ((f32[9,64,128]{2,0,1:T(8,128)}), f32[9,64,128]{2,0,1:T(8,128)S(1)}, u32[]{:S(2)}, u32[]{:S(2)}) async-start(f32[9,64,128]{2,0,1:T(8,128)} %copy.87), calls=%async_computation.2 | async-start | bytes 1048576 | tf_op jit(solution)/shard_map/all_to_all | solution.py:70
  325.4 390.2 %all-reduce.9.cloned.1.call-start = ((), (), s32[]{:S(2)}) async-start(), calls=%async_computation.3 | async-start | bytes 33554432 | tf_op jit(solution)/shard_map/psum | solution.py:77
Sparse Core Ops, SparseCore 0:
  416.6 298.9 all-reduce.8
where the time goes:
time: 733 us; the launch traced here: 732 us
  waiting for transfers between devices  312 us (43%)
  local copies, waits for them, and re-layouts  186 us (25%)
  other arithmetic  174 us (24%)
  starting transfers between devices  29.5 us (4%)
  between operations  14.3 us (2%)
  matrix products  14.2 us (2%)
    psum x1, waiting for transfers between devices, shards(): look_grad = lax.psum(totals[5:], 'view')  277 us
    another operation x83, other arithmetic  73.7 us
    scatter-add x1, other arithmetic, shards(): totals = jnp.zeros((9, own_table.shape[1]), jnp.float32).at[:, asked_ids....  57.5 us
    unnamed x24, local copies, waits for them, and re-layouts  50.7 us
    gather x1, local copies, waits for them, and re-layouts, shards(): fetched[:, target_owner, fetch_index] * used.astype(jnp.float32)[None, :]  40.5 us
    gather x2, local copies, waits for them, and re-layouts, shards(): picked = own_table[:, received_ids]  37 us
    mul x16, other arithmetic, render(): weight = jnp.exp(prefix_sum) * alphas  21.8 us
    all_to_all x1, waiting for transfers between devices, shards(): lax.all_to_all(picked, 'owner', split_axis=1, concat_axis=1, tiled=True)  17.6 us
  transfers between devices with their start and end apart: 4, of which 3 were waited for; matrix products, arithmetic and copies ran while one was open for 4% of the time, Pallas kernels for 0%

commit v1 on v0

v1 whole, which is shorter than its diff:
```python
import functools

import jax
import jax.numpy as jnp
from jax import lax
from jax.experimental import pallas as pl
from jax.experimental.pallas import tpu as pltpu
from jax.sharding import PartitionSpec as P

K = 256
TS = 16
LANES = 128
LOW = 64
F32 = jnp.float32
BF16 = jnp.bfloat16
LOG2E = 1.4426950408889634


def split2(x):
    high = x.astype(BF16)
    return high, (x - high.astype(F32)).astype(BF16)


def split3(x):
    high = x.astype(BF16)
    rest = x - high.astype(F32)
    middle = rest.astype(BF16)
    return high, middle, (rest - middle.astype(F32)).astype(BF16)


def dot_nn(a, b):
    return lax.dot_general(a, b, (((1,), (0,)), ((), ())), preferred_element_type=F32)


def dot_nt(a, b):
    return lax.dot_general(a, b, (((1,), (1,)), ((), ())), preferred_element_type=F32)


def row_iota(rows, columns):
    return lax.broadcasted_iota(jnp.int32, (rows, columns), 0)


def lane_iota(rows, columns):
    return lax.broadcasted_iota(jnp.int32, (rows, columns), 1)


def named_mask(owner_row, count, owners):
    live = lane_iota(1, K) < count
    shown = jnp.where(live, owner_row, -1)
    return row_iota(owners, K) == shown


def plan_kernel(counts_ref, owner_ref, local_ref, request_ref, rank_ref):
    tiles = owner_ref.shape[0]
    owners = request_ref.shape[0]
    before = (row_iota(K, K) < lane_iota(K, K)).astype(BF16)
    carry = jnp.zeros((owners, 1), F32)
    total = jnp.zeros((owners, 2 * LANES), F32)
    for t in range(tiles):
        named = named_mask(owner_ref[t : t + 1, :], counts_ref[0, t], owners).astype(F32)
        named_half = named.astype(BF16)
        inside = dot_nn(named_half, before)
        rank = jnp.sum(named * (inside + carry), axis=0, keepdims=True).astype(jnp.int32)
        carry = carry + jnp.sum(named, axis=1, keepdims=True)
        rank_ref[t : t + 1, :] = rank
        ids = local_ref[t : t + 1, :] + 1
        at_rank = row_iota(LANES, K) == rank
        high = jnp.where(at_rank, (ids >> 7).astype(F32), 0.0).astype(BF16)
        low = jnp.where(at_rank, (ids & 127).astype(F32), 0.0).astype(BF16)
        total = total + dot_nt(named_half, jnp.concatenate([high, low], 0))
    request_ref[...] = (total[:, :LANES] * 128.0 + total[:, LANES:]).astype(jnp.int32) - 1


def pair_row(ref, at):
    both = ref[pl.ds(at, 2), :]
    return jnp.concatenate([both[0:1, :], both[1:2, :]], 1)


def high_part(ids):
    part = (ids >> 7) + jnp.where((ids & LOW) != 0, 256, 0)
    return jnp.where(ids < 0, -1, part)


def gather_kernel(ids_ref, geo_ref, app_ref, out_ref, table_ref):
    owners = ids_ref.shape[0]
    for c in range(9):
        values = geo_ref[c] if c < 5 else app_ref[c - 5]
        high, low = split2(values.T)
        table_ref[c * LOW : (c + 1) * LOW, :] = jnp.concatenate(
            [high[:LOW], high[LOW:], low[:LOW], low[LOW:]], 1
        )

    def group(g, _):
        blocks = []
        for j in range(4):
            ids = pair_row(ids_ref, pl.multiple_of(g * 8, 8) + 2 * j)
            hot = (row_iota(512, 256) == high_part(ids)).astype(F32).astype(BF16)
            found = dot_nn(table_ref[...], jnp.concatenate([hot, hot], 0))
            mask = row_iota(LOW, 256) == (ids & (LOW - 1))
            rows = [
                jnp.sum(jnp.where(mask, found[c * LOW : (c + 1) * LOW], 0.0), axis=0, keepdims=True)
                for c in range(9)
            ]
            values = jnp.concatenate(rows, 0)
            blocks += [values[:, :LANES], values[:, LANES:]]
        out_ref[pl.ds(pl.multiple_of(g * 72, 8), 72), :] = jnp.concatenate(blocks, 0)
        return 0

    lax.fori_loop(0, owners // 8, group, 0)


def pixel_rows():
    pixel = lane_iota(1, K)
    u = ((pixel & (TS - 1)).astype(F32) + 0.5) / TS - 0.5
    v = ((pixel >> 4).astype(F32) + 0.5) / TS - 0.5
    one = jnp.ones((1, K), F32)
    zero = jnp.zeros((2, K), F32)
    return jnp.concatenate([u * u, u * v, v * v, u, v, one, zero], 0)


def tile_kernel(
    counts_ref, owner_ref, rank_ref, cot_ref, fetched_ref, out_ref, table_ref, grad_ref, dots_ref
):
    tiles = owner_ref.shape[0]
    owners = fetched_ref.shape[0] // 9
    for c in range(9):
        high, low = split2(fetched_ref[pl.ds(c, owners, stride=9), :])
        table_ref[c * owners : (c + 1) * owners, :] = jnp.concatenate([high, low], 1)
    grad_ref[...] = jnp.zeros_like(grad_ref)
    pixels = pixel_rows()
    monomials = pixels.astype(BF16)
    pixel_columns = jnp.concatenate([pixels] * 4, 0).T.astype(BF16)
    before = (row_iota(K, K) < lane_iota(K, K)).astype(BF16)
    after = (row_iota(K, K) > lane_iota(K, K)).astype(BF16)
    dots_ref[0:K] = before
    dots_ref[K : 2 * K] = before
    dots_ref[2 * K : 3 * K] = after
    dots_ref[3 * K : 4 * K] = after

    def one_tile(t, _):
        named = named_mask(owner_ref[pl.ds(t, 1), :], counts_ref[0, t], owners)
        at_rank = (row_iota(LANES, K) == rank_ref[pl.ds(t, 1), :]).astype(F32).astype(BF16)
        spread = dot_nn(table_ref[...], jnp.concatenate([at_rank, at_rank], 0))
        entries = [
            jnp.sum(
                jnp.where(named, spread[c * owners : (c + 1) * owners], 0.0), axis=0, keepdims=True
            )
            for c in range(9)
        ]
        cx, cy, a, b, c2 = entries[0] - 0.5, entries[1] - 0.5, entries[2], entries[3], entries[4]
        opacity = 1.0 / (1.0 + jnp.exp(-entries[8]))
        live = lane_iota(1, K) < counts_ref[0, t]
        ax, ay = a * cx + b * cy, b * cx + c2 * cy
        base = jnp.log(0.99 * opacity) * LOG2E - (0.5 * LOG2E) * (ax * cx + ay * cy)
        zero = jnp.zeros((2, K), F32)
        coefs = jnp.concatenate(
            [
                (-0.5 * LOG2E) * a,
                -LOG2E * b,
                (-0.5 * LOG2E) * c2,
                LOG2E * ax,
                LOG2E * ay,
                jnp.where(live, base, -400.0),
                zero,
            ],
            0,
        )
        parts = split3(coefs)
        exponent = dot_nn(
            pixel_columns, jnp.concatenate([*parts, jnp.zeros((8, K), BF16)], 0)
        )
        alphas = jnp.exp2(exponent)
        log_keep = jnp.log(1.0 - alphas)
        prefix = dot_nn(jnp.concatenate(split2(log_keep), 1), dots_ref[0 : 2 * K])
        weight = jnp.exp(prefix) * alphas
        cot_high, cot_low = split2(cot_ref[t])
        ch, cl = cot_high.astype(F32), cot_low.astype(F32)
        pad = jnp.zeros((4, K), F32)
        cot_columns = jnp.concatenate([ch, ch, cl, cl, pad], 0).T.astype(BF16)
        colors = jnp.concatenate(entries[5:8], 0)
        color_high, color_low = split2(colors)
        kh, kl = color_high.astype(F32), color_low.astype(F32)
        slopes = dot_nn(cot_columns, jnp.concatenate([kh, kl, kh, kl, pad], 0).astype(BF16))
        pull = weight * slopes
        suffix = dot_nn(jnp.concatenate(split2(pull), 1), dots_ref[2 * K : 4 * K])
        q = pull - alphas * jnp.exp(-log_keep) * suffix
        q_high, q_low = split2(q)
        moments = dot_nn(monomials, q_high) + dot_nn(monomials, q_low)
        w_high, w_low = split2(weight)
        cot_rows = jnp.concatenate([ch, cl, jnp.zeros((2, K), F32)], 0).astype(BF16)
        tints = dot_nn(cot_rows, w_high) + dot_nn(cot_rows, w_low)
        tints = tints[0:3] + tints[3:6]
        mxx, mxy, myy, mx, my, m0 = [moments[i : i + 1] for i in range(6)]
        sx, sy = mx - cx * m0, my - cy * m0
        sxx = mxx - cx * (mx + sx)
        sxy = mxy - cx * my - cy * sx
        syy = myy - cy * (my + sy)
        rows = [
            a * sx + b * sy,
            b * sx + c2 * sy,
            -0.5 * sxx,
            -sxy,
            -0.5 * syy,
            tints[0:1],
            tints[1:2],
            tints[2:3],
            (1.0 - opacity) * m0,
        ]
        placed = []
        for row in rows:
            row_high = row.astype(BF16).astype(F32)
            high = jnp.where(named, row_high, 0.0).astype(BF16)
            low = jnp.where(named, row - row_high, 0.0).astype(BF16)
            placed.append(jnp.concatenate([high, low], 1))
        grad_ref[...] += dot_nt(
            jnp.concatenate(placed, 0), jnp.concatenate([at_rank, at_rank], 1)
        )
        return 0

    lax.fori_loop(0, tiles, one_tile, 0)
    for c in range(9):
        out_ref[pl.ds(c, owners, stride=9), :] = grad_ref[c * owners : (c + 1) * owners, :]


def scatter_kernel(first, number, ids_ref, vals_ref, out_ref, acc_ref):
    owners = ids_ref.shape[0]
    acc_ref[...] = jnp.zeros_like(acc_ref)

    def group(g, _):
        values = vals_ref[pl.ds(pl.multiple_of(g * 72, 8), 72), :]
        sides, hots = [], []
        for j in range(4):
            ids = pair_row(ids_ref, pl.multiple_of(g * 8, 8) + 2 * j)
            hot = (row_iota(512, 256) == high_part(ids)).astype(F32).astype(BF16)
            mask = row_iota(LOW, 256) == (ids & (LOW - 1))
            stacked = []
            for c in range(first, first + number):
                at = 18 * j + c
                row = jnp.concatenate([values[at : at + 1], values[at + 9 : at + 10]], 1)
                row_high = row.astype(BF16).astype(F32)
                high = jnp.where(mask, row_high, 0.0).astype(BF16)
                low = jnp.where(mask, row - row_high, 0.0).astype(BF16)
                stacked.append(jnp.concatenate([high, low], 1))
            sides.append(jnp.concatenate(stacked, 0))
            hots += [hot, hot]
        acc_ref[...] += dot_nt(jnp.concatenate(sides, 1), jnp.concatenate(hots, 1))
        return 0

    lax.fori_loop(0, owners // 8, group, 0)
    for c in range(number):
        part = acc_ref[c * LOW : (c + 1) * LOW, :]
        out_ref[c] = jnp.concatenate([part[:, :256], part[:, 256:]], 0).T


VMEM = pl.BlockSpec(memory_space=pltpu.VMEM)
SMEM = pl.BlockSpec(memory_space=pltpu.SMEM)
LIMIT = pltpu.CompilerParams(vmem_limit_bytes=40 * 1024 * 1024)


def exchange(values, owners, axis="owner"):
    sent = values.reshape(owners, 1, -1)
    got = lax.all_to_all(sent, axis, split_axis=0, concat_axis=0, tiled=True)
    return got.reshape(values.shape)


def shards(geometry, appearance, list_owner, list_local, counts, cotangent):
    owners = lax.axis_size("owner")
    tiles = counts.shape[1]
    gauss = geometry.shape[2]
    target = list_owner.reshape(tiles, K)
    local = list_local.reshape(tiles, K)
    requests, ranks = pl.pallas_call(
        plan_kernel,
        out_shape=(
            jax.ShapeDtypeStruct((owners, LANES), jnp.int32),
            jax.ShapeDtypeStruct((tiles, K), jnp.int32),
        ),
        in_specs=[SMEM, VMEM, VMEM],
        out_specs=(VMEM, VMEM),
        compiler_params=LIMIT,
    )(counts, target, local)
    ids = exchange(requests, owners)
    picked = pl.pallas_call(
        gather_kernel,
        out_shape=jax.ShapeDtypeStruct((owners * 9, LANES), F32),
        in_specs=[VMEM, VMEM, VMEM],
        out_specs=VMEM,
        scratch_shapes=[pltpu.VMEM((9 * LOW, 1024), BF16)],
        compiler_params=LIMIT,
    )(ids, geometry.reshape(5, gauss // LANES, LANES), appearance.reshape(4, gauss // LANES, LANES))
    fetched = exchange(picked, owners)
    outgoing = pl.pallas_call(
        tile_kernel,
        out_shape=jax.ShapeDtypeStruct((owners * 9, LANES), F32),
        in_specs=[SMEM, VMEM, VMEM, VMEM, VMEM],
        out_specs=VMEM,
        scratch_shapes=[
            pltpu.VMEM((9 * owners, 2 * LANES), BF16),
            pltpu.VMEM((9 * owners, LANES), F32),
            pltpu.VMEM((4 * K, K), BF16),
        ],
        compiler_params=LIMIT,
    )(counts, target, ranks, cotangent[0], fetched)
    returned = exchange(outgoing, owners)

    def scatter(first, number):
        return pl.pallas_call(
            functools.partial(scatter_kernel, first, number),
            out_shape=jax.ShapeDtypeStruct((number, gauss // LANES, LANES), F32),
            in_specs=[VMEM, VMEM],
            out_specs=VMEM,
            scratch_shapes=[pltpu.VMEM((number * LOW, 512), F32)],
            compiler_params=LIMIT,
        )(ids, returned)

    look = lax.psum(scatter(5, 4), "view")
    geo = scatter(0, 5)
    return (geo.reshape(1, 5, gauss), look.reshape(4, gauss))


def solution(mesh):
    placed = (
        P("view", None, "owner"),
        P(None, "owner"),
        P("view", "owner", None),
        P("view", "owner"),
        P("view", "owner"),
        P("view", "owner", None, None),
    )
    return jax.shard_map(
        shards,
        mesh=mesh,
        in_specs=placed,
        out_specs=(P("view", None, "owner"), P(None, "owner")),
        check_vma=False,
    )
```

time: 733 us -> 171 us (0.23)
  waiting for transfers between devices: 312 us -> 55.6 us
  local copies, waits for them, and re-layouts: 186 us -> 5.95 us
  other arithmetic: 174 us -> 2.81 us
  Pallas kernels: 0 us -> 54.6 us
  blocking collectives: 0 us -> 18.4 us
  matrix products: 14.2 us -> 0 us
  starting transfers between devices: 29.5 us -> 18.1 us
    psum x1, waiting for transfers between devices: 277 us -> 33.6 us  [shards(): look = lax.psum(scatter(5, 4), 'view')]
    gather x3 -> x0, local copies, waits for them, and re-layouts: 77.5 us -> none  [the longest x1 40.5 us: shards(): fetched[:, target_owner, fetch_index] * used.astype(jnp.float32)[None, :]]
    another operation x83 -> x0, other arithmetic: 73.7 us -> none
    scatter-add x1 -> x0, other arithmetic: 57.5 us -> none  [shards(): totals = jnp.zeros((9, own_table.shape[1]), jnp.float32).at[:, asked_ids....]
    pallas_call x0 -> x5, Pallas kernels: none -> 54.6 us  [the longest x1 23.6 us: shards(): pl.pallas_call(tile_kernel, out_shape=jax.ShapeDtypeStruct((owners * 9, L...]
    unnamed x24 -> x13, local copies, waits for them, and re-layouts: 50.7 us -> 5.94 us
    mul x96 -> x0, other arithmetic: 29.8 us -> none  [the longest x16 21.8 us: render(): weight = jnp.exp(prefix_sum) * alphas]
    all_to_all x0 -> x1, blocking collectives: none -> 18.4 us  [exchange(): got = lax.all_to_all(sent, axis, split_axis=0, concat_axis=0, tiled=True)]
  transfers between devices with their start and end apart: 4 -> 3, of which waited for: 3 -> 3; matrix products, arithmetic and copies ran while one was open for 4% -> 1% of each run, Pallas kernels for 0% -> 5%
where the time goes in v1:
time: 171 us; the launch traced here: 170 us
  waiting for transfers between devices  55.6 us (33%)
  Pallas kernels  54.6 us (32%)
  blocking collectives  18.4 us (11%)
  starting transfers between devices  18.1 us (11%)
  between operations  14.1 us (8%)
  local copies, waits for them, and re-layouts  5.95 us (3%)
  other arithmetic  2.81 us (2%)
    psum x1, waiting for transfers between devices, shards(): look = lax.psum(scatter(5, 4), 'view')  33.6 us
    pallas_call x1, Pallas kernels, shards(): pl.pallas_call(tile_kernel, out_shape=jax.ShapeDtypeStruct((owners * 9, L...  23.6 us
    all_to_all x2, waiting for transfers between devices, exchange(): got = lax.all_to_all(sent, axis, split_axis=0, concat_axis=0, tiled=True)  21.9 us
    all_to_all x1, blocking collectives, exchange(): got = lax.all_to_all(sent, axis, split_axis=0, concat_axis=0, tiled=True)  18.4 us
    all_to_all x2, starting transfers between devices, exchange(): got = lax.all_to_all(sent, axis, split_axis=0, concat_axis=0, tiled=True)  18 us
    pallas_call x2, Pallas kernels, scatter(): pl.pallas_call(functools.partial(scatter_kernel, first, number), out_shap...  14.5 us
    pallas_call x1, Pallas kernels, shards(): pl.pallas_call(gather_kernel, out_shape=jax.ShapeDtypeStruct((owners * 9,...  13.3 us
    unnamed x13, local copies, waits for them, and re-layouts  5.94 us
  transfers between devices with their start and end apart: 3, of which 3 were waited for; matrix products, arithmetic and copies ran while one was open for 1% of the time, Pallas kernels for 5%

profile of v1, /device:TPU:1, one launch (start us, length us, event | category | flops | bytes accessed | tf_op | source)
XLA Modules:
  0.0 169.5 jit_solution(17767628819842910082)
XLA Ops:
  7.2 0.0 copy-start
  7.2 0.5 broadcast.6
  7.7 1.4 reduce.6
  9.1 1.4 reduce.7
  10.5 0.0 copy-start.1
  10.5 0.6 copy-done.1
  11.2 3.2 %shard_map.77 = (s32[64,128]{1,0:T(8,128)}, s32[16,256]{1,0:T(8,128)S(1)}) custom-call(s32[1,16]{1,0:T(1,128)S(1)} %copy-done.1, s32[16,256]{1,0:T(8,128)S(1)} %reshape.40.owner_ref, s32[16,256]{1,0:T(8,128)S(1)} %reshape.41.local_ref), custom_call_target="tpu_custom_call" | custom-call | tf_op jit(solution)/shard_map/pallas_call | solution.py:272
  14.4 13.2 %all-to-all-start = ((s32[64,1,128]{2,1,0:T(1,128)}), s32[64,1,128]{2,1,0:T(1,128)S(1)}, u32[]{:S(2)}, u32[]{:S(2)}) async-start(s32[64,1,128]{2,1,0:T(1,128)} %bitcast.1), calls=%async_computation | async-start | bytes 65536 | tf_op jit(solution)/shard_map/all_to_all | solution.py:262
  27.6 1.1 copy.23
  28.7 8.2 %all-to-all-done = s32[64,1,128]{2,1,0:T(1,128)S(1)} async-done(((s32[64,1,128]{2,1,0:T(1,128)}), s32[64,1,128]{2,1,0:T(1,128)S(1)}, u32[]{:S(2)}, u32[]{:S(2)}) %all-to-all-start) | async-done | bytes 32800 | tf_op jit(solution)/shard_map/all_to_all | solution.py:262
  36.9 0.0 copy-done
  36.9 13.3 %shard_map.78 = f32[576,128]{1,0:T(8,128)} custom-call(s32[64,128]{1,0:T(8,128)S(1)} %bitcast.29, f32[5,256,128]{2,1,0:T(8,128)S(1)} %bitcast.28, f32[4,256,128]{2,1,0:T(8,128)S(1)} %bitcast.24), custom_call_target="tpu_custom_call" | custom-call | tf_op jit(solution)/shard_map/pallas_call | solution.py:283
  50.2 0.0 copy-start.3
  50.2 4.9 %all-to-all-start.1 = ((f32[64,1,1152]{2,1,0:T(1,128)}), f32[64,1,1152]{2,1,0:T(1,128)S(1)}, u32[]{:S(2)}, u32[]{:S(2)}) async-start(f32[64,1,1152]{2,1,0:T(1,128)} %bitcast.5), calls=%async_computation.1 | async-start | bytes 589824 | tf_op jit(solution)/shard_map/all_to_all | solution.py:262
  55.0 0.0 all-reduce.2.cloned.1.call-start
  55.1 0.0 copy-done.3
  55.1 13.7 %all-to-all-done.1 = f32[64,1,1152]{2,1,0:T(1,128)S(1)} async-done(((f32[64,1,1152]{2,1,0:T(1,128)}), f32[64,1,1152]{2,1,0:T(1,128)S(1)}, u32[]{:S(2)}, u32[]{:S(2)}) %all-to-all-start.1) | async-done | bytes 294944 | tf_op jit(solution)/shard_map/all_to_all | solution.py:262
  68.8 0.0 copy-start.2
  68.8 0.7 copy-done.2
  69.5 23.6 %shard_map.79 = f32[576,128]{1,0:T(8,128)S(1)} custom-call(s32[1,16]{1,0:T(1,128)S(1)} %copy-done.2, s32[16,256]{1,0:T(8,128)S(1)} %reshape.40.owner_ref, s32[16,256]{1,0:T(8,128)S(1)} %get-tuple-element.5.rank_ref, f32[16,3,256]{2,1,0:T(4,128)S(1)} %bitcast.32, f32[576,128]{1,0:T(8,128)S(1)} %bitcast.26), custom_call_target="tpu_custom_call" | custom-call | tf_op jit(solution)/shard_map/pallas_call | solution.py:292
  93.1 18.4 %all_to_all.15 = f32[64,1,1152]{2,1,0:T(1,128)S(1)} all-to-all(f32[64,1,1152]{2,1,0:T(1,128)S(1)} %bitcast.27), channel_id=1, replica_groups=mesh['owner'=64,'view'=4] {'owner'}, dimensions={0} | all-to-all | bytes 589824 | tf_op jit(solution)/shard_map/all_to_all | solution.py:262
  111.5 6.2 %shard_map.81 = f32[4,256,128]{2,1,0:T(8,128)S(1)} custom-call(s32[64,128]{1,0:T(8,128)S(1)} %bitcast.30, f32[576,128]{1,0:T(8,128)S(1)} %bitcast.22), custom_call_target="tpu_custom_call" | custom-call | tf_op jit(solution)/shard_map/pallas_call | solution.py:307
  117.8 1.1 copy.22
  118.9 0.0 all-reduce.2.cloned.1.call-update
  118.9 8.2 %shard_map.80 = f32[5,256,128]{2,1,0:T(8,128)} custom-call(s32[64,128]{1,0:T(8,128)S(1)} %bitcast.31, f32[576,128]{1,0:T(8,128)S(1)} %bitcast.23), custom_call_target="tpu_custom_call" | custom-call | tf_op jit(solution)/shard_map/pallas_call | solution.py:307
  127.1 33.6 %all-reduce.2.cloned.1.call-done = f32[4,32768]{1,0:T(4,128)} async-done(((f32[4,32768]{1,0:T(4,128)}), f32[4,32768]{1,0:T(4,128)}) %all-reduce.2.cloned.1.call-update) | async-done | bytes 524304 | tf_op jit(solution)/shard_map/psum | solution.py:316
  160.8 1.9 %copy.26 = f32[4,32768]{1,0:T(4,128)} copy(f32[4,32768]{1,0:T(4,128)} %all-reduce.2.cloned.1.call-done) | data formatting | bytes 1048576
  (3 shorter events, 0.0 us)
Async XLA Ops:
  7.2 29.7 %copy-start = (f32[1,5,32768]{2,0,1:T(1,128)S(1)}, f32[1,5,32768]{2,0,1:T(1,128)}, u32[]{:S(2)}) copy-start(f32[1,5,32768]{2,0,1:T(1,128)} %param.6) | copy-start | bytes 1966084
  10.5 0.7 copy-start.1
  14.4 22.5 %all-to-all-start = ((s32[64,1,128]{2,1,0:T(1,128)}), s32[64,1,128]{2,1,0:T(1,128)S(1)}, u32[]{:S(2)}, u32[]{:S(2)}) async-start(s32[64,1,128]{2,1,0:T(1,128)} %bitcast.1), calls=%async_computation | async-start | bytes 65536 | tf_op jit(solution)/shard_map/all_to_all | solution.py:262
  50.2 4.9 %copy-start.3 = (f32[1,16,3,256]{3,1,2,0:T(8,128)S(1)}, f32[1,16,3,256]{3,1,2,0:T(8,128)}, u32[]{:S(2)}) copy-start(f32[1,16,3,256]{3,1,2,0:T(8,128)} %param.11) | copy-start | bytes 147460
  50.2 18.7 %all-to-all-start.1 = ((f32[64,1,1152]{2,1,0:T(1,128)}), f32[64,1,1152]{2,1,0:T(1,128)S(1)}, u32[]{:S(2)}, u32[]{:S(2)}) async-start(f32[64,1,1152]{2,1,0:T(1,128)} %bitcast.5), calls=%async_computation.1 | async-start | bytes 589824 | tf_op jit(solution)/shard_map/all_to_all | solution.py:262
  55.0 105.7 %all-reduce.2.cloned.1.call-start = ((), (), s32[]{:S(2)}) async-start(), calls=%async_computation.3 | async-start | bytes 1048576 | tf_op jit(solution)/shard_map/psum | solution.py:316
  68.8 0.7 copy-start.2
Sparse Core Ops, SparseCore 0:
  119.0 41.7 all-reduce.1

commit v2 on v1

v2 whole, which is shorter than its diff:
```python
import functools
import math

import jax
import jax.numpy as jnp
from jax import lax
from jax.experimental import pallas as pl
from jax.experimental.pallas import tpu as pltpu
from jax.sharding import PartitionSpec as P

K = 256
TS = 16
LANES = 128
LOW = 64
F32 = jnp.float32
BF16 = jnp.bfloat16
LOG2E = 1.4426950408889634


def split2(x):
    high = x.astype(BF16)
    return high, (x - high.astype(F32)).astype(BF16)


def split3(x):
    high = x.astype(BF16)
    rest = x - high.astype(F32)
    middle = rest.astype(BF16)
    return high, middle, (rest - middle.astype(F32)).astype(BF16)


def dot_nn(a, b):
    return lax.dot_general(a, b, (((1,), (0,)), ((), ())), preferred_element_type=F32)


def dot_nt(a, b):
    return lax.dot_general(a, b, (((1,), (1,)), ((), ())), preferred_element_type=F32)


def row_iota(rows, columns):
    return lax.broadcasted_iota(jnp.int32, (rows, columns), 0)


def lane_iota(rows, columns):
    return lax.broadcasted_iota(jnp.int32, (rows, columns), 1)


def named_mask(owner_row, count, owners):
    live = lane_iota(1, K) < count
    shown = jnp.where(live, owner_row, -1)
    return row_iota(owners, K) == shown


def plan_kernel(counts_ref, owner_ref, local_ref, request_ref, rank_ref):
    tiles = rank_ref.shape[0]
    owners = request_ref.shape[0]
    before = (row_iota(K, K) < lane_iota(K, K)).astype(BF16)
    carry = jnp.zeros((owners, 1), F32)
    total = jnp.zeros((owners, 2 * LANES), F32)
    for t in range(tiles):
        at = slice(t * K, (t + 1) * K)
        named = named_mask(owner_ref[:, at], counts_ref[0, t], owners).astype(F32)
        named_half = named.astype(BF16)
        inside = dot_nn(named_half, before)
        rank = jnp.sum(named * (inside + carry), axis=0, keepdims=True).astype(jnp.int32)
        carry = carry + jnp.sum(named, axis=1, keepdims=True)
        rank_ref[t : t + 1, :] = rank
        ids = local_ref[:, at] + 1
        hits = hits16(LANES, rank)
        high = keep16(hits, (ids >> 7).astype(F32).astype(BF16))
        low = keep16(hits, (ids & 127).astype(F32).astype(BF16))
        total = total + dot_nt(named_half, jnp.concatenate([high, low], 0))
    request_ref[...] = (total[:, :LANES] * 128.0 + total[:, LANES:]).astype(jnp.int32)


def table_kernel(geo_ref, app_ref, table_ref):
    for c in range(9):
        values = geo_ref[c] if c < 5 else app_ref[c - 5]
        high, low = split2(values.T)
        table_ref[c * LOW : (c + 1) * LOW, :] = jnp.concatenate(
            [high[:LOW], high[LOW:], low[:LOW], low[LOW:]], 1
        )


WIDE = 8


def ids_row(ref, at):
    return jnp.concatenate([ref[pl.ds(at, 1), :], ref[pl.ds(at + 1, 1), :]], 1) - 1


def hits16(rows, row):
    return lax.broadcasted_iota(jnp.int16, (rows, row.shape[1]), 0) == row.astype(jnp.int16)


def keep16(hits, row):
    return jnp.where(hits, row, jnp.zeros_like(row))


def hot16(rows, row):
    return keep16(hits16(rows, row), jnp.ones((rows, row.shape[1]), BF16))


def hot_rows(ids):
    part = (ids >> 7) + jnp.where((ids & LOW) != 0, 256, 0)
    part = jnp.where(ids < 0, -1, part)
    return hot16(512, part)


def low_mask(ids):
    return row_iota(LOW, 256) == (ids & (LOW - 1))


def chunks_of(total):
    return (total + WIDE * LANES - 1) // (WIDE * LANES)


def merge(now, rolled, offset, following):
    fits = lane_iota(*now.shape) >= (offset & 127)
    block = now + jnp.where(fits, rolled, jnp.zeros_like(rolled))
    spilt = jnp.where(fits, jnp.zeros_like(rolled), rolled)
    return block, jnp.where((following >> 7) > (offset >> 7), spilt, block)


def gather_kernel(
    asked_ref, table_ref, out_ref, packed_ref, place_ref, found_ref, sem
):
    owners = asked_ref.shape[0]
    valid = (asked_ref[...] > 0).astype(F32).astype(BF16)
    earlier = (row_iota(owners, owners) > lane_iota(owners, owners)).astype(F32).astype(BF16)
    ones = jnp.ones((8, LANES), BF16)
    offsets = dot_nt(ones, dot_nn(earlier, valid).astype(BF16))
    amounts = dot_nt(ones, valid)
    packed_ref[0:owners, :] = jnp.zeros((owners, LANES), jnp.int32)
    place = jnp.concatenate([offsets, amounts], 1).astype(jnp.int32)
    packed_ref[owners : owners + 8, 0 : 2 * owners] = place
    copy = pltpu.make_async_copy(packed_ref.at[pl.ds(owners, 8), :], place_ref, sem)
    copy.start()
    copy.wait()
    total = place_ref[0, owners - 1] + place_ref[0, 2 * owners - 1]

    def compact(g, now):
        for j in range(8):
            s = g * 8 + j
            offset = place_ref[0, s]
            following = offset + place_ref[0, owners + s]
            row = jnp.broadcast_to(asked_ref[pl.ds(s, 1), :], (8, LANES))
            rolled = pltpu.roll(row, offset & 127, 1)
            block, now = merge(now, rolled, offset, following)
            packed_ref[pl.ds(offset >> 7, 1), :] = block[0:1]
        return now

    now = lax.fori_loop(0, owners // 8, compact, jnp.zeros((8, LANES), jnp.int32))

    @pl.when(total < owners * LANES)
    def _():
        packed_ref[pl.ds(total >> 7, 1), :] = now[0:1]

    def chunk(j, _):
        for at in range(0, WIDE, 2):
            ids = ids_row(packed_ref, WIDE * j + at)
            hot = hot_rows(ids)
            found = dot_nn(table_ref[...], jnp.concatenate([hot, hot], 0))
            mask = low_mask(ids)
            rows = [
                jnp.sum(jnp.where(mask, found[c * LOW : (c + 1) * LOW], 0.0), axis=0, keepdims=True)
                for c in range(9)
            ]
            values = jnp.concatenate(rows, 0)
            found_ref[WIDE * j + at, 0:9, :] = values[:, :LANES]
            found_ref[WIDE * j + at + 1, 0:9, :] = values[:, LANES:]
        return 0

    lax.fori_loop(0, chunks_of(total), chunk, 0)

    def expand(g, _):
        blocks = []
        for j in range(8):
            s = g * 8 + j
            offset, amount = place_ref[0, s], place_ref[0, owners + s]
            here, back = offset >> 7, (LANES - (offset & 127)) & 127
            first = pltpu.roll(found_ref[here], back, 1)
            second = pltpu.roll(found_ref[here + 1], back, 1)
            lanes = lane_iota(16, LANES)
            values = jnp.where(lanes + (offset & 127) < LANES, first, second)
            blocks.append(jnp.where(lanes < amount, values, 0.0)[0:9])
        out_ref[pl.ds(pl.multiple_of(g * 72, 8), 72), :] = jnp.concatenate(blocks, 0)
        return 0

    lax.fori_loop(0, owners // 8, expand, 0)


def pixel_rows():
    pixel = lane_iota(1, K)
    u = ((pixel & (TS - 1)).astype(F32) + 0.5) / TS - 0.5
    v = ((pixel >> 4).astype(F32) + 0.5) / TS - 0.5
    one = jnp.ones((1, K), F32)
    zero = jnp.zeros((2, K), F32)
    return jnp.concatenate([u * u, u * v, v * v, u, v, one, zero], 0)


def tile_kernel(
    unrolls,
    counts_ref,
    owner_ref,
    rank_ref,
    cot_ref,
    fetched_ref,
    out_ref,
    table_ref,
    grad_ref,
    dots_ref,
    entry_ref,
    coef_ref,
    sums_ref,
):
    tiles = rank_ref.shape[0]
    owners = fetched_ref.shape[0] // 9
    unrolls = [math.gcd(tiles, n) for n in unrolls]
    for c in range(9):
        high, low = split2(fetched_ref[pl.ds(c, owners, stride=9), :])
        table_ref[c * owners : (c + 1) * owners, :] = jnp.concatenate([high, low], 1)
    grad_ref[...] = jnp.zeros_like(grad_ref)
    pixels = pixel_rows()
    monomials = pixels.astype(BF16)
    pixel_columns = jnp.concatenate([pixels] * 4, 0).T.astype(BF16)
    before = (row_iota(K, K) < lane_iota(K, K)).astype(BF16)
    after = (row_iota(K, K) > lane_iota(K, K)).astype(BF16)
    dots_ref[0:K] = before
    dots_ref[K : 2 * K] = before
    dots_ref[2 * K : 3 * K] = after
    dots_ref[3 * K : 4 * K] = after

    def owner_row(t):
        row = owner_ref[:, pl.ds(pl.multiple_of(t * K, K), K)]
        return jnp.where(lane_iota(1, K) < counts_ref[0, t], row, -1)

    def fetch(g, _):
        several = [unrolls[0] * g + i for i in range(unrolls[0])]
        hots = [hot16(LANES, rank_ref[pl.ds(t, 1), :]) for t in several]
        spreads = [dot_nn(table_ref[...], jnp.concatenate([hot, hot], 0)) for hot in hots]
        for t, spread in zip(several, spreads):
            named = row_iota(owners, K) == owner_row(t)
            for c in range(9):
                kept = jnp.where(named, spread[c * owners : (c + 1) * owners], 0.0)
                entry_ref[c, pl.ds(t, 1), :] = jnp.sum(kept, axis=0, keepdims=True)
        return 0

    lax.fori_loop(0, tiles // unrolls[0], fetch, 0)
    cx, cy = entry_ref[0] - 0.5, entry_ref[1] - 0.5
    a, b, c2 = entry_ref[2], entry_ref[3], entry_ref[4]
    opacity = 1.0 / (1.0 + jnp.exp(-entry_ref[8]))
    spots = lane_iota(1, K)
    left = jnp.concatenate([counts_ref[0, t] - spots for t in range(tiles)], 0)
    ax, ay = a * cx + b * cy, b * cx + c2 * cy
    base = jnp.log(0.99 * opacity) * LOG2E - (0.5 * LOG2E) * (ax * cx + ay * cy)
    coefs = [
        (-0.5 * LOG2E) * a,
        -LOG2E * b,
        (-0.5 * LOG2E) * c2,
        LOG2E * ax,
        LOG2E * ay,
        jnp.where(left > 0, base, -400.0),
    ]
    for i, coef in enumerate(coefs):
        coef_ref[:, i, :] = coef
    coef_ref[:, 6, :] = jnp.zeros_like(a)
    coef_ref[:, 7, :] = jnp.zeros_like(a)

    def shade(g, _):
        several = [unrolls[1] * g + i for i in range(unrolls[1])]
        blank, pad = jnp.zeros((8, K), BF16), jnp.zeros((4, K), F32)
        exponents = [
            dot_nn(pixel_columns, jnp.concatenate([*split3(coef_ref[t]), blank], 0))
            for t in several
        ]
        slopes, cot_rows = [], []
        for t in several:
            cot_high, cot_low = split2(cot_ref[t])
            ch, cl = cot_high.astype(F32), cot_low.astype(F32)
            cot_columns = jnp.concatenate([ch, ch, cl, cl, pad], 0).T.astype(BF16)
            colors = jnp.concatenate([entry_ref[c, pl.ds(t, 1), :] for c in range(5, 8)], 0)
            color_high, color_low = split2(colors)
            kh, kl = color_high.astype(F32), color_low.astype(F32)
            color_rows = jnp.concatenate([kh, kl, kh, kl, pad], 0).astype(BF16)
            slopes.append(dot_nn(cot_columns, color_rows))
            cot_rows.append(jnp.concatenate([ch, cl, pad[0:2]], 0).astype(BF16))
        alphas = [jnp.exp2(exponent) for exponent in exponents]
        log_keeps = [jnp.log(1.0 - alpha) for alpha in alphas]
        prefixes = [
            dot_nn(jnp.concatenate(split2(log_keep), 1), dots_ref[0 : 2 * K])
            for log_keep in log_keeps
        ]
        weights = [jnp.exp(prefix) * alpha for prefix, alpha in zip(prefixes, alphas)]
        pulls = [weight * slope for weight, slope in zip(weights, slopes)]
        suffixes = [
            dot_nn(jnp.concatenate(split2(pull), 1), dots_ref[2 * K : 4 * K]) for pull in pulls
        ]
        for t, weight, rows in zip(several, weights, cot_rows):
            both = jnp.concatenate(split2(weight), 0)
            sums_ref[t, 8:16, :] = dot_nn(jnp.concatenate([rows, rows], 1), both)
        mass = jnp.concatenate([monomials, monomials], 1)
        for t, alpha, log_keep, pull, suffix in zip(several, alphas, log_keeps, pulls, suffixes):
            q = pull - alpha * jnp.exp(-log_keep) * suffix
            sums_ref[t, 0:8, :] = dot_nn(mass, jnp.concatenate(split2(q), 0))
        return 0

    lax.fori_loop(0, tiles // unrolls[1], shade, 0)
    mxx, mxy, myy, mx, my, m0 = [sums_ref[:, i, :] for i in range(6)]
    sx, sy = mx - cx * m0, my - cy * m0
    entry_ref[0] = a * sx + b * sy
    entry_ref[1] = b * sx + c2 * sy
    entry_ref[2] = -0.5 * (mxx - cx * (mx + sx))
    entry_ref[3] = -(mxy - cx * my - cy * sx)
    entry_ref[4] = -0.5 * (myy - cy * (my + sy))
    for i in range(3):
        entry_ref[5 + i] = sums_ref[:, 8 + i, :] + sums_ref[:, 11 + i, :]
    entry_ref[8] = (1.0 - opacity) * m0

    def give(g, _):
        sides, hots = [], []
        for i in range(unrolls[2]):
            t = unrolls[2] * g + i
            hot = hot16(LANES, rank_ref[pl.ds(t, 1), :])
            hits = hits16(owners, owner_row(t))
            placed = []
            for c in range(9):
                high, low = split2(entry_ref[c, pl.ds(t, 1), :])
                placed.append(jnp.concatenate([keep16(hits, high), keep16(hits, low)], 1))
            sides.append(jnp.concatenate(placed, 0))
            hots += [hot, hot]
        grad_ref[...] += dot_nt(jnp.concatenate(sides, 1), jnp.concatenate(hots, 1))
        return 0

    lax.fori_loop(0, tiles // unrolls[2], give, 0)
    for c in range(9):
        out_ref[pl.ds(c, owners, stride=9), :] = grad_ref[c * owners : (c + 1) * owners, :]


def collect_kernel(place_ref, vals_ref, geo_ref, look_ref):
    owners = geo_ref.shape[0]
    total = place_ref[0, owners - 1] + place_ref[0, 2 * owners - 1]
    blank = jnp.zeros((16, LANES), F32)

    def store(at, block):
        geo_ref[pl.ds(at, 1), 0:5, :] = block[None, 0:5]
        look_ref[pl.ds(at, 1), :, :] = block[None, 5:9]

    def compact(g, now):
        values = vals_ref[pl.ds(pl.multiple_of(g * 72, 8), 72), :]
        for j in range(8):
            s = g * 8 + j
            offset = place_ref[0, s]
            following = offset + place_ref[0, owners + s]
            row = jnp.concatenate([values[9 * j : 9 * j + 9], blank[0:7]], 0)
            rolled = pltpu.roll(row, offset & 127, 1)
            block, now = merge(now, rolled, offset, following)
            store(offset >> 7, block)
        return now

    now = lax.fori_loop(0, owners // 8, compact, blank)

    @pl.when(total < owners * LANES)
    def _():
        store(total >> 7, now)

    for more in range(1, WIDE):

        @pl.when(total + more * LANES < owners * LANES)
        def _():
            store((total >> 7) + more, blank)


def add_chunks(ids_ref, value_refs, total, acc_ref, transposed=False):
    def chunk(j, _):
        sides, hots = [], []
        for at in range(0, WIDE, 2):
            first = WIDE * j + at
            ids = ids_row(ids_ref, first)
            hot = hot_rows(ids)
            hits = hits16(LOW, ids & (LOW - 1))
            stacked = []
            for ref, number in value_refs:
                for c in range(number):
                    row = jnp.concatenate(
                        [ref[first, c : c + 1, :], ref[first + 1, c : c + 1, :]], 1
                    )
                    high, low = split2(row)
                    stacked.append(
                        jnp.concatenate([keep16(hits, high), keep16(hits, low)], 1)
                    )
            sides.append(jnp.concatenate(stacked, 0))
            hots += [hot, hot]
        side, hot = jnp.concatenate(sides, 1), jnp.concatenate(hots, 1)
        if transposed:
            acc_ref[...] += dot_nt(hot, side)
        else:
            acc_ref[...] += dot_nt(side, hot)
        return 0

    lax.fori_loop(0, chunks_of(total), chunk, 0)


def spread_out(part):
    return jnp.concatenate([part[:, :256], part[:, 256:]], 0).T


def scatter_kernel(place_ref, ids_ref, geo_vals_ref, look_vals_ref, geo_ref, look_acc_ref, acc_ref):
    owners = geo_vals_ref.shape[0]
    total = place_ref[0, owners - 1] + place_ref[0, 2 * owners - 1]
    acc_ref[...] = jnp.zeros_like(acc_ref)
    add_chunks(ids_ref, [(geo_vals_ref, 5), (look_vals_ref, 4)], total, acc_ref)
    for c in range(5):
        geo_ref[c] = spread_out(acc_ref[c * LOW : (c + 1) * LOW, :])
    look_acc_ref[...] = acc_ref[5 * LOW :, :]


def finish_kernel(*refs):
    others = (len(refs) - 5) // 2
    ids_refs, vals_refs = refs[:others], refs[others : 2 * others]
    start_ref, look_ref, acc_ref, place_ref, sem = refs[2 * others :]
    owners = vals_refs[0].shape[0]
    copies = [
        pltpu.make_async_copy(ref.at[pl.ds(owners, 8), :], place_ref.at[i], sem.at[i])
        for i, ref in enumerate(ids_refs)
    ]
    for copy in copies:
        copy.start()
    acc_ref[...] = start_ref[...].T
    for copy in copies:
        copy.wait()
    for i in range(others):
        total = place_ref[i, 0, owners - 1] + place_ref[i, 0, 2 * owners - 1]
        add_chunks(ids_refs[i], [(vals_refs[i], 4)], total, acc_ref, transposed=True)
    for c in range(4):
        part = acc_ref[:, c * LOW : (c + 1) * LOW]
        look_ref[:, c, :] = jnp.concatenate([part[:256], part[256:]], 1)


VMEM = pl.BlockSpec(memory_space=pltpu.VMEM)
SMEM = pl.BlockSpec(memory_space=pltpu.SMEM)
LIMIT = pltpu.CompilerParams(vmem_limit_bytes=40 * 1024 * 1024)


def exchange(values, owners, axis="owner"):
    sent = values.reshape(owners, 1, -1)
    got = lax.all_to_all(sent, axis, split_axis=0, concat_axis=0, tiled=True)
    return got.reshape(values.shape)


def shards(geometry, appearance, list_owner, list_local, counts, cotangent):
    owners = lax.axis_size("owner")
    views = lax.axis_size("view")
    tiles = counts.shape[1]
    gauss = geometry.shape[2]
    rows = gauss // LANES
    target = list_owner.reshape(1, tiles * K)
    requests, ranks = pl.pallas_call(
        plan_kernel,
        out_shape=(
            jax.ShapeDtypeStruct((owners, LANES), jnp.int32),
            jax.ShapeDtypeStruct((tiles, K), jnp.int32),
        ),
        in_specs=[SMEM, VMEM, VMEM],
        out_specs=(VMEM, VMEM),
        compiler_params=LIMIT,
    )(counts, target, list_local)
    table = pl.pallas_call(
        table_kernel,
        out_shape=jax.ShapeDtypeStruct((9 * LOW, 1024), BF16),
        in_specs=[VMEM, VMEM],
        out_specs=VMEM,
        compiler_params=LIMIT,
    )(geometry.reshape(5, rows, LANES), appearance.reshape(4, rows, LANES))
    asked = exchange(requests, owners)
    picked, packed = pl.pallas_call(
        gather_kernel,
        out_shape=(
            jax.ShapeDtypeStruct((owners * 9, LANES), F32),
            jax.ShapeDtypeStruct((owners + 8, LANES), jnp.int32),
        ),
        in_specs=[VMEM, VMEM],
        out_specs=(VMEM, VMEM),
        scratch_shapes=[
            pltpu.SMEM((8, LANES), jnp.int32),
            pltpu.VMEM((owners + WIDE, 16, LANES), F32),
            pltpu.SemaphoreType.DMA,
        ],
        compiler_params=LIMIT,
    )(asked, table)
    fetched = exchange(picked, owners)
    shifts = [[(i, (i + k) % views) for i in range(views)] for k in range(1, views)]
    other_ids = [lax.ppermute(packed, "view", shift) for shift in shifts]
    fetched, other_ids = lax.optimization_barrier((fetched, other_ids))
    outgoing = pl.pallas_call(
        functools.partial(tile_kernel, (8, 4, 8)),
        out_shape=jax.ShapeDtypeStruct((owners * 9, LANES), F32),
        in_specs=[SMEM, VMEM, VMEM, VMEM, VMEM],
        out_specs=VMEM,
        scratch_shapes=[
            pltpu.VMEM((9 * owners, 2 * LANES), BF16),
            pltpu.VMEM((9 * owners, LANES), F32),
            pltpu.VMEM((4 * K, K), BF16),
            pltpu.VMEM((9, tiles, K), F32),
            pltpu.VMEM((tiles, 8, K), F32),
            pltpu.VMEM((tiles, 16, K), F32),
        ],
        compiler_params=LIMIT,
    )(counts, target, ranks, cotangent[0], fetched)
    returned = exchange(outgoing, owners)
    place = packed[owners:]
    geo_vals, look_vals = pl.pallas_call(
        collect_kernel,
        out_shape=(
            jax.ShapeDtypeStruct((owners, 8, LANES), F32),
            jax.ShapeDtypeStruct((owners, 4, LANES), F32),
        ),
        in_specs=[SMEM, VMEM],
        out_specs=(VMEM, VMEM),
        compiler_params=LIMIT,
    )(place, returned)
    other_vals = [lax.ppermute(look_vals, "view", shift) for shift in shifts]
    geo, look_acc = pl.pallas_call(
        scatter_kernel,
        out_shape=(
            jax.ShapeDtypeStruct((5, rows, LANES), F32),
            jax.ShapeDtypeStruct((4 * LOW, 512), F32),
        ),
        in_specs=[SMEM, VMEM, VMEM, VMEM],
        out_specs=(VMEM, VMEM),
        scratch_shapes=[pltpu.VMEM((9 * LOW, 512), F32)],
        compiler_params=LIMIT,
    )(place, packed, geo_vals, look_vals)
    look = pl.pallas_call(
        finish_kernel,
        out_shape=jax.ShapeDtypeStruct((rows, 4, LANES), F32),
        in_specs=[VMEM] * (2 * views - 1),
        out_specs=VMEM,
        scratch_shapes=[
            pltpu.VMEM((512, 4 * LOW), F32),
            pltpu.SMEM((views - 1, 8, LANES), jnp.int32),
            pltpu.SemaphoreType.DMA((views - 1,)),
        ],
        compiler_params=LIMIT,
    )(*other_ids, *other_vals, look_acc)
    look = jnp.transpose(look, (1, 0, 2)).reshape(4, gauss)
    return (geo.reshape(1, 5, gauss), look)


def solution(mesh):
    placed = (
        P("view", None, "owner"),
        P(None, "owner"),
        P("view", "owner", None),
        P("view", "owner"),
        P("view", "owner"),
        P("view", "owner", None, None),
    )
    return jax.shard_map(
        shards,
        mesh=mesh,
        in_specs=placed,
        out_specs=(P("view", None, "owner"), P(None, "owner")),
        check_vma=False,
    )
```

time: 171 us -> 112 us (0.65)
  waiting for transfers between devices: 55.6 us -> 34.2 us
  blocking collectives: 18.4 us -> 0 us
  Pallas kernels: 54.6 us -> 40.1 us
  starting transfers between devices: 18.1 us -> 31.6 us
  between operations: 14.1 us -> 0.92 us
  other arithmetic: 2.81 us -> 0 us
  local copies, waits for them, and re-layouts: 5.95 us -> 3.29 us
    psum x1 -> x0, waiting for transfers between devices: 33.6 us -> none  [shards(): look = lax.psum(scatter(5, 4), 'view')]
    all_to_all x1 -> x0, blocking collectives: 18.4 us -> none  [exchange(): got = lax.all_to_all(sent, axis, split_axis=0, concat_axis=0, tiled=True)]
    pallas_call x4 -> x6, Pallas kernels: 51.4 us -> 36.8 us  [the longest x1 12.8 us: shards(): pl.pallas_call(functools.partial(tile_kernel, (8, 4, 8)), out_shape=jax.S...]
    ppermute x0 -> x6, starting transfers between devices: none -> 6.83 us  [the longest x3 3.69 us: shards(): other_ids = [lax.ppermute(packed, 'view', shift) for shift in shifts]]
    all_to_all x2 -> x3, starting transfers between devices: 18 us -> 24.7 us  [exchange(): got = lax.all_to_all(sent, axis, split_axis=0, concat_axis=0, tiled=True)]
    ppermute x0 -> x6, waiting for transfers between devices: none -> 6.41 us  [the longest x3 3.82 us: shards(): other_ids = [lax.ppermute(packed, 'view', shift) for shift in shifts]]
    all_to_all x2 -> x3, waiting for transfers between devices: 21.9 us -> 27.7 us  [exchange(): got = lax.all_to_all(sent, axis, split_axis=0, concat_axis=0, tiled=True)]
    unnamed x2 -> x0, other arithmetic: 2.81 us -> none
  transfers between devices with their start and end apart: 3 -> 9, of which waited for: 3 -> 6; matrix products, arithmetic and copies ran while one was open for 1% -> 1% of each run, Pallas kernels for 5% -> 6%
where the time goes in v2:
time: 112 us; the launch traced here: 110 us
  Pallas kernels  40.1 us (36%)
  waiting for transfers between devices  34.2 us (31%)
  starting transfers between devices  31.6 us (28%)
  local copies, waits for them, and re-layouts  3.29 us (3%)
    all_to_all x3, waiting for transfers between devices, exchange(): got = lax.all_to_all(sent, axis, split_axis=0, concat_axis=0, tiled=True)  27.7 us
    all_to_all x3, starting transfers between devices, exchange(): got = lax.all_to_all(sent, axis, split_axis=0, concat_axis=0, tiled=True)  24.7 us
    pallas_call x1, Pallas kernels, shards(): pl.pallas_call(functools.partial(tile_kernel, (8, 4, 8)), out_shape=jax.S...  12.8 us
    pallas_call x1, Pallas kernels, shards(): pl.pallas_call(finish_kernel, out_shape=jax.ShapeDtypeStruct((rows, 4, LA...  8.79 us
    pallas_call x1, Pallas kernels, shards(): pl.pallas_call(gather_kernel, out_shape=(jax.ShapeDtypeStruct((owners * 9...  7.32 us
    pallas_call x1, Pallas kernels, shards(): pl.pallas_call(scatter_kernel, out_shape=(jax.ShapeDtypeStruct((5, rows,...  6.01 us
    ppermute x3, waiting for transfers between devices, shards(): other_ids = [lax.ppermute(packed, 'view', shift) for shift in shifts]  3.82 us
    ppermute x3, starting transfers between devices, shards(): other_ids = [lax.ppermute(packed, 'view', shift) for shift in shifts]  3.69 us
  transfers between devices with their start and end apart: 9, of which 6 were waited for; matrix products, arithmetic and copies ran while one was open for 1% of the time, Pallas kernels for 6%

profile of v2, /device:TPU:1, one launch (start us, length us, event | category | flops | bytes accessed | tf_op | source)
XLA Modules:
  0.0 110.0 jit_solution(4795588706189848561)
XLA Ops:
  0.6 0.0 copy-start
  0.6 0.0 copy-start.1
  0.7 0.8 copy-done.1
  1.4 0.0 copy-start.3
  1.4 0.7 copy-done.3
  2.1 0.0 copy-start.4
  2.1 0.7 copy-done.4
  2.8 3.2 %shard_map.77 = (s32[64,128]{1,0:T(8,128)}, s32[16,256]{1,0:T(8,128)S(1)}) custom-call(s32[1,16]{1,0:T(1,128)S(1)} %copy-done.4, s32[1,4096]{1,0:T(1,128)S(1)} %bitcast.27, s32[1,4096]{1,0:T(1,128)S(1)} %copy-done.3), custom_call_target="tpu_custom_call" | custom-call | tf_op jit(solution)/shard_map/pallas_call | solution.py:458
  6.0 13.2 %all-to-all-start = ((s32[64,1,128]{2,1,0:T(1,128)}), s32[64,1,128]{2,1,0:T(1,128)S(1)}, u32[]{:S(2)}, u32[]{:S(2)}) async-start(s32[64,1,128]{2,1,0:T(1,128)} %bitcast.2), calls=%async_computation | async-start | bytes 65536 | tf_op jit(solution)/shard_map/all_to_all | solution.py:447
  19.2 1.1 copy.20
  20.3 0.0 copy-done
  20.3 0.4 shard_map.78.table_ref
  20.7 0.0 copy-start.6
  20.7 0.0 copy-start.2
  20.7 0.0 copy-start.5
  20.7 7.8 %all-to-all-done = s32[64,1,128]{2,1,0:T(1,128)S(1)} async-done(((s32[64,1,128]{2,1,0:T(1,128)}), s32[64,1,128]{2,1,0:T(1,128)S(1)}, u32[]{:S(2)}, u32[]{:S(2)}) %all-to-all-start) | async-done | bytes 32800 | tf_op jit(solution)/shard_map/all_to_all | solution.py:447
  28.5 7.3 %shard_map.79 = (f32[576,128]{1,0:T(8,128)}, s32[72,128]{1,0:T(8,128)S(1)}) custom-call(s32[64,128]{1,0:T(8,128)S(1)} %bitcast.26, bf16[576,1024]{1,0:T(8,128)(2,1)S(1)} %shard_map.78.table_ref), custom_call_target="tpu_custom_call" | custom-call | tf_op jit(solution)/shard_map/pallas_call | solution.py:476
  35.8 6.2 %all-to-all-start.1 = ((f32[64,1,1152]{2,1,0:T(1,128)}), f32[64,1,1152]{2,1,0:T(1,128)S(1)}, u32[]{:S(2)}, u32[]{:S(2)}) async-start(f32[64,1,1152]{2,1,0:T(1,128)} %bitcast.6), calls=%async_computation.1 | async-start | bytes 589824 | tf_op jit(solution)/shard_map/all_to_all | solution.py:447
  42.0 2.6 %collective-permute-start.2 = (s32[72,128]{1,0:T(8,128)S(1)}, s32[72,128]{1,0:T(8,128)S(1)}, u32[]{:S(2)}, u32[]{:S(2)}) collective-permute-start(s32[72,128]{1,0:T(8,128)S(1)} %get-tuple-element.15.ids_ref), channel_id=1, source_target_pairs={{0,3},{1,0},{2,1},{3,2},{4,7},{5,4},{6,5},{7,6},{8,11},{9,8},{10,9... | collective-permute-start | bytes 110600 | tf_op jit(solution)/shard_map/ppermute | solution.py:493
  44.6 0.5 collective-permute-start.1
  45.1 0.6 collective-permute-start
  45.7 0.0 copy-done.6
  45.7 0.0 collective-permute-done.2.refs_2_
  45.7 3.4 %collective-permute-done.1.refs_1_ = s32[72,128]{1,0:T(8,128)S(1)} collective-permute-done((s32[72,128]{1,0:T(8,128)S(1)}, s32[72,128]{1,0:T(8,128)S(1)}, u32[]{:S(2)}, u32[]{:S(2)}) %collective-permute-start.1) | collective-permute-done | bytes 36896 | tf_op jit(solution)/shard_map/ppermute | solution.py:493
  49.2 0.4 collective-permute-done.refs_0_
  49.6 6.2 %all-to-all-done.1 = f32[64,1,1152]{2,1,0:T(1,128)S(1)} async-done(((f32[64,1,1152]{2,1,0:T(1,128)}), f32[64,1,1152]{2,1,0:T(1,128)S(1)}, u32[]{:S(2)}, u32[]{:S(2)}) %all-to-all-start.1) | async-done | bytes 294944 | tf_op jit(solution)/shard_map/all_to_all | solution.py:447
  55.8 0.0 copy-done.2
  55.8 0.0 copy-done.5
  55.8 12.8 %shard_map.80 = f32[576,128]{1,0:T(8,128)} custom-call(s32[1,16]{1,0:T(1,128)S(1)} %copy-done.5, s32[1,4096]{1,0:T(1,128)S(1)} %bitcast.28, s32[16,256]{1,0:T(8,128)S(1)} %get-tuple-element.16.rank_ref, f32[16,3,256]{2,1,0:T(4,128)S(1)} %bitcast.25, f32[576,128]{1,0:T(8,128)S(1)} %bitcast.22), custom_call_target="tpu_custom_call" | custom-call | tf_op jit(solution)/shard_map/pallas_call | solution.py:495
  68.6 5.4 %all-to-all-start.2 = ((f32[64,1,1152]{2,1,0:T(1,128)}), f32[64,1,1152]{2,1,0:T(1,128)S(1)}, u32[]{:S(2)}, u32[]{:S(2)}) async-start(f32[64,1,1152]{2,1,0:T(1,128)} %bitcast.8), calls=%async_computation.2 | async-start | bytes 589824 | tf_op jit(solution)/shard_map/all_to_all | solution.py:447
  74.0 13.7 %all-to-all-done.2 = f32[64,1,1152]{2,1,0:T(1,128)S(1)} async-done(((f32[64,1,1152]{2,1,0:T(1,128)}), f32[64,1,1152]{2,1,0:T(1,128)S(1)}, u32[]{:S(2)}, u32[]{:S(2)}) %all-to-all-start.2) | async-done | bytes 294944 | tf_op jit(solution)/shard_map/all_to_all | solution.py:447
  87.7 1.6 %shard_map.81 = (f32[64,8,128]{2,1,0:T(8,128)S(1)}, f32[64,4,128]{2,1,0:T(4,128)S(1)}) custom-call(s32[8,128]{1,0:T(8,128)S(1)} %slice.3.place_ref, f32[576,128]{1,0:T(8,128)S(1)} %bitcast.23), custom_call_target="tpu_custom_call" | custom-call | tf_op jit(solution)/shard_map/pallas_call | solution.py:512
  89.3 2.0 %collective-permute-start.5 = (f32[64,4,128]{2,1,0:T(4,128)S(1)}, f32[64,4,128]{2,1,0:T(4,128)S(1)}, u32[]{:S(2)}, u32[]{:S(2)}) collective-permute-start(f32[64,4,128]{2,1,0:T(4,128)S(1)} %get-tuple-element.20.look_vals_ref), channel_id=1, source_target_pairs={{0,3},{1,0},{2,1},{3,2},{4,7},{5,4},{6,5},{7,6},{8,11},{9,8},{10,9... | collective-permute-start | bytes 393224 | tf_op jit(solution)/shard_map/ppermute | solution.py:522
  91.3 0.5 collective-permute-start.4
  91.8 0.6 collective-permute-start.3
  92.4 6.0 %shard_map.82 = (f32[5,256,128]{2,1,0:T(8,128)}, f32[256,512]{1,0:T(8,128)S(1)}) custom-call(s32[8,128]{1,0:T(8,128)S(1)} %slice.3.place_ref, s32[72,128]{1,0:T(8,128)S(1)} %get-tuple-element.15.ids_ref, f32[64,8,128]{2,1,0:T(8,128)S(1)} %get-tuple-element.19.geo_vals_ref, f32[64,4,128]{2,1,0:T(4,128)S(1)} %get-tuple-element.20.look_vals_ref), custom_call_target="tpu_custom_call" | custom-call | tf_op jit(solution)/shard_map/pallas_call | solution.py:523
  98.5 0.0 collective-permute-done.5.refs_5_
  98.5 0.0 collective-permute-done.4.refs_4_
  98.5 2.6 %collective-permute-done.3.refs_3_ = f32[64,4,128]{2,1,0:T(4,128)S(1)} collective-permute-done((f32[64,4,128]{2,1,0:T(4,128)S(1)}, f32[64,4,128]{2,1,0:T(4,128)S(1)}, u32[]{:S(2)}, u32[]{:S(2)}) %collective-permute-start.3) | collective-permute-done | bytes 131104 | tf_op jit(solution)/shard_map/ppermute | solution.py:522
  101.0 8.8 %shard_map.83 = f32[256,4,128]{2,1,0:T(4,128)} custom-call(s32[72,128]{1,0:T(8,128)S(1)} %collective-permute-done.refs_0_, s32[72,128]{1,0:T(8,128)S(1)} %collective-permute-done.1.refs_1_, s32[72,128]{1,0:T(8,128)S(1)} %collective-permute-done.2.refs_2_, f32[64,4,128]{2,1,0:T(4,128)S(1)} %collective-permute-done.3.refs_3_, ...), custom_call_target="tpu_custom_call" | custom-call | tf_op jit(solution)/shard_map/pallas_call | solution.py:534
  (2 shorter events, 0.0 us)
Async XLA Ops:
  0.6 19.7 %copy-start = (f32[1,5,32768]{2,0,1:T(1,128)S(1)}, f32[1,5,32768]{2,0,1:T(1,128)}, u32[]{:S(2)}) copy-start(f32[1,5,32768]{2,0,1:T(1,128)} %param.6) | copy-start | bytes 1966084
  0.6 0.8 copy-start.1
  1.4 0.7 copy-start.3
  2.1 0.7 copy-start.4
  6.0 22.5 %all-to-all-start = ((s32[64,1,128]{2,1,0:T(1,128)}), s32[64,1,128]{2,1,0:T(1,128)S(1)}, u32[]{:S(2)}, u32[]{:S(2)}) async-start(s32[64,1,128]{2,1,0:T(1,128)} %bitcast.2), calls=%async_computation | async-start | bytes 65536 | tf_op jit(solution)/shard_map/all_to_all | solution.py:447
  20.7 25.0 %copy-start.6 = (f32[1,16,3,256]{3,1,2,0:T(8,128)S(1)}, f32[1,16,3,256]{3,1,2,0:T(8,128)}, u32[]{:S(2)}) copy-start(f32[1,16,3,256]{3,1,2,0:T(8,128)} %param.11) | copy-start | bytes 147460
  20.7 35.1 %copy-start.2 = (s32[1,4096,1]{1,2,0:T(1,128)S(1)}, s32[1,4096,1]{1,2,0:T(1,128)}, u32[]{:S(2)}) copy-start(s32[1,4096,1]{1,2,0:T(1,128)} %param.8) | copy-start | bytes 49156
  20.7 35.1 %copy-start.5 = (s32[1,16]{1,0:T(1,128)S(1)}, s32[1,16]{1,0:T(1,128)}, u32[]{:S(2)}) copy-start(s32[1,16]{1,0:T(1,128)} %counts_ref.3) | copy-start | bytes 196
  35.8 20.0 %all-to-all-start.1 = ((f32[64,1,1152]{2,1,0:T(1,128)}), f32[64,1,1152]{2,1,0:T(1,128)S(1)}, u32[]{:S(2)}, u32[]{:S(2)}) async-start(f32[64,1,1152]{2,1,0:T(1,128)} %bitcast.6), calls=%async_computation.1 | async-start | bytes 589824 | tf_op jit(solution)/shard_map/all_to_all | solution.py:447
  42.0 3.7 %collective-permute-start.2 = (s32[72,128]{1,0:T(8,128)S(1)}, s32[72,128]{1,0:T(8,128)S(1)}, u32[]{:S(2)}, u32[]{:S(2)}) collective-permute-start(s32[72,128]{1,0:T(8,128)S(1)} %get-tuple-element.15.ids_ref), channel_id=1, source_target_pairs={{0,3},{1,0},{2,1},{3,2},{4,7},{5,4},{6,5},{7,6},{8,11},{9,8},{10,9... | collective-permute-start | bytes 110600 | tf_op jit(solution)/shard_map/ppermute | solution.py:493
  44.6 4.6 %collective-permute-start.1 = (s32[72,128]{1,0:T(8,128)S(1)}, s32[72,128]{1,0:T(8,128)S(1)}, u32[]{:S(2)}, u32[]{:S(2)}) collective-permute-start(s32[72,128]{1,0:T(8,128)S(1)} %get-tuple-element.15.ids_ref), channel_id=1, source_target_pairs={{0,2},{1,3},{2,0},{3,1},{4,6},{5,7},{6,4},{7,5},{8,10},{9,11},{10,... | collective-permute-start | bytes 110600 | tf_op jit(solution)/shard_map/ppermute | solution.py:493
  45.1 4.5 %collective-permute-start = (s32[72,128]{1,0:T(8,128)S(1)}, s32[72,128]{1,0:T(8,128)S(1)}, u32[]{:S(2)}, u32[]{:S(2)}) collective-permute-start(s32[72,128]{1,0:T(8,128)S(1)} %get-tuple-element.15.ids_ref), channel_id=1, source_target_pairs={{0,1},{1,2},{2,3},{3,0},{4,5},{5,6},{6,7},{7,4},{8,9},{9,10},{10,1... | collective-permute-start | bytes 110600 | tf_op jit(solution)/shard_map/ppermute | solution.py:493
  68.6 19.1 %all-to-all-start.2 = ((f32[64,1,1152]{2,1,0:T(1,128)}), f32[64,1,1152]{2,1,0:T(1,128)S(1)}, u32[]{:S(2)}, u32[]{:S(2)}) async-start(f32[64,1,1152]{2,1,0:T(1,128)} %bitcast.8), calls=%async_computation.2 | async-start | bytes 589824 | tf_op jit(solution)/shard_map/all_to_all | solution.py:447
  89.3 9.2 %collective-permute-start.5 = (f32[64,4,128]{2,1,0:T(4,128)S(1)}, f32[64,4,128]{2,1,0:T(4,128)S(1)}, u32[]{:S(2)}, u32[]{:S(2)}) collective-permute-start(f32[64,4,128]{2,1,0:T(4,128)S(1)} %get-tuple-element.20.look_vals_ref), channel_id=1, source_target_pairs={{0,3},{1,0},{2,1},{3,2},{4,7},{5,4},{6,5},{7,6},{8,11},{9,8},{10,9... | collective-permute-start | bytes 393224 | tf_op jit(solution)/shard_map/ppermute | solution.py:522
  91.3 7.1 %collective-permute-start.4 = (f32[64,4,128]{2,1,0:T(4,128)S(1)}, f32[64,4,128]{2,1,0:T(4,128)S(1)}, u32[]{:S(2)}, u32[]{:S(2)}) collective-permute-start(f32[64,4,128]{2,1,0:T(4,128)S(1)} %get-tuple-element.20.look_vals_ref), channel_id=1, source_target_pairs={{0,2},{1,3},{2,0},{3,1},{4,6},{5,7},{6,4},{7,5},{8,10},{9,11},{10,... | collective-permute-start | bytes 393224 | tf_op jit(solution)/shard_map/ppermute | solution.py:522
  91.8 9.2 %collective-permute-start.3 = (f32[64,4,128]{2,1,0:T(4,128)S(1)}, f32[64,4,128]{2,1,0:T(4,128)S(1)}, u32[]{:S(2)}, u32[]{:S(2)}) collective-permute-start(f32[64,4,128]{2,1,0:T(4,128)S(1)} %get-tuple-element.20.look_vals_ref), channel_id=1, source_target_pairs={{0,1},{1,2},{2,3},{3,0},{4,5},{5,6},{6,7},{7,4},{8,9},{9,10},{10,1... | collective-permute-start | bytes 393224 | tf_op jit(solution)/shard_map/ppermute | solution.py:522

commit v3 on v2

v3 whole, which is shorter than its diff:
```python
import functools
import math

import jax
import jax.numpy as jnp
from jax import lax
from jax.experimental import pallas as pl
from jax.experimental.pallas import tpu as pltpu
from jax.sharding import PartitionSpec as P

K = 256
TS = 16
LANES = 128
LOW = 64
F32 = jnp.float32
BF16 = jnp.bfloat16
LOG2E = 1.4426950408889634


def split2(x):
    high = x.astype(BF16)
    return high, (x - high.astype(F32)).astype(BF16)


def split3(x):
    high = x.astype(BF16)
    rest = x - high.astype(F32)
    middle = rest.astype(BF16)
    return high, middle, (rest - middle.astype(F32)).astype(BF16)


def dot_nn(a, b):
    return lax.dot_general(a, b, (((1,), (0,)), ((), ())), preferred_element_type=F32)


def dot_nt(a, b):
    return lax.dot_general(a, b, (((1,), (1,)), ((), ())), preferred_element_type=F32)


def row_iota(rows, columns):
    return lax.broadcasted_iota(jnp.int32, (rows, columns), 0)


def lane_iota(rows, columns):
    return lax.broadcasted_iota(jnp.int32, (rows, columns), 1)


def named_mask(owner_row, count, owners):
    live = lane_iota(1, K) < count
    shown = jnp.where(live, owner_row, -1)
    return row_iota(owners, K) == shown


def plan_kernel(counts_ref, owner_hbm, local_hbm, request_ref, rank_ref, owner_ref, local_ref, sem):
    copies = [
        pltpu.make_async_copy(owner_hbm, owner_ref, sem.at[0]),
        pltpu.make_async_copy(local_hbm, local_ref, sem.at[1]),
    ]
    for copy in copies:
        copy.start()
    tiles = rank_ref.shape[0]
    owners = request_ref.shape[0]
    before = (row_iota(K, K) < lane_iota(K, K)).astype(BF16)
    for copy in copies:
        copy.wait()
    rows = [owner_ref[:, t * K : (t + 1) * K] for t in range(tiles)]
    rows = [
        jnp.where(lane_iota(1, K) < counts_ref[0, t], row, -1) for t, row in enumerate(rows)
    ]
    ids = [local_ref[:, t * K : (t + 1) * K] for t in range(tiles)]
    units = [jnp.where((i & LOW) != 0, 256.0, 1.0) for i in ids]
    found = [hits16(owners, row) for row in rows]
    halves = [keep16(f, jnp.ones((owners, K), BF16)) for f in found]
    scaled = [keep16(f, unit.astype(BF16)) for f, unit in zip(found, units)]
    inside = dot_nn(jnp.concatenate(scaled, 0), before)
    carry = jnp.zeros((owners, 1), F32)
    sides = []
    for t, row in enumerate(rows):
        named = row_iota(owners, K) == row
        here = inside[t * owners : (t + 1) * owners]
        both = jnp.sum(jnp.where(named, here + carry, 0.0), axis=0, keepdims=True)
        both = both.astype(jnp.int32)
        rank = jnp.where((ids[t] & LOW) != 0, LANES - 1 - (both >> 8), both & 255)
        carry = carry + jnp.sum(jnp.where(named, units[t], 0.0), axis=1, keepdims=True)
        rank_ref[t : t + 1, :] = rank
        asked = ids[t] + 1
        hits = hits16(LANES, rank)
        high = keep16(hits, (asked >> 7).astype(F32).astype(BF16))
        low = keep16(hits, (asked & 127).astype(F32).astype(BF16))
        sides.append(jnp.concatenate([high, low], 0))
    total = dot_nt(jnp.concatenate(halves, 1), jnp.concatenate(sides, 1))
    request_ref[...] = (total[:, :LANES] * 128.0 + total[:, LANES:]).astype(jnp.int32)


def table_kernel(geo_ref, app_ref, table_ref):
    for c in range(9):
        values = geo_ref[c] if c < 5 else app_ref[c - 5]
        high, low = split2(values.T)
        for bucket in range(2):
            at = slice(bucket * LOW, (bucket + 1) * LOW)
            table_ref[bucket, c * LOW : (c + 1) * LOW, :] = jnp.concatenate(
                [high[at], low[at]], 1
            )


WIDE = 8
NARROW = 4


def ids_row(ref, at):
    return jnp.concatenate([ref[pl.ds(at, 1), :], ref[pl.ds(at + 1, 1), :]], 1) - 1


def hits16(rows, row):
    return lax.broadcasted_iota(jnp.int16, (rows, row.shape[1]), 0) == row.astype(jnp.int16)


def keep16(hits, row):
    return jnp.where(hits, row, jnp.zeros_like(row))


def hot16(rows, row):
    return keep16(hits16(rows, row), jnp.ones((rows, row.shape[1]), BF16))


def hot_rows(ids, bucket):
    fits = (ids >= 0) & (((ids >> 6) & 1) == bucket)
    return hot16(256, jnp.where(fits, ids >> 7, -1))


def low_mask(ids):
    return row_iota(LOW, 256) == (ids & (LOW - 1))


def each_chunk(totals, owners, chunk):
    most = jnp.maximum(totals[0], totals[1])
    large = most // (WIDE * LANES)
    small = (most - large * (WIDE * LANES) + NARROW * LANES - 1) // (NARROW * LANES)

    def wide(j, _):
        chunk(WIDE * j, 0, WIDE)
        chunk(owners - WIDE * (j + 1), 1, WIDE)
        return 0

    def narrow(j, _):
        done = WIDE * large + NARROW * j
        chunk(done, 0, NARROW)
        chunk(owners - done - NARROW, 1, NARROW)
        return 0

    lax.fori_loop(0, large, wide, 0)
    lax.fori_loop(0, small, narrow, 0)


def compact(owners, ends_ref, bucket, start, row_at, load, store):
    lanes = lane_iota(*row_at(0, 0).shape)

    def group(g, carry):
        offset, now = carry
        for j in range(8):
            s = g * 8 + j
            end = start + ends_ref[0, bucket * owners + s]
            amount = end - offset
            row = row_at(g, j)
            if bucket == 0:
                row = jnp.where(lanes < amount, row, jnp.zeros_like(row))
                rolled = pltpu.roll(row, offset & 127, 1)
            else:
                row = jnp.where(lanes >= LANES - amount, row, jnp.zeros_like(row))
                rolled = pltpu.roll(row, end & 127, 1)
            fits = lanes >= (offset & 127)
            block = now + jnp.where(fits, rolled, jnp.zeros_like(rolled))
            spilt = jnp.where(fits, jnp.zeros_like(rolled), rolled)
            store(offset >> 7, block)
            now = jnp.where((end >> 7) > (offset >> 7), spilt, block)
            offset = end
        return offset, now

    offset, now = lax.fori_loop(0, owners // 8, group, (start, load(start >> 7)))
    store(offset >> 7, now)


def gather_kernel(asked_ref, table_ref, out_ref, packed_ref, ends_ref, found_ref):
    owners = asked_ref.shape[0]
    asked = asked_ref[...]
    odd = ((asked - 1) & LOW) != 0
    valid = [(asked > 0) & ~odd, (asked > 0) & odd]
    valid = jnp.concatenate([v.astype(F32).astype(BF16) for v in valid], 1)
    upto = (row_iota(owners, owners) >= lane_iota(owners, owners)).astype(F32).astype(BF16)
    sides = ((lane_iota(8, 2 * LANES) >> 7) == row_iota(8, 2 * LANES)).astype(F32).astype(BF16)
    ends = dot_nt(sides, dot_nn(upto, valid).astype(BF16)).astype(jnp.int32)
    packed_ref[...] = jnp.zeros_like(packed_ref)
    for s in range(owners):
        ends_ref[0, s] = ends[0, s]
        ends_ref[0, owners + s] = ends[1, s]
    totals = ends[0, owners - 1], ends[1, owners - 1]
    base = owners * LANES - totals[1]

    def row_at(g, j):
        return jnp.broadcast_to(asked_ref[pl.ds(g * 8 + j, 1), :], (8, LANES))

    def load(at):
        return jnp.broadcast_to(packed_ref[pl.ds(at, 1), :], (8, LANES))

    def store(at, block):
        packed_ref[pl.ds(at, 1), :] = block[0:1]

    for bucket in range(2):
        compact(owners, ends_ref, bucket, base if bucket else 0, row_at, load, store)
    packed_ref[owners + 1 : owners + 2, 0 : 2 * owners] = jnp.concatenate(
        [ends[0:1], ends[1:2]], 1
    )

    def chunk(row, bucket, wide):
        for at in range(0, wide, 2):
            ids = ids_row(packed_ref, row + at)
            hot = hot_rows(ids, bucket)
            found = dot_nn(table_ref[bucket], jnp.concatenate([hot, hot], 0))
            mask = low_mask(ids)
            rows = [
                jnp.sum(jnp.where(mask, found[c * LOW : (c + 1) * LOW], 0.0), axis=0, keepdims=True)
                for c in range(9)
            ]
            values = jnp.concatenate(rows, 0)
            found_ref[bucket, row + at + 1, 0:9, :] = values[:, :LANES]
            found_ref[bucket, row + at + 2, 0:9, :] = values[:, LANES:]

    each_chunk(totals, owners, chunk)

    def expand(g, offsets):
        lanes = lane_iota(16, LANES)
        low, high = offsets
        blocks = []
        for j in range(8):
            s = g * 8 + j
            low_end, high_end = ends_ref[0, s], base + ends_ref[0, owners + s]
            sources = []
            for bucket, at, row in ((0, low, (low >> 7) + 1), (1, high_end, high_end >> 7)):
                back = (LANES - (at & 127)) & 127
                first = pltpu.roll(found_ref[bucket, row], back, 1)
                second = pltpu.roll(found_ref[bucket, row + 1], back, 1)
                sources.append(jnp.where(lanes + (at & 127) < LANES, first, second))
            values = jnp.where(lanes >= LANES - (high_end - high), sources[1], 0.0)
            values = jnp.where(lanes < low_end - low, sources[0], values)
            blocks.append(values[0:9])
            low, high = low_end, high_end
        out_ref[pl.ds(pl.multiple_of(g * 72, 8), 72), :] = jnp.concatenate(blocks, 0)
        return low, high

    lax.fori_loop(0, owners // 8, expand, (0, base))


def pixel_rows():
    pixel = lane_iota(1, K)
    u = ((pixel & (TS - 1)).astype(F32) + 0.5) / TS - 0.5
    v = ((pixel >> 4).astype(F32) + 0.5) / TS - 0.5
    one = jnp.ones((1, K), F32)
    zero = jnp.zeros((2, K), F32)
    return jnp.concatenate([u * u, u * v, v * v, u, v, one, zero], 0)


def tile_kernel(
    unrolls,
    counts_ref,
    owner_ref,
    rank_ref,
    cot_ref,
    fetched_ref,
    out_ref,
    table_ref,
    grad_ref,
    dots_ref,
    entry_ref,
    coef_ref,
    sums_ref,
):
    tiles = rank_ref.shape[0]
    owners = fetched_ref.shape[0] // 9
    unrolls = [math.gcd(tiles, n) for n in unrolls]
    half = owners // 2
    for c in range(9):
        even = fetched_ref[pl.ds(c, half, stride=18), :]
        odd = fetched_ref[pl.ds(9 + c, half, stride=18), :]
        high, low = split2(jnp.concatenate([even, odd], 1))
        table_ref[c * half : (c + 1) * half, :] = jnp.concatenate([high, low], 1)
    grad_ref[...] = jnp.zeros_like(grad_ref)
    pixels = pixel_rows()
    monomials = pixels.astype(BF16)
    pixel_columns = jnp.concatenate([pixels] * 4, 0).T.astype(BF16)
    before = (row_iota(K, K) < lane_iota(K, K)).astype(BF16)
    after = (row_iota(K, K) > lane_iota(K, K)).astype(BF16)
    dots_ref[0:K] = before
    dots_ref[K : 2 * K] = after

    def owner_row(t):
        row = owner_ref[:, pl.ds(pl.multiple_of(t * K, K), K)]
        return jnp.where(lane_iota(1, K) < counts_ref[0, t], row, -1)

    def hot_place(t):
        row = owner_row(t)
        return hot16(2 * LANES, rank_ref[pl.ds(t, 1), :] + (row & 1) * LANES)

    def fetch(g, _):
        several = [unrolls[0] * g + i for i in range(unrolls[0])]
        hots = [hot_place(t) for t in several]
        spreads = [dot_nn(table_ref[...], jnp.concatenate([hot, hot], 0)) for hot in hots]
        for t, spread in zip(several, spreads):
            named = row_iota(half, K) == (owner_row(t) >> 1)
            for c in range(9):
                kept = jnp.where(named, spread[c * half : (c + 1) * half], 0.0)
                entry_ref[c, pl.ds(t, 1), :] = jnp.sum(kept, axis=0, keepdims=True)
        return 0

    lax.fori_loop(0, tiles // unrolls[0], fetch, 0)
    cx, cy = entry_ref[0] - 0.5, entry_ref[1] - 0.5
    a, b, c2 = entry_ref[2], entry_ref[3], entry_ref[4]
    opacity = 1.0 / (1.0 + jnp.exp(-entry_ref[8]))
    spots = lane_iota(1, K)
    left = jnp.concatenate([counts_ref[0, t] - spots for t in range(tiles)], 0)
    ax, ay = a * cx + b * cy, b * cx + c2 * cy
    base = jnp.log(0.99 * opacity) * LOG2E - (0.5 * LOG2E) * (ax * cx + ay * cy)
    coefs = [
        (-0.5 * LOG2E) * a,
        -LOG2E * b,
        (-0.5 * LOG2E) * c2,
        LOG2E * ax,
        LOG2E * ay,
        jnp.where(left > 0, base, -400.0),
    ]
    for i, coef in enumerate(coefs):
        coef_ref[:, i, :] = coef
    coef_ref[:, 6, :] = jnp.zeros_like(a)
    coef_ref[:, 7, :] = jnp.zeros_like(a)

    def scans(arrays, triangle):
        parts = [part for array in arrays for part in split2(array)]
        done = dot_nn(jnp.concatenate(parts, 0), triangle)
        pieces = [done[i * K : (i + 1) * K] for i in range(len(parts))]
        return [high + low for high, low in zip(pieces[0::2], pieces[1::2])]

    def shade(g, _):
        several = [unrolls[1] * g + i for i in range(unrolls[1])]
        blank, pad = jnp.zeros((8, K), BF16), jnp.zeros((4, K), F32)
        exponents = [
            dot_nn(pixel_columns, jnp.concatenate([*split3(coef_ref[t]), blank], 0))
            for t in several
        ]
        slopes, cot_rows = [], []
        for t in several:
            cot_high, cot_low = split2(cot_ref[t])
            ch, cl = cot_high.astype(F32), cot_low.astype(F32)
            cot_columns = jnp.concatenate([ch, ch, cl, cl, pad], 0).T.astype(BF16)
            colors = jnp.concatenate([entry_ref[c, pl.ds(t, 1), :] for c in range(5, 8)], 0)
            color_high, color_low = split2(colors)
            kh, kl = color_high.astype(F32), color_low.astype(F32)
            color_rows = jnp.concatenate([kh, kl, kh, kl, pad], 0).astype(BF16)
            slopes.append(dot_nn(cot_columns, color_rows))
            cot_rows.append(jnp.concatenate([ch, cl, pad[0:2]], 0).astype(BF16))
        alphas = [jnp.exp2(exponent) for exponent in exponents]
        log_keeps = [jnp.log(1.0 - alpha) for alpha in alphas]
        prefixes = scans(log_keeps, dots_ref[0:K])
        weights = [jnp.exp(prefix) * alpha for prefix, alpha in zip(prefixes, alphas)]
        pulls = [weight * slope for weight, slope in zip(weights, slopes)]
        suffixes = scans(pulls, dots_ref[K : 2 * K])
        for t, weight, rows in zip(several, weights, cot_rows):
            both = jnp.concatenate(split2(weight), 0)
            sums_ref[t, 8:16, :] = dot_nn(jnp.concatenate([rows, rows], 1), both)
        mass = jnp.concatenate([monomials, monomials], 1)
        for t, alpha, log_keep, pull, suffix in zip(several, alphas, log_keeps, pulls, suffixes):
            q = pull - alpha * jnp.exp(-log_keep) * suffix
            sums_ref[t, 0:8, :] = dot_nn(mass, jnp.concatenate(split2(q), 0))
        return 0

    lax.fori_loop(0, tiles // unrolls[1], shade, 0)
    mxx, mxy, myy, mx, my, m0 = [sums_ref[:, i, :] for i in range(6)]
    sx, sy = mx - cx * m0, my - cy * m0
    entry_ref[0] = a * sx + b * sy
    entry_ref[1] = b * sx + c2 * sy
    entry_ref[2] = -0.5 * (mxx - cx * (mx + sx))
    entry_ref[3] = -(mxy - cx * my - cy * sx)
    entry_ref[4] = -0.5 * (myy - cy * (my + sy))
    for i in range(3):
        entry_ref[5 + i] = sums_ref[:, 8 + i, :] + sums_ref[:, 11 + i, :]
    entry_ref[8] = (1.0 - opacity) * m0

    def give(g, _):
        sides, hots = [], []
        for i in range(unrolls[2]):
            t = unrolls[2] * g + i
            hot = hot_place(t)
            hits = hits16(half, owner_row(t) >> 1)
            placed = []
            for c in range(9):
                high, low = split2(entry_ref[c, pl.ds(t, 1), :])
                placed.append(jnp.concatenate([keep16(hits, high), keep16(hits, low)], 1))
            sides.append(jnp.concatenate(placed, 0))
            hots += [hot, hot]
        grad_ref[...] += dot_nt(jnp.concatenate(sides, 1), jnp.concatenate(hots, 1))
        return 0

    lax.fori_loop(0, tiles // unrolls[2], give, 0)
    for c in range(9):
        part = grad_ref[c * half : (c + 1) * half, :]
        out_ref[pl.ds(c, half, stride=18), :] = part[:, :LANES]
        out_ref[pl.ds(9 + c, half, stride=18), :] = part[:, LANES:]


def collect_kernel(ends_ref, vals_ref, geo_ref, look_ref):
    owners = vals_ref.shape[0] // 9
    base = owners * LANES - ends_ref[0, 2 * owners - 1]
    geo_ref[...] = jnp.zeros_like(geo_ref)
    look_ref[...] = jnp.zeros_like(look_ref)
    blank = jnp.zeros((7, LANES), F32)

    def row_at(g, j):
        rows = vals_ref[pl.ds(pl.multiple_of(g * 72, 8), 72), :]
        return jnp.concatenate([rows[9 * j : 9 * j + 9], blank], 0)

    def load(at):
        return jnp.concatenate([geo_ref[at, 0:5], look_ref[at], blank], 0)

    def store(at, block):
        geo_ref[pl.ds(at, 1), 0:5, :] = block[None, 0:5]
        look_ref[pl.ds(at, 1), :, :] = block[None, 5:9]

    for bucket in range(2):
        compact(owners, ends_ref, bucket, base if bucket else 0, row_at, load, store)


def add_chunks(ids_ref, value_refs, totals, owners, acc_ref, transposed=False):
    def chunk(row, bucket, wide):
        sides, hots = [], []
        for at in range(0, wide, 2):
            first = row + at
            ids = ids_row(ids_ref, first)
            hot = hot_rows(ids, bucket)
            hits = hits16(LOW, ids & (LOW - 1))
            stacked = []
            for ref, number in value_refs:
                for c in range(number):
                    pair = jnp.concatenate(
                        [ref[first, c : c + 1, :], ref[first + 1, c : c + 1, :]], 1
                    )
                    high, low = split2(pair)
                    stacked.append(
                        jnp.concatenate([keep16(hits, high), keep16(hits, low)], 1)
                    )
            sides.append(jnp.concatenate(stacked, 0))
            hots += [hot, hot]
        side, hot = jnp.concatenate(sides, 1), jnp.concatenate(hots, 1)
        if transposed:
            acc_ref[bucket] += dot_nt(hot, side)
        else:
            acc_ref[bucket] += dot_nt(side, hot)

    each_chunk(totals, owners, chunk)


def scatter_kernel(ends_ref, ids_ref, geo_vals_ref, look_vals_ref, geo_ref, look_acc_ref, acc_ref):
    owners = geo_vals_ref.shape[0] - 1
    totals = ends_ref[0, owners - 1], ends_ref[0, 2 * owners - 1]
    acc_ref[...] = jnp.zeros_like(acc_ref)
    add_chunks(ids_ref, [(geo_vals_ref, 5), (look_vals_ref, 4)], totals, owners, acc_ref)
    for c in range(5):
        at = slice(c * LOW, (c + 1) * LOW)
        geo_ref[c] = jnp.concatenate([acc_ref[0, at], acc_ref[1, at]], 0).T
    look_acc_ref[...] = acc_ref[:, 5 * LOW :, :]


def finish_kernel(*refs):
    others = (len(refs) - 3) // 2
    ids_refs, vals_refs = refs[:others], refs[others : 2 * others]
    start_ref, look_ref, acc_ref = refs[2 * others :]
    owners = vals_refs[0].shape[0] - 1
    places = [ref[owners + 1 : owners + 2, :] for ref in ids_refs]
    totals = [(place[0, owners - 1], place[0, 2 * owners - 1]) for place in places]
    for bucket in range(2):
        acc_ref[bucket] = start_ref[bucket].T
    for i, ends in enumerate(totals):
        add_chunks(ids_refs[i], [(vals_refs[i], 4)], ends, owners, acc_ref, transposed=True)
    for c in range(4):
        at = slice(c * LOW, (c + 1) * LOW)
        look_ref[:, c, :] = jnp.concatenate([acc_ref[0, :, at], acc_ref[1, :, at]], 1)


HBM = pl.BlockSpec(memory_space=pltpu.HBM)
VMEM = pl.BlockSpec(memory_space=pltpu.VMEM)
SMEM = pl.BlockSpec(memory_space=pltpu.SMEM)
LIMIT = pltpu.CompilerParams(vmem_limit_bytes=40 * 1024 * 1024)


def exchange(values, owners, axis="owner"):
    sent = values.reshape(owners, 1, -1)
    got = lax.all_to_all(sent, axis, split_axis=0, concat_axis=0, tiled=True)
    return got.reshape(values.shape)


def shards(geometry, appearance, list_owner, list_local, counts, cotangent):
    owners = lax.axis_size("owner")
    views = lax.axis_size("view")
    tiles = counts.shape[1]
    gauss = geometry.shape[2]
    rows = gauss // LANES
    target = list_owner.reshape(1, tiles * K)
    requests, ranks = pl.pallas_call(
        plan_kernel,
        out_shape=(
            jax.ShapeDtypeStruct((owners, LANES), jnp.int32),
            jax.ShapeDtypeStruct((tiles, K), jnp.int32),
        ),
        in_specs=[SMEM, HBM, HBM],
        out_specs=(VMEM, VMEM),
        scratch_shapes=[
            pltpu.VMEM((1, tiles * K), jnp.int32),
            pltpu.VMEM((1, tiles * K), jnp.int32),
            pltpu.SemaphoreType.DMA((2,)),
        ],
        compiler_params=pltpu.CompilerParams(vmem_limit_bytes=60 * 1024 * 1024),
    )(counts, target, list_local)
    table = pl.pallas_call(
        table_kernel,
        out_shape=jax.ShapeDtypeStruct((2, 9 * LOW, 512), BF16),
        in_specs=[VMEM, VMEM],
        out_specs=VMEM,
        compiler_params=LIMIT,
    )(geometry.reshape(5, rows, LANES), appearance.reshape(4, rows, LANES))
    asked = exchange(requests, owners)
    picked, packed = pl.pallas_call(
        gather_kernel,
        out_shape=(
            jax.ShapeDtypeStruct((owners * 9, LANES), F32),
            jax.ShapeDtypeStruct((owners + 8, LANES), jnp.int32),
        ),
        in_specs=[VMEM, VMEM],
        out_specs=(VMEM, VMEM),
        scratch_shapes=[
            pltpu.SMEM((8, LANES), jnp.int32),
            pltpu.VMEM((2, owners + 2, 16, LANES), F32),
        ],
        compiler_params=LIMIT,
    )(asked, table)
    fetched = exchange(picked, owners)
    shifts = [[(i, (i + k) % views) for i in range(views)] for k in range(1, views)]
    other_ids = [lax.ppermute(packed, "view", shift) for shift in shifts]
    fetched, other_ids = lax.optimization_barrier((fetched, other_ids))
    outgoing = pl.pallas_call(
        functools.partial(tile_kernel, (16, 8, 16)),
        out_shape=jax.ShapeDtypeStruct((owners * 9, LANES), F32),
        in_specs=[SMEM, VMEM, VMEM, VMEM, VMEM],
        out_specs=VMEM,
        scratch_shapes=[
            pltpu.VMEM((9 * owners // 2, 4 * LANES), BF16),
            pltpu.VMEM((9 * owners // 2, 2 * LANES), F32),
            pltpu.VMEM((2 * K, K), BF16),
            pltpu.VMEM((9, tiles, K), F32),
            pltpu.VMEM((tiles, 8, K), F32),
            pltpu.VMEM((tiles, 16, K), F32),
        ],
        compiler_params=LIMIT,
    )(counts, target, ranks, cotangent[0], fetched)
    returned = exchange(outgoing, owners)
    ends = packed[owners + 1 :]
    geo_vals, look_vals = pl.pallas_call(
        collect_kernel,
        out_shape=(
            jax.ShapeDtypeStruct((owners + 1, 8, LANES), F32),
            jax.ShapeDtypeStruct((owners + 1, 4, LANES), F32),
        ),
        in_specs=[SMEM, VMEM],
        out_specs=(VMEM, VMEM),
        compiler_params=LIMIT,
    )(ends, returned)
    other_vals = [lax.ppermute(look_vals, "view", shift) for shift in shifts]
    geo, look_acc = pl.pallas_call(
        scatter_kernel,
        out_shape=(
            jax.ShapeDtypeStruct((5, rows, LANES), F32),
            jax.ShapeDtypeStruct((2, 4 * LOW, 256), F32),
        ),
        in_specs=[SMEM, VMEM, VMEM, VMEM],
        out_specs=(VMEM, VMEM),
        scratch_shapes=[pltpu.VMEM((2, 9 * LOW, 256), F32)],
        compiler_params=LIMIT,
    )(ends, packed, geo_vals, look_vals)
    look = pl.pallas_call(
        finish_kernel,
        out_shape=jax.ShapeDtypeStruct((rows, 4, LANES), F32),
        in_specs=[VMEM] * (2 * views - 1),
        out_specs=VMEM,
        scratch_shapes=[
            pltpu.VMEM((2, 256, 4 * LOW), F32),
        ],
        compiler_params=LIMIT,
    )(*other_ids, *other_vals, look_acc)
    look = jnp.transpose(look, (1, 0, 2)).reshape(4, gauss)
    return (geo.reshape(1, 5, gauss), look)


def solution(mesh):
    placed = (
        P("view", None, "owner"),
        P(None, "owner"),
        P("view", "owner", None),
        P("view", "owner"),
        P("view", "owner"),
        P("view", "owner", None, None),
    )
    return jax.shard_map(
        shards,
        mesh=mesh,
        in_specs=placed,
        out_specs=(P("view", None, "owner"), P(None, "owner")),
        check_vma=False,
    )
```

time: 112 us -> 99.8 us (0.89); the launches traced: 110 us -> 99.1 us
  Pallas kernels: 40.1 us -> 29.4 us
  waiting for transfers between devices: 34.2 us -> 37.5 us
  local copies, waits for them, and re-layouts: 3.29 us -> 1.15 us
  starting transfers between devices: 31.6 us -> 30.4 us
    pallas_call x1, Pallas kernels: 8.79 us -> 4.56 us  [shards(): pl.pallas_call(finish_kernel, out_shape=jax.ShapeDtypeStruct((rows, 4, LA...]
    ppermute x3, waiting for transfers between devices: 2.59 us -> 5.63 us  [shards(): other_vals = [lax.ppermute(look_vals, 'view', shift) for shift in shifts]]
    pallas_call x1, Pallas kernels: 6.01 us -> 3.39 us  [shards(): pl.pallas_call(scatter_kernel, out_shape=(jax.ShapeDtypeStruct((5, rows,...]
    unnamed x16 -> x12, local copies, waits for them, and re-layouts: 3.29 us -> 1.14 us
    pallas_call x3, Pallas kernels: 14.7 us -> 12.6 us  [the longest x1 10.2 us: shards(): pl.pallas_call(functools.partial(tile_kernel, (16, 8, 16)), out_shape=jax...]
    pallas_call x1, Pallas kernels: 7.32 us -> 5.4 us  [shards(): pl.pallas_call(gather_kernel, out_shape=(jax.ShapeDtypeStruct((owners * 9...]
  transfers between devices with their start and end apart: 9 -> 9, of which waited for: 6 -> 8; matrix products, arithmetic and copies ran while one was open for 1% -> 1% of each run, Pallas kernels for 6% -> 4%
where the time goes in v3:
time: 99.8 us; the launch traced here: 99.1 us
  waiting for transfers between devices  37.5 us (38%)
  starting transfers between devices  30.4 us (30%)
  Pallas kernels  29.4 us (29%)
  local copies, waits for them, and re-layouts  1.15 us (1%)
    all_to_all x3, waiting for transfers between devices, exchange(): got = lax.all_to_all(sent, axis, split_axis=0, concat_axis=0, tiled=True)  27.7 us
    all_to_all x3, starting transfers between devices, exchange(): got = lax.all_to_all(sent, axis, split_axis=0, concat_axis=0, tiled=True)  24.2 us
    pallas_call x1, Pallas kernels, shards(): pl.pallas_call(functools.partial(tile_kernel, (16, 8, 16)), out_shape=jax...  10.2 us
    ppermute x3, waiting for transfers between devices, shards(): other_vals = [lax.ppermute(look_vals, 'view', shift) for shift in shifts]  5.63 us
    pallas_call x1, Pallas kernels, shards(): pl.pallas_call(gather_kernel, out_shape=(jax.ShapeDtypeStruct((owners * 9...  5.4 us
    pallas_call x1, Pallas kernels, shards(): pl.pallas_call(finish_kernel, out_shape=jax.ShapeDtypeStruct((rows, 4, LA...  4.56 us
    ppermute x3, waiting for transfers between devices, shards(): other_ids = [lax.ppermute(packed, 'view', shift) for shift in shifts]  4.16 us
    pallas_call x1, Pallas kernels, shards(): pl.pallas_call(scatter_kernel, out_shape=(jax.ShapeDtypeStruct((5, rows,...  3.39 us
  transfers between devices with their start and end apart: 9, of which 8 were waited for; matrix products, arithmetic and copies ran while one was open for 1% of the time, Pallas kernels for 4%

profile of v3, /device:TPU:1, one launch (start us, length us, event | category | flops | bytes accessed | tf_op | source)
XLA Modules:
  0.0 99.1 jit_solution(4364809134628002271)
XLA Ops:
  0.6 0.0 copy-start
  0.6 3.4 %shard_map.77 = (s32[64,128]{1,0:T(8,128)}, s32[16,256]{1,0:T(8,128)}) custom-call(s32[1,16]{1,0:T(1,128)} %counts_ref.3, s32[1,4096]{1,0:T(1,128)} %bitcast.27, s32[1,4096]{1,0:T(1,128)} %local_hbm.1), custom_call_target="tpu_custom_call" | custom-call | tf_op jit(solution)/shard_map/pallas_call | solution.py:505
  4.0 13.2 %all-to-all-start = ((s32[64,1,128]{2,1,0:T(1,128)}), s32[64,1,128]{2,1,0:T(1,128)S(1)}, u32[]{:S(2)}, u32[]{:S(2)}) async-start(s32[64,1,128]{2,1,0:T(1,128)} %bitcast.31), calls=%async_computation | async-start | bytes 65536 | tf_op jit(solution)/shard_map/all_to_all | solution.py:494
  17.2 1.1 %copy.20 = f32[1,4,256,128]{3,2,1,0:T(8,128)S(1)} copy(f32[1,4,256,128]{3,1,2,0:T(4,128)} %bitcast.29) | data formatting | bytes 1048576
  18.3 0.0 copy-done
  18.3 0.4 shard_map.78.table_ref
  18.7 0.0 copy-start.4
  18.7 0.0 copy-start.1
  18.7 0.0 copy-start.2
  18.7 0.0 copy-start.3
  18.7 7.8 %all-to-all-done = s32[64,1,128]{2,1,0:T(1,128)S(1)} async-done(((s32[64,1,128]{2,1,0:T(1,128)}), s32[64,1,128]{2,1,0:T(1,128)S(1)}, u32[]{:S(2)}, u32[]{:S(2)}) %all-to-all-start) | async-done | bytes 32800 | tf_op jit(solution)/shard_map/all_to_all | solution.py:494
  26.5 5.4 %shard_map.79 = (f32[576,128]{1,0:T(8,128)}, s32[72,128]{1,0:T(8,128)S(1)}) custom-call(s32[64,128]{1,0:T(8,128)S(1)} %bitcast.26, bf16[2,576,512]{2,1,0:T(8,128)(2,1)S(1)} %shard_map.78.table_ref), custom_call_target="tpu_custom_call" | custom-call | tf_op jit(solution)/shard_map/pallas_call | solution.py:528
  31.9 5.7 %all-to-all-start.1 = ((f32[64,1,1152]{2,1,0:T(1,128)}), f32[64,1,1152]{2,1,0:T(1,128)S(1)}, u32[]{:S(2)}, u32[]{:S(2)}) async-start(f32[64,1,1152]{2,1,0:T(1,128)} %bitcast.6), calls=%async_computation.1 | async-start | bytes 589824 | tf_op jit(solution)/shard_map/all_to_all | solution.py:494
  37.6 2.6 %collective-permute-start.2 = (s32[72,128]{1,0:T(8,128)S(1)}, s32[72,128]{1,0:T(8,128)S(1)}, u32[]{:S(2)}, u32[]{:S(2)}) collective-permute-start(s32[72,128]{1,0:T(8,128)S(1)} %get-tuple-element.15.ids_ref), channel_id=1, source_target_pairs={{0,3},{1,0},{2,1},{3,2},{4,7},{5,4},{6,5},{7,6},{8,11},{9,8},{10,9... | collective-permute-start | bytes 110600 | tf_op jit(solution)/shard_map/ppermute | solution.py:544
  40.1 0.5 collective-permute-start.1
  40.7 0.3 collective-permute-start
  40.9 0.0 copy-done.4
  41.0 0.2 collective-permute-done.2.refs_2_
  41.2 3.5 %collective-permute-done.1.refs_1_ = s32[72,128]{1,0:T(8,128)S(1)} collective-permute-done((s32[72,128]{1,0:T(8,128)S(1)}, s32[72,128]{1,0:T(8,128)S(1)}, u32[]{:S(2)}, u32[]{:S(2)}) %collective-permute-start.1) | collective-permute-done | bytes 36896 | tf_op jit(solution)/shard_map/ppermute | solution.py:544
  44.7 0.4 collective-permute-done.refs_0_
  45.1 6.2 %all-to-all-done.1 = f32[64,1,1152]{2,1,0:T(1,128)S(1)} async-done(((f32[64,1,1152]{2,1,0:T(1,128)}), f32[64,1,1152]{2,1,0:T(1,128)S(1)}, u32[]{:S(2)}, u32[]{:S(2)}) %all-to-all-start.1) | async-done | bytes 294944 | tf_op jit(solution)/shard_map/all_to_all | solution.py:494
  51.3 0.0 copy-done.1
  51.3 0.0 copy-done.2
  51.3 0.0 copy-done.3
  51.3 10.2 %shard_map.80 = f32[576,128]{1,0:T(8,128)} custom-call(s32[1,16]{1,0:T(1,128)S(1)} %copy-done.3, s32[1,4096]{1,0:T(1,128)S(1)} %bitcast.28, s32[16,256]{1,0:T(8,128)S(1)} %copy-done.2, f32[16,3,256]{2,1,0:T(4,128)S(1)} %bitcast.25, f32[576,128]{1,0:T(8,128)S(1)} %bitcast.22), custom_call_target="tpu_custom_call" | custom-call | tf_op jit(solution)/shard_map/pallas_call | solution.py:546
  61.5 5.4 %all-to-all-start.2 = ((f32[64,1,1152]{2,1,0:T(1,128)}), f32[64,1,1152]{2,1,0:T(1,128)S(1)}, u32[]{:S(2)}, u32[]{:S(2)}) async-start(f32[64,1,1152]{2,1,0:T(1,128)} %bitcast.8), calls=%async_computation.2 | async-start | bytes 589824 | tf_op jit(solution)/shard_map/all_to_all | solution.py:494
  66.9 13.7 %all-to-all-done.2 = f32[64,1,1152]{2,1,0:T(1,128)S(1)} async-done(((f32[64,1,1152]{2,1,0:T(1,128)}), f32[64,1,1152]{2,1,0:T(1,128)S(1)}, u32[]{:S(2)}, u32[]{:S(2)}) %all-to-all-start.2) | async-done | bytes 294944 | tf_op jit(solution)/shard_map/all_to_all | solution.py:494
  80.6 2.1 %shard_map.81 = (f32[65,8,128]{2,1,0:T(8,128)S(1)}, f32[65,4,128]{2,1,0:T(4,128)S(1)}) custom-call(s32[7,128]{1,0:T(8,128)S(1)} %slice.3.ends_ref, f32[576,128]{1,0:T(8,128)S(1)} %bitcast.23), custom_call_target="tpu_custom_call" | custom-call | tf_op jit(solution)/shard_map/pallas_call | solution.py:563
  82.7 2.0 %collective-permute-start.5 = (f32[65,4,128]{2,1,0:T(4,128)S(1)}, f32[65,4,128]{2,1,0:T(4,128)S(1)}, u32[]{:S(2)}, u32[]{:S(2)}) collective-permute-start(f32[65,4,128]{2,1,0:T(4,128)S(1)} %get-tuple-element.20.look_vals_ref), channel_id=1, source_target_pairs={{0,3},{1,0},{2,1},{3,2},{4,7},{5,4},{6,5},{7,6},{8,11},{9,8},{10,9... | collective-permute-start | bytes 399368 | tf_op jit(solution)/shard_map/ppermute | solution.py:573
  84.7 0.5 collective-permute-start.4
  85.2 0.3 collective-permute-start.3
  85.5 3.4 %shard_map.82 = (f32[5,256,128]{2,1,0:T(8,128)}, f32[2,256,256]{2,1,0:T(8,128)S(1)}) custom-call(s32[7,128]{1,0:T(8,128)S(1)} %slice.3.ends_ref, s32[72,128]{1,0:T(8,128)S(1)} %get-tuple-element.15.ids_ref, f32[65,8,128]{2,1,0:T(8,128)S(1)} %get-tuple-element.19.geo_vals_ref, f32[65,4,128]{2,1,0:T(4,128)S(1)} %get-tuple-element.20.look_vals_ref), custom_call_target="tpu_custom_call" | custom-call | tf_op jit(solution)/shard_map/pallas_call | solution.py:574
  88.9 0.0 collective-permute-done.5.refs_5_
  88.9 2.0 %collective-permute-done.4.refs_4_ = f32[65,4,128]{2,1,0:T(4,128)S(1)} collective-permute-done((f32[65,4,128]{2,1,0:T(4,128)S(1)}, f32[65,4,128]{2,1,0:T(4,128)S(1)}, u32[]{:S(2)}, u32[]{:S(2)}) %collective-permute-start.4) | collective-permute-done | bytes 133152 | tf_op jit(solution)/shard_map/ppermute | solution.py:573
  90.9 3.6 %collective-permute-done.3.refs_3_ = f32[65,4,128]{2,1,0:T(4,128)S(1)} collective-permute-done((f32[65,4,128]{2,1,0:T(4,128)S(1)}, f32[65,4,128]{2,1,0:T(4,128)S(1)}, u32[]{:S(2)}, u32[]{:S(2)}) %collective-permute-start.3) | collective-permute-done | bytes 133152 | tf_op jit(solution)/shard_map/ppermute | solution.py:573
  94.5 4.6 %shard_map.83 = f32[256,4,128]{2,1,0:T(4,128)} custom-call(s32[72,128]{1,0:T(8,128)S(1)} %collective-permute-done.refs_0_, s32[72,128]{1,0:T(8,128)S(1)} %collective-permute-done.1.refs_1_, s32[72,128]{1,0:T(8,128)S(1)} %collective-permute-done.2.refs_2_, f32[65,4,128]{2,1,0:T(4,128)S(1)} %collective-permute-done.3.refs_3_, ...), custom_call_target="tpu_custom_call" | custom-call | tf_op jit(solution)/shard_map/pallas_call | solution.py:585
  (2 shorter events, 0.0 us)
Async XLA Ops:
  0.6 17.6 %copy-start = (f32[1,5,32768]{2,0,1:T(1,128)S(1)}, f32[1,5,32768]{2,0,1:T(1,128)}, u32[]{:S(2)}) copy-start(f32[1,5,32768]{2,0,1:T(1,128)} %param.6) | copy-start | bytes 1966084
  4.0 22.5 %all-to-all-start = ((s32[64,1,128]{2,1,0:T(1,128)}), s32[64,1,128]{2,1,0:T(1,128)S(1)}, u32[]{:S(2)}, u32[]{:S(2)}) async-start(s32[64,1,128]{2,1,0:T(1,128)} %bitcast.31), calls=%async_computation | async-start | bytes 65536 | tf_op jit(solution)/shard_map/all_to_all | solution.py:494
  18.7 22.3 %copy-start.4 = (f32[1,16,3,256]{3,1,2,0:T(8,128)S(1)}, f32[1,16,3,256]{3,1,2,0:T(8,128)}, u32[]{:S(2)}) copy-start(f32[1,16,3,256]{3,1,2,0:T(8,128)} %param.11) | copy-start | bytes 147460
  18.7 32.6 %copy-start.1 = (s32[1,4096,1]{1,2,0:T(1,128)S(1)}, s32[1,4096,1]{1,2,0:T(1,128)}, u32[]{:S(2)}) copy-start(s32[1,4096,1]{1,2,0:T(1,128)} %param.8) | copy-start | bytes 49156
  18.7 32.6 %copy-start.2 = (s32[16,256]{1,0:T(8,128)S(1)}, s32[16,256]{1,0:T(8,128)}, u32[]{:S(2)}) copy-start(s32[16,256]{1,0:T(8,128)} %get-tuple-element.16.rank_ref) | copy-start | bytes 49156
  18.7 32.6 %copy-start.3 = (s32[1,16]{1,0:T(1,128)S(1)}, s32[1,16]{1,0:T(1,128)}, u32[]{:S(2)}) copy-start(s32[1,16]{1,0:T(1,128)} %counts_ref.3) | copy-start | bytes 196
  31.9 19.4 %all-to-all-start.1 = ((f32[64,1,1152]{2,1,0:T(1,128)}), f32[64,1,1152]{2,1,0:T(1,128)S(1)}, u32[]{:S(2)}, u32[]{:S(2)}) async-start(f32[64,1,1152]{2,1,0:T(1,128)} %bitcast.6), calls=%async_computation.1 | async-start | bytes 589824 | tf_op jit(solution)/shard_map/all_to_all | solution.py:494
  37.6 3.6 %collective-permute-start.2 = (s32[72,128]{1,0:T(8,128)S(1)}, s32[72,128]{1,0:T(8,128)S(1)}, u32[]{:S(2)}, u32[]{:S(2)}) collective-permute-start(s32[72,128]{1,0:T(8,128)S(1)} %get-tuple-element.15.ids_ref), channel_id=1, source_target_pairs={{0,3},{1,0},{2,1},{3,2},{4,7},{5,4},{6,5},{7,6},{8,11},{9,8},{10,9... | collective-permute-start | bytes 110600 | tf_op jit(solution)/shard_map/ppermute | solution.py:544
  40.1 4.6 %collective-permute-start.1 = (s32[72,128]{1,0:T(8,128)S(1)}, s32[72,128]{1,0:T(8,128)S(1)}, u32[]{:S(2)}, u32[]{:S(2)}) collective-permute-start(s32[72,128]{1,0:T(8,128)S(1)} %get-tuple-element.15.ids_ref), channel_id=1, source_target_pairs={{0,2},{1,3},{2,0},{3,1},{4,6},{5,7},{6,4},{7,5},{8,10},{9,11},{10,... | collective-permute-start | bytes 110600 | tf_op jit(solution)/shard_map/ppermute | solution.py:544
  40.7 4.5 %collective-permute-start = (s32[72,128]{1,0:T(8,128)S(1)}, s32[72,128]{1,0:T(8,128)S(1)}, u32[]{:S(2)}, u32[]{:S(2)}) collective-permute-start(s32[72,128]{1,0:T(8,128)S(1)} %get-tuple-element.15.ids_ref), channel_id=1, source_target_pairs={{0,1},{1,2},{2,3},{3,0},{4,5},{5,6},{6,7},{7,4},{8,9},{9,10},{10,1... | collective-permute-start | bytes 110600 | tf_op jit(solution)/shard_map/ppermute | solution.py:544
  61.5 19.1 %all-to-all-start.2 = ((f32[64,1,1152]{2,1,0:T(1,128)}), f32[64,1,1152]{2,1,0:T(1,128)S(1)}, u32[]{:S(2)}, u32[]{:S(2)}) async-start(f32[64,1,1152]{2,1,0:T(1,128)} %bitcast.8), calls=%async_computation.2 | async-start | bytes 589824 | tf_op jit(solution)/shard_map/all_to_all | solution.py:494
  82.7 6.2 %collective-permute-start.5 = (f32[65,4,128]{2,1,0:T(4,128)S(1)}, f32[65,4,128]{2,1,0:T(4,128)S(1)}, u32[]{:S(2)}, u32[]{:S(2)}) collective-permute-start(f32[65,4,128]{2,1,0:T(4,128)S(1)} %get-tuple-element.20.look_vals_ref), channel_id=1, source_target_pairs={{0,3},{1,0},{2,1},{3,2},{4,7},{5,4},{6,5},{7,6},{8,11},{9,8},{10,9... | collective-permute-start | bytes 399368 | tf_op jit(solution)/shard_map/ppermute | solution.py:573
  84.7 6.2 %collective-permute-start.4 = (f32[65,4,128]{2,1,0:T(4,128)S(1)}, f32[65,4,128]{2,1,0:T(4,128)S(1)}, u32[]{:S(2)}, u32[]{:S(2)}) collective-permute-start(f32[65,4,128]{2,1,0:T(4,128)S(1)} %get-tuple-element.20.look_vals_ref), channel_id=1, source_target_pairs={{0,2},{1,3},{2,0},{3,1},{4,6},{5,7},{6,4},{7,5},{8,10},{9,11},{10,... | collective-permute-start | bytes 399368 | tf_op jit(solution)/shard_map/ppermute | solution.py:573
  85.2 9.3 %collective-permute-start.3 = (f32[65,4,128]{2,1,0:T(4,128)S(1)}, f32[65,4,128]{2,1,0:T(4,128)S(1)}, u32[]{:S(2)}, u32[]{:S(2)}) collective-permute-start(f32[65,4,128]{2,1,0:T(4,128)S(1)} %get-tuple-element.20.look_vals_ref), channel_id=1, source_target_pairs={{0,1},{1,2},{2,3},{3,0},{4,5},{5,6},{6,7},{7,4},{8,9},{9,10},{10,1... | collective-permute-start | bytes 399368 | tf_op jit(solution)/shard_map/ppermute | solution.py:573

commit v4 on v3

--- a/solution.py
+++ b/solution.py
@@ -152,35 +152,37 @@
     lax.fori_loop(0, small, narrow, 0)
 
 
-def compact(owners, ends_ref, bucket, start, row_at, load, store):
-    lanes = lane_iota(*row_at(0, 0).shape)
+def compact(owners, ends_ref, base, row_at, store):
+    blank = jnp.zeros((8, LANES), row_at(0, 0).dtype)
+    lanes = lane_iota(8, LANES)
 
     def group(g, carry):
-        offset, now = carry
+        carry = list(carry)
         for j in range(8):
             s = g * 8 + j
-            end = start + ends_ref[0, bucket * owners + s]
-            amount = end - offset
             row = row_at(g, j)
-            if bucket == 0:
-                row = jnp.where(lanes < amount, row, jnp.zeros_like(row))
-                rolled = pltpu.roll(row, offset & 127, 1)
-            else:
-                row = jnp.where(lanes >= LANES - amount, row, jnp.zeros_like(row))
-                rolled = pltpu.roll(row, end & 127, 1)
-            fits = lanes >= (offset & 127)
-            block = now + jnp.where(fits, rolled, jnp.zeros_like(rolled))
-            spilt = jnp.where(fits, jnp.zeros_like(rolled), rolled)
-            store(offset >> 7, block)
-            now = jnp.where((end >> 7) > (offset >> 7), spilt, block)
-            offset = end
-        return offset, now
-
-    offset, now = lax.fori_loop(0, owners // 8, group, (start, load(start >> 7)))
-    store(offset >> 7, now)
-
-
-def gather_kernel(asked_ref, table_ref, out_ref, packed_ref, ends_ref, found_ref):
+            for bucket in range(2):
+                offset, now = carry[bucket]
+                end = ends_ref[0, bucket * owners + s] + (base if bucket else 0)
+                if bucket == 0:
+                    part = jnp.where(lanes < end - offset, row, blank)
+                    rolled = pltpu.roll(part, offset & 127, 1)
+                else:
+                    part = jnp.where(lanes >= LANES - (end - offset), row, blank)
+                    rolled = pltpu.roll(part, end & 127, 1)
+                fits = lanes >= (offset & 127)
+                block = now + jnp.where(fits, rolled, blank)
+                spilt = jnp.where(fits, blank, rolled)
+                store(bucket, offset >> 7, block)
+                carry[bucket] = end, jnp.where((end >> 7) > (offset >> 7), spilt, block)
+        return tuple(carry)
+
+    carry = lax.fori_loop(0, owners // 8, group, ((0, blank), (base, blank)))
+    for bucket, (offset, now) in enumerate(carry):
+        store(bucket, offset >> 7, now)
+
+
+def gather_kernel(asked_ref, table_ref, out_ref, packed_ref, ends_ref, held_ref, found_ref):
     owners = asked_ref.shape[0]
     asked = asked_ref[...]
     odd = ((asked - 1) & LOW) != 0
@@ -189,7 +191,7 @@
     upto = (row_iota(owners, owners) >= lane_iota(owners, owners)).astype(F32).astype(BF16)
     sides = ((lane_iota(8, 2 * LANES) >> 7) == row_iota(8, 2 * LANES)).astype(F32).astype(BF16)
     ends = dot_nt(sides, dot_nn(upto, valid).astype(BF16)).astype(jnp.int32)
-    packed_ref[...] = jnp.zeros_like(packed_ref)
+    held_ref[...] = jnp.zeros_like(held_ref)
     for s in range(owners):
         ends_ref[0, s] = ends[0, s]
         ends_ref[0, owners + s] = ends[1, s]
@@ -199,21 +201,18 @@
     def row_at(g, j):
         return jnp.broadcast_to(asked_ref[pl.ds(g * 8 + j, 1), :], (8, LANES))
 
-    def load(at):
-        return jnp.broadcast_to(packed_ref[pl.ds(at, 1), :], (8, LANES))
-
-    def store(at, block):
-        packed_ref[pl.ds(at, 1), :] = block[0:1]
-
-    for bucket in range(2):
-        compact(owners, ends_ref, bucket, base if bucket else 0, row_at, load, store)
+    def store(bucket, at, block):
+        held_ref[bucket, pl.ds(at, 1), :] = block[0:1]
+
+    compact(owners, ends_ref, base, row_at, store)
+    packed_ref[...] = held_ref[0] + held_ref[1]
     packed_ref[owners + 1 : owners + 2, 0 : 2 * owners] = jnp.concatenate(
         [ends[0:1], ends[1:2]], 1
     )
 
     def chunk(row, bucket, wide):
         for at in range(0, wide, 2):
-            ids = ids_row(packed_ref, row + at)
+            ids = ids_row(held_ref.at[bucket], row + at)
             hot = hot_rows(ids, bucket)
             found = dot_nn(table_ref[bucket], jnp.concatenate([hot, hot], 0))
             mask = low_mask(ids)
@@ -405,26 +404,26 @@
         out_ref[pl.ds(9 + c, half, stride=18), :] = part[:, LANES:]
 
 
-def collect_kernel(ends_ref, vals_ref, geo_ref, look_ref):
+def collect(ends_ref, vals_ref, first, number, held_ref):
     owners = vals_ref.shape[0] // 9
     base = owners * LANES - ends_ref[0, 2 * owners - 1]
-    geo_ref[...] = jnp.zeros_like(geo_ref)
-    look_ref[...] = jnp.zeros_like(look_ref)
-    blank = jnp.zeros((7, LANES), F32)
+    held_ref[...] = jnp.zeros_like(held_ref)
+    blank = jnp.zeros((8 - number, LANES), F32)
 
     def row_at(g, j):
         rows = vals_ref[pl.ds(pl.multiple_of(g * 72, 8), 72), :]
-        return jnp.concatenate([rows[9 * j : 9 * j + 9], blank], 0)
-
-    def load(at):
-        return jnp.concatenate([geo_ref[at, 0:5], look_ref[at], blank], 0)
-
-    def store(at, block):
-        geo_ref[pl.ds(at, 1), 0:5, :] = block[None, 0:5]
-        look_ref[pl.ds(at, 1), :, :] = block[None, 5:9]
-
-    for bucket in range(2):
-        compact(owners, ends_ref, bucket, base if bucket else 0, row_at, load, store)
+        at = 9 * j + first
+        return jnp.concatenate([rows[at : at + number], blank], 0)
+
+    def store(bucket, at, block):
+        held_ref[bucket, pl.ds(at, 1), :, :] = block[None]
+
+    compact(owners, ends_ref, base, row_at, store)
+
+
+def collect_kernel(ends_ref, vals_ref, look_ref, held_ref):
+    collect(ends_ref, vals_ref, 5, 4, held_ref)
+    look_ref[...] = held_ref[0, :, 0:4, :] + held_ref[1, :, 0:4, :]
 
 
 def add_chunks(ids_ref, value_refs, totals, owners, acc_ref, transposed=False):
@@ -436,7 +435,7 @@
             hot = hot_rows(ids, bucket)
             hits = hits16(LOW, ids & (LOW - 1))
             stacked = []
-            for ref, number in value_refs:
+            for ref, number in value_refs[bucket]:
                 for c in range(number):
                     pair = jnp.concatenate(
                         [ref[first, c : c + 1, :], ref[first + 1, c : c + 1, :]], 1
@@ -456,28 +455,32 @@
     each_chunk(totals, owners, chunk)
 
 
-def scatter_kernel(ends_ref, ids_ref, geo_vals_ref, look_vals_ref, geo_ref, look_acc_ref, acc_ref):
-    owners = geo_vals_ref.shape[0] - 1
+def scatter_kernel(
+    ends_ref, ids_ref, vals_ref, look_vals_ref, geo_ref, look_acc_ref, acc_ref, held_ref
+):
+    owners = vals_ref.shape[0] // 9
     totals = ends_ref[0, owners - 1], ends_ref[0, 2 * owners - 1]
+    collect(ends_ref, vals_ref, 0, 5, held_ref)
     acc_ref[...] = jnp.zeros_like(acc_ref)
-    add_chunks(ids_ref, [(geo_vals_ref, 5), (look_vals_ref, 4)], totals, owners, acc_ref)
+    values = [[(held_ref.at[bucket], 5), (look_vals_ref, 4)] for bucket in range(2)]
+    add_chunks(ids_ref, values, totals, owners, acc_ref)
     for c in range(5):
         at = slice(c * LOW, (c + 1) * LOW)
         geo_ref[c] = jnp.concatenate([acc_ref[0, at], acc_ref[1, at]], 0).T
-    look_acc_ref[...] = acc_ref[:, 5 * LOW :, :]
-
-
-def finish_kernel(*refs):
-    others = (len(refs) - 3) // 2
-    ids_refs, vals_refs = refs[:others], refs[others : 2 * others]
-    start_ref, look_ref, acc_ref = refs[2 * others :]
-    owners = vals_refs[0].shape[0] - 1
-    places = [ref[owners + 1 : owners + 2, :] for ref in ids_refs]
-    totals = [(place[0, owners - 1], place[0, 2 * owners - 1]) for place in places]
     for bucket in range(2):
-        acc_ref[bucket] = start_ref[bucket].T
-    for i, ends in enumerate(totals):
-        add_chunks(ids_refs[i], [(vals_refs[i], 4)], ends, owners, acc_ref, transposed=True)
+        look_acc_ref[bucket] = acc_ref[bucket, 5 * LOW :, :].T
+
+
+def add_view(ids_ref, vals_ref, start_ref, acc_ref):
+    owners = vals_ref.shape[0] - 1
+    place = ids_ref[owners + 1 : owners + 2, :]
+    acc_ref[...] = start_ref[...]
+    totals = place[0, owners - 1], place[0, 2 * owners - 1]
+    add_chunks(ids_ref, [[(vals_ref, 4)]] * 2, totals, owners, acc_ref, transposed=True)
+
+
+def finish_kernel(ids_ref, vals_ref, start_ref, look_ref, acc_ref):
+    add_view(ids_ref, vals_ref, start_ref, acc_ref)
     for c in range(4):
         at = slice(c * LOW, (c + 1) * LOW)
         look_ref[:, c, :] = jnp.concatenate([acc_ref[0, :, at], acc_ref[1, :, at]], 1)
@@ -535,6 +538,7 @@
         out_specs=(VMEM, VMEM),
         scratch_shapes=[
             pltpu.SMEM((8, LANES), jnp.int32),
+            pltpu.VMEM((2, owners + 8, LANES), jnp.int32),
             pltpu.VMEM((2, owners + 2, 16, LANES), F32),
         ],
         compiler_params=LIMIT,
@@ -560,38 +564,37 @@
     )(counts, target, ranks, cotangent[0], fetched)
     returned = exchange(outgoing, owners)
     ends = packed[owners + 1 :]
-    geo_vals, look_vals = pl.pallas_call(
+    look_vals = pl.pallas_call(
         collect_kernel,
-        out_shape=(
-            jax.ShapeDtypeStruct((owners + 1, 8, LANES), F32),
-            jax.ShapeDtypeStruct((owners + 1, 4, LANES), F32),
-        ),
+        out_shape=jax.ShapeDtypeStruct((owners + 1, 4, LANES), F32),
         in_specs=[SMEM, VMEM],
-        out_specs=(VMEM, VMEM),
+        out_specs=VMEM,
+        scratch_shapes=[pltpu.VMEM((2, owners + 1, 8, LANES), F32)],
         compiler_params=LIMIT,
     )(ends, returned)
     other_vals = [lax.ppermute(look_vals, "view", shift) for shift in shifts]
-    geo, look_acc = pl.pallas_call(
+    sums = jax.ShapeDtypeStruct((2, 256, 4 * LOW), F32)
+    geo, look = pl.pallas_call(
         scatter_kernel,
-        out_shape=(
-            jax.ShapeDtypeStruct((5, rows, LANES), F32),
-            jax.ShapeDtypeStruct((2, 4 * LOW, 256), F32),
-        ),
+        out_shape=(jax.ShapeDtypeStruct((5, rows, LANES), F32), sums),
         in_specs=[SMEM, VMEM, VMEM, VMEM],
         out_specs=(VMEM, VMEM),
-        scratch_shapes=[pltpu.VMEM((2, 9 * LOW, 256), F32)],
-        compiler_params=LIMIT,
-    )(ends, packed, geo_vals, look_vals)
-    look = pl.pallas_call(
-        finish_kernel,
-        out_shape=jax.ShapeDtypeStruct((rows, 4, LANES), F32),
-        in_specs=[VMEM] * (2 * views - 1),
-        out_specs=VMEM,
         scratch_shapes=[
-            pltpu.VMEM((2, 256, 4 * LOW), F32),
+            pltpu.VMEM((2, 9 * LOW, 256), F32),
+            pltpu.VMEM((2, owners + 1, 8, LANES), F32),
         ],
         compiler_params=LIMIT,
-    )(*other_ids, *other_vals, look_acc)
+    )(ends, packed, returned, look_vals)
+    for i in reversed(range(views - 1)):
+        last = i == 0
+        look = pl.pallas_call(
+            finish_kernel if last else add_view,
+            out_shape=jax.ShapeDtypeStruct((rows, 4, LANES), F32) if last else sums,
+            in_specs=[VMEM, VMEM, VMEM],
+            out_specs=VMEM,
+            scratch_shapes=[pltpu.VMEM((2, 256, 4 * LOW), F32)] if last else [],
+            compiler_params=LIMIT,
+        )(other_ids[i], other_vals[i], look)
     look = jnp.transpose(look, (1, 0, 2)).reshape(4, gauss)
     return (geo.reshape(1, 5, gauss), look)
 

time: 99.8 us -> 96.3 us (0.965)
  waiting for transfers between devices: 37.5 us -> 32.3 us
  starting transfers between devices: 30.4 us -> 31.9 us
    ppermute x3, waiting for transfers between devices: 5.63 us -> 2.07 us  [shards(): other_vals = [lax.ppermute(look_vals, 'view', shift) for shift in shifts]]
    ppermute x3, waiting for transfers between devices: 4.16 us -> 1.9 us  [shards(): other_ids = [lax.ppermute(packed, 'view', shift) for shift in shifts]]
    ppermute x3, starting transfers between devices: 3.36 us -> 4.9 us  [shards(): other_ids = [lax.ppermute(packed, 'view', shift) for shift in shifts]]
    pallas_call x2 -> x4, Pallas kernels: 6.66 us -> 6.09 us  [the longest x3 4.66 us: shards(): pl.pallas_call(finish_kernel if last else add_view, out_shape=jax.ShapeDt...]
  transfers between devices with their start and end apart: 9 -> 9, of which waited for: 8 -> 7; matrix products, arithmetic and copies ran while one was open for 1% -> 1% of each run, Pallas kernels for 4% -> 7%
where the time goes in v4:
time: 96.3 us; the launch traced here: 95.2 us
  waiting for transfers between devices  32.3 us (34%)
  starting transfers between devices  31.9 us (33%)
  Pallas kernels  29 us (30%)
  local copies, waits for them, and re-layouts  1.15 us (1%)
    all_to_all x3, waiting for transfers between devices, exchange(): got = lax.all_to_all(sent, axis, split_axis=0, concat_axis=0, tiled=True)  28.4 us
    all_to_all x3, starting transfers between devices, exchange(): got = lax.all_to_all(sent, axis, split_axis=0, concat_axis=0, tiled=True)  23.3 us
    pallas_call x1, Pallas kernels, shards(): pl.pallas_call(functools.partial(tile_kernel, (16, 8, 16)), out_shape=jax...  10.2 us
    ppermute x3, starting transfers between devices, shards(): other_ids = [lax.ppermute(packed, 'view', shift) for shift in shifts]  4.9 us
    pallas_call x1, Pallas kernels, shards(): pl.pallas_call(gather_kernel, out_shape=(jax.ShapeDtypeStruct((owners * 9...  4.82 us
    pallas_call x3, Pallas kernels, shards(): pl.pallas_call(finish_kernel if last else add_view, out_shape=jax.ShapeDt...  4.66 us
    pallas_call x1, Pallas kernels, shards(): pl.pallas_call(scatter_kernel, out_shape=(jax.ShapeDtypeStruct((5, rows,...  4.19 us
    ppermute x3, starting transfers between devices, shards(): other_vals = [lax.ppermute(look_vals, 'view', shift) for shift in shifts]  3.68 us
  transfers between devices with their start and end apart: 9, of which 7 were waited for; matrix products, arithmetic and copies ran while one was open for 1% of the time, Pallas kernels for 7%

profile of v4, /device:TPU:1, one launch (start us, length us, event | category | flops | bytes accessed | tf_op | source)
XLA Modules:
  0.0 95.2 jit_solution(10540487772151617673)
XLA Ops:
  0.6 0.0 copy-start
  0.6 3.4 %shard_map.77 = (s32[64,128]{1,0:T(8,128)}, s32[16,256]{1,0:T(8,128)}) custom-call(s32[1,16]{1,0:T(1,128)} %counts_ref.3, s32[1,4096]{1,0:T(1,128)} %bitcast.28, s32[1,4096]{1,0:T(1,128)} %local_hbm.1), custom_call_target="tpu_custom_call" | custom-call | tf_op jit(solution)/shard_map/pallas_call | solution.py:508
  4.0 13.2 %all-to-all-start = ((s32[64,1,128]{2,1,0:T(1,128)}), s32[64,1,128]{2,1,0:T(1,128)S(1)}, u32[]{:S(2)}, u32[]{:S(2)}) async-start(s32[64,1,128]{2,1,0:T(1,128)} %bitcast.32), calls=%async_computation | async-start | bytes 65536 | tf_op jit(solution)/shard_map/all_to_all | solution.py:497
  17.2 1.1 %copy.20 = f32[1,4,256,128]{3,2,1,0:T(8,128)S(1)} copy(f32[1,4,256,128]{3,1,2,0:T(4,128)} %bitcast.31) | data formatting | bytes 1048576
  18.3 0.0 copy-done
  18.3 0.4 shard_map.78.table_ref
  18.7 0.0 copy-start.4
  18.7 0.0 copy-start.1
  18.7 0.0 copy-start.2
  18.7 0.0 copy-start.3
  18.7 7.8 %all-to-all-done = s32[64,1,128]{2,1,0:T(1,128)S(1)} async-done(((s32[64,1,128]{2,1,0:T(1,128)}), s32[64,1,128]{2,1,0:T(1,128)S(1)}, u32[]{:S(2)}, u32[]{:S(2)}) %all-to-all-start) | async-done | bytes 32800 | tf_op jit(solution)/shard_map/all_to_all | solution.py:497
  26.5 4.8 %shard_map.79 = (f32[576,128]{1,0:T(8,128)}, s32[72,128]{1,0:T(8,128)S(1)}) custom-call(s32[64,128]{1,0:T(8,128)S(1)} %bitcast.27, bf16[2,576,512]{2,1,0:T(8,128)(2,1)S(1)} %shard_map.78.table_ref), custom_call_target="tpu_custom_call" | custom-call | tf_op jit(solution)/shard_map/pallas_call | solution.py:531
  31.3 5.3 %all-to-all-start.1 = ((f32[64,1,1152]{2,1,0:T(1,128)}), f32[64,1,1152]{2,1,0:T(1,128)S(1)}, u32[]{:S(2)}, u32[]{:S(2)}) async-start(f32[64,1,1152]{2,1,0:T(1,128)} %bitcast.6), calls=%async_computation.1 | async-start | bytes 589824 | tf_op jit(solution)/shard_map/all_to_all | solution.py:497
  36.6 1.3 %collective-permute-start = (s32[72,128]{1,0:T(8,128)S(1)}, s32[72,128]{1,0:T(8,128)S(1)}, u32[]{:S(2)}, u32[]{:S(2)}) collective-permute-start(s32[72,128]{1,0:T(8,128)S(1)} %get-tuple-element.13.ids_ref), channel_id=1, source_target_pairs={{0,1},{1,2},{2,3},{3,0},{4,5},{5,6},{6,7},{7,4},{8,9},{9,10},{10,1... | collective-permute-start | bytes 110600 | tf_op jit(solution)/shard_map/ppermute | solution.py:548
  37.9 2.5 %collective-permute-start.1 = (s32[72,128]{1,0:T(8,128)S(1)}, s32[72,128]{1,0:T(8,128)S(1)}, u32[]{:S(2)}, u32[]{:S(2)}) collective-permute-start(s32[72,128]{1,0:T(8,128)S(1)} %get-tuple-element.13.ids_ref), channel_id=1, source_target_pairs={{0,2},{1,3},{2,0},{3,1},{4,6},{5,7},{6,4},{7,5},{8,10},{9,11},{10,... | collective-permute-start | bytes 110600 | tf_op jit(solution)/shard_map/ppermute | solution.py:548
  40.4 1.2 %collective-permute-start.2 = (s32[72,128]{1,0:T(8,128)S(1)}, s32[72,128]{1,0:T(8,128)S(1)}, u32[]{:S(2)}, u32[]{:S(2)}) collective-permute-start(s32[72,128]{1,0:T(8,128)S(1)} %get-tuple-element.13.ids_ref), channel_id=1, source_target_pairs={{0,3},{1,0},{2,1},{3,2},{4,7},{5,4},{6,5},{7,6},{8,11},{9,8},{10,9... | collective-permute-start | bytes 110600 | tf_op jit(solution)/shard_map/ppermute | solution.py:548
  41.5 0.0 copy-done.4
  41.6 0.0 collective-permute-done.ids_ref
  41.6 0.9 collective-permute-done.1.ids_ref
  42.5 0.9 collective-permute-done.2.ids_ref
  43.5 6.9 %all-to-all-done.1 = f32[64,1,1152]{2,1,0:T(1,128)S(1)} async-done(((f32[64,1,1152]{2,1,0:T(1,128)}), f32[64,1,1152]{2,1,0:T(1,128)S(1)}, u32[]{:S(2)}, u32[]{:S(2)}) %all-to-all-start.1) | async-done | bytes 294944 | tf_op jit(solution)/shard_map/all_to_all | solution.py:497
  50.4 0.0 copy-done.1
  50.4 0.0 copy-done.2
  50.4 0.0 copy-done.3
  50.4 10.2 %shard_map.80 = f32[576,128]{1,0:T(8,128)} custom-call(s32[1,16]{1,0:T(1,128)S(1)} %copy-done.3, s32[1,4096]{1,0:T(1,128)S(1)} %bitcast.29, s32[16,256]{1,0:T(8,128)S(1)} %copy-done.2, f32[16,3,256]{2,1,0:T(4,128)S(1)} %bitcast.26, f32[576,128]{1,0:T(8,128)S(1)} %bitcast.24), custom_call_target="tpu_custom_call" | custom-call | tf_op jit(solution)/shard_map/pallas_call | solution.py:550
  60.5 4.9 %all-to-all-start.2 = ((f32[64,1,1152]{2,1,0:T(1,128)}), f32[64,1,1152]{2,1,0:T(1,128)S(1)}, u32[]{:S(2)}, u32[]{:S(2)}) async-start(f32[64,1,1152]{2,1,0:T(1,128)} %bitcast.8), calls=%async_computation.2 | async-start | bytes 589824 | tf_op jit(solution)/shard_map/all_to_all | solution.py:497
  65.4 13.7 %all-to-all-done.2 = f32[64,1,1152]{2,1,0:T(1,128)S(1)} async-done(((f32[64,1,1152]{2,1,0:T(1,128)}), f32[64,1,1152]{2,1,0:T(1,128)S(1)}, u32[]{:S(2)}, u32[]{:S(2)}) %all-to-all-start.2) | async-done | bytes 294944 | tf_op jit(solution)/shard_map/all_to_all | solution.py:497
  79.1 1.4 %shard_map.81.look_vals_ref = f32[65,4,128]{2,1,0:T(4,128)S(1)} custom-call(s32[7,128]{1,0:T(8,128)S(1)} %slice.3.ends_ref, f32[576,128]{1,0:T(8,128)S(1)} %bitcast.21), custom_call_target="tpu_custom_call" | custom-call | tf_op jit(solution)/shard_map/pallas_call | solution.py:567
  80.6 2.5 %collective-permute-start.5 = (f32[65,4,128]{2,1,0:T(4,128)S(1)}, f32[65,4,128]{2,1,0:T(4,128)S(1)}, u32[]{:S(2)}, u32[]{:S(2)}) collective-permute-start(f32[65,4,128]{2,1,0:T(4,128)S(1)} %shard_map.81.look_vals_ref), channel_id=1, source_target_pairs={{0,3},{1,0},{2,1},{3,2},{4,7},{5,4},{6,5},{7,6},{8,11},{9,8},{10,9... | collective-permute-start | bytes 399368 | tf_op jit(solution)/shard_map/ppermute | solution.py:575
  83.1 0.5 collective-permute-start.4
  83.6 0.6 collective-permute-start.3
  84.2 4.2 %shard_map.82 = (f32[5,256,128]{2,1,0:T(8,128)}, f32[2,256,256]{2,1,0:T(8,128)S(1)}) custom-call(s32[7,128]{1,0:T(8,128)S(1)} %slice.3.ends_ref, s32[72,128]{1,0:T(8,128)S(1)} %get-tuple-element.13.ids_ref, f32[576,128]{1,0:T(8,128)S(1)} %bitcast.22, f32[65,4,128]{2,1,0:T(4,128)S(1)} %shard_map.81.look_vals_ref), custom_call_target="tpu_custom_call" | custom-call | tf_op jit(solution)/shard_map/pallas_call | solution.py:577
  88.4 0.2 collective-permute-done.5.vals_ref
  88.6 1.3 %shard_map.83.start_ref = f32[2,256,256]{2,1,0:T(8,128)S(1)} custom-call(s32[72,128]{1,0:T(8,128)S(1)} %collective-permute-done.2.ids_ref, f32[65,4,128]{2,1,0:T(4,128)S(1)} %collective-permute-done.5.vals_ref, f32[2,256,256]{2,1,0:T(8,128)S(1)} %get-tuple-element.21.start_ref), custom_call_target="tpu_custom_call" | custom-call | tf_op jit(solution)/shard_map/pallas_call | solution.py:590
  90.0 0.0 collective-permute-done.4.vals_ref
  90.0 1.1 %shard_map.84.start_ref = f32[2,256,256]{2,1,0:T(8,128)S(1)} custom-call(s32[72,128]{1,0:T(8,128)S(1)} %collective-permute-done.1.ids_ref, f32[65,4,128]{2,1,0:T(4,128)S(1)} %collective-permute-done.4.vals_ref, f32[2,256,256]{2,1,0:T(8,128)S(1)} %shard_map.83.start_ref), custom_call_target="tpu_custom_call" | custom-call | tf_op jit(solution)/shard_map/pallas_call | solution.py:590
  91.1 1.9 %collective-permute-done.3.vals_ref = f32[65,4,128]{2,1,0:T(4,128)S(1)} collective-permute-done((f32[65,4,128]{2,1,0:T(4,128)S(1)}, f32[65,4,128]{2,1,0:T(4,128)S(1)}, u32[]{:S(2)}, u32[]{:S(2)}) %collective-permute-start.3) | collective-permute-done | bytes 133152 | tf_op jit(solution)/shard_map/ppermute | solution.py:575
  92.9 2.3 %shard_map.85 = f32[256,4,128]{2,1,0:T(4,128)} custom-call(s32[72,128]{1,0:T(8,128)S(1)} %collective-permute-done.ids_ref, f32[65,4,128]{2,1,0:T(4,128)S(1)} %collective-permute-done.3.vals_ref, f32[2,256,256]{2,1,0:T(8,128)S(1)} %shard_map.84.start_ref), custom_call_target="tpu_custom_call" | custom-call | tf_op jit(solution)/shard_map/pallas_call | solution.py:590
  (2 shorter events, 0.0 us)
Async XLA Ops:
  0.6 17.6 %copy-start = (f32[1,5,32768]{2,0,1:T(1,128)S(1)}, f32[1,5,32768]{2,0,1:T(1,128)}, u32[]{:S(2)}) copy-start(f32[1,5,32768]{2,0,1:T(1,128)} %param.6) | copy-start | bytes 1966084
  4.0 22.5 %all-to-all-start = ((s32[64,1,128]{2,1,0:T(1,128)}), s32[64,1,128]{2,1,0:T(1,128)S(1)}, u32[]{:S(2)}, u32[]{:S(2)}) async-start(s32[64,1,128]{2,1,0:T(1,128)} %bitcast.32), calls=%async_computation | async-start | bytes 65536 | tf_op jit(solution)/shard_map/all_to_all | solution.py:497
  18.7 22.9 %copy-start.4 = (f32[1,16,3,256]{3,1,2,0:T(8,128)S(1)}, f32[1,16,3,256]{3,1,2,0:T(8,128)}, u32[]{:S(2)}) copy-start(f32[1,16,3,256]{3,1,2,0:T(8,128)} %param.11) | copy-start | bytes 147460
  18.7 31.7 %copy-start.1 = (s32[1,4096,1]{1,2,0:T(1,128)S(1)}, s32[1,4096,1]{1,2,0:T(1,128)}, u32[]{:S(2)}) copy-start(s32[1,4096,1]{1,2,0:T(1,128)} %param.8) | copy-start | bytes 49156
  18.7 31.7 %copy-start.2 = (s32[16,256]{1,0:T(8,128)S(1)}, s32[16,256]{1,0:T(8,128)}, u32[]{:S(2)}) copy-start(s32[16,256]{1,0:T(8,128)} %get-tuple-element.14.rank_ref) | copy-start | bytes 49156
  18.7 31.7 %copy-start.3 = (s32[1,16]{1,0:T(1,128)S(1)}, s32[1,16]{1,0:T(1,128)}, u32[]{:S(2)}) copy-start(s32[1,16]{1,0:T(1,128)} %counts_ref.3) | copy-start | bytes 196
  31.3 19.1 %all-to-all-start.1 = ((f32[64,1,1152]{2,1,0:T(1,128)}), f32[64,1,1152]{2,1,0:T(1,128)S(1)}, u32[]{:S(2)}, u32[]{:S(2)}) async-start(f32[64,1,1152]{2,1,0:T(1,128)} %bitcast.6), calls=%async_computation.1 | async-start | bytes 589824 | tf_op jit(solution)/shard_map/all_to_all | solution.py:497
  36.6 4.9 %collective-permute-start = (s32[72,128]{1,0:T(8,128)S(1)}, s32[72,128]{1,0:T(8,128)S(1)}, u32[]{:S(2)}, u32[]{:S(2)}) collective-permute-start(s32[72,128]{1,0:T(8,128)S(1)} %get-tuple-element.13.ids_ref), channel_id=1, source_target_pairs={{0,1},{1,2},{2,3},{3,0},{4,5},{5,6},{6,7},{7,4},{8,9},{9,10},{10,1... | collective-permute-start | bytes 110600 | tf_op jit(solution)/shard_map/ppermute | solution.py:548
  37.9 4.6 %collective-permute-start.1 = (s32[72,128]{1,0:T(8,128)S(1)}, s32[72,128]{1,0:T(8,128)S(1)}, u32[]{:S(2)}, u32[]{:S(2)}) collective-permute-start(s32[72,128]{1,0:T(8,128)S(1)} %get-tuple-element.13.ids_ref), channel_id=1, source_target_pairs={{0,2},{1,3},{2,0},{3,1},{4,6},{5,7},{6,4},{7,5},{8,10},{9,11},{10,... | collective-permute-start | bytes 110600 | tf_op jit(solution)/shard_map/ppermute | solution.py:548
  40.4 3.1 %collective-permute-start.2 = (s32[72,128]{1,0:T(8,128)S(1)}, s32[72,128]{1,0:T(8,128)S(1)}, u32[]{:S(2)}, u32[]{:S(2)}) collective-permute-start(s32[72,128]{1,0:T(8,128)S(1)} %get-tuple-element.13.ids_ref), channel_id=1, source_target_pairs={{0,3},{1,0},{2,1},{3,2},{4,7},{5,4},{6,5},{7,6},{8,11},{9,8},{10,9... | collective-permute-start | bytes 110600 | tf_op jit(solution)/shard_map/ppermute | solution.py:548
  60.5 18.6 %all-to-all-start.2 = ((f32[64,1,1152]{2,1,0:T(1,128)}), f32[64,1,1152]{2,1,0:T(1,128)S(1)}, u32[]{:S(2)}, u32[]{:S(2)}) async-start(f32[64,1,1152]{2,1,0:T(1,128)} %bitcast.8), calls=%async_computation.2 | async-start | bytes 589824 | tf_op jit(solution)/shard_map/all_to_all | solution.py:497
  80.6 8.1 %collective-permute-start.5 = (f32[65,4,128]{2,1,0:T(4,128)S(1)}, f32[65,4,128]{2,1,0:T(4,128)S(1)}, u32[]{:S(2)}, u32[]{:S(2)}) collective-permute-start(f32[65,4,128]{2,1,0:T(4,128)S(1)} %shard_map.81.look_vals_ref), channel_id=1, source_target_pairs={{0,3},{1,0},{2,1},{3,2},{4,7},{5,4},{6,5},{7,6},{8,11},{9,8},{10,9... | collective-permute-start | bytes 399368 | tf_op jit(solution)/shard_map/ppermute | solution.py:575
  83.1 6.8 %collective-permute-start.4 = (f32[65,4,128]{2,1,0:T(4,128)S(1)}, f32[65,4,128]{2,1,0:T(4,128)S(1)}, u32[]{:S(2)}, u32[]{:S(2)}) collective-permute-start(f32[65,4,128]{2,1,0:T(4,128)S(1)} %shard_map.81.look_vals_ref), channel_id=1, source_target_pairs={{0,2},{1,3},{2,0},{3,1},{4,6},{5,7},{6,4},{7,5},{8,10},{9,11},{10,... | collective-permute-start | bytes 399368 | tf_op jit(solution)/shard_map/ppermute | solution.py:575
  83.6 9.3 %collective-permute-start.3 = (f32[65,4,128]{2,1,0:T(4,128)S(1)}, f32[65,4,128]{2,1,0:T(4,128)S(1)}, u32[]{:S(2)}, u32[]{:S(2)}) collective-permute-start(f32[65,4,128]{2,1,0:T(4,128)S(1)} %shard_map.81.look_vals_ref), channel_id=1, source_target_pairs={{0,1},{1,2},{2,3},{3,0},{4,5},{5,6},{6,7},{7,4},{8,9},{9,10},{10,1... | collective-permute-start | bytes 399368 | tf_op jit(solution)/shard_map/ppermute | solution.py:575

commit v5 on v4

--- a/solution.py
+++ b/solution.py
@@ -45,20 +45,26 @@
     return lax.broadcasted_iota(jnp.int32, (rows, columns), 1)
 
 
-def named_mask(owner_row, count, owners):
-    live = lane_iota(1, K) < count
-    shown = jnp.where(live, owner_row, -1)
-    return row_iota(owners, K) == shown
-
-
-def plan_kernel(counts_ref, owner_hbm, local_hbm, request_ref, rank_ref, owner_ref, local_ref, sem):
+def plan_kernel(
+    counts_hbm,
+    owner_hbm,
+    local_hbm,
+    request_ref,
+    pair_ref,
+    place_ref,
+    counts_ref,
+    owner_ref,
+    local_ref,
+    sem,
+):
     copies = [
-        pltpu.make_async_copy(owner_hbm, owner_ref, sem.at[0]),
-        pltpu.make_async_copy(local_hbm, local_ref, sem.at[1]),
+        pltpu.make_async_copy(counts_hbm, counts_ref, sem.at[0]),
+        pltpu.make_async_copy(owner_hbm, owner_ref, sem.at[1]),
+        pltpu.make_async_copy(local_hbm, local_ref, sem.at[2]),
     ]
     for copy in copies:
         copy.start()
-    tiles = rank_ref.shape[0]
+    tiles = pair_ref.shape[0]
     owners = request_ref.shape[0]
     before = (row_iota(K, K) < lane_iota(K, K)).astype(BF16)
     for copy in copies:
@@ -82,7 +88,8 @@
         both = both.astype(jnp.int32)
         rank = jnp.where((ids[t] & LOW) != 0, LANES - 1 - (both >> 8), both & 255)
         carry = carry + jnp.sum(jnp.where(named, units[t], 0.0), axis=1, keepdims=True)
-        rank_ref[t : t + 1, :] = rank
+        pair_ref[t : t + 1, :] = row >> 1
+        place_ref[t : t + 1, :] = rank + (row & 1) * LANES
         asked = ids[t] + 1
         hits = hits16(LANES, rank)
         high = keep16(hits, (asked >> 7).astype(F32).astype(BF16))
@@ -104,7 +111,6 @@
 
 
 WIDE = 8
-NARROW = 4
 
 
 def ids_row(ref, at):
@@ -134,22 +140,21 @@
 
 def each_chunk(totals, owners, chunk):
     most = jnp.maximum(totals[0], totals[1])
-    large = most // (WIDE * LANES)
-    small = (most - large * (WIDE * LANES) + NARROW * LANES - 1) // (NARROW * LANES)
+    steps = (most + 2 * LANES - 1) // (2 * LANES)
+    large, left = (steps + 1) // 4, steps % 4
 
     def wide(j, _):
         chunk(WIDE * j, 0, WIDE)
         chunk(owners - WIDE * (j + 1), 1, WIDE)
         return 0
 
-    def narrow(j, _):
-        done = WIDE * large + NARROW * j
-        chunk(done, 0, NARROW)
-        chunk(owners - done - NARROW, 1, NARROW)
-        return 0
-
     lax.fori_loop(0, large, wide, 0)
-    lax.fori_loop(0, small, narrow, 0)
+    for units in (1, 2):
+
+        @pl.when(left == units)
+        def _():
+            chunk(WIDE * large, 0, 2 * units)
+            chunk(owners - WIDE * large - 2 * units, 1, 2 * units)
 
 
 def compact(owners, ends_ref, base, row_at, store):
@@ -260,9 +265,8 @@
 
 def tile_kernel(
     unrolls,
-    counts_ref,
-    owner_ref,
-    rank_ref,
+    pair_ref,
+    place_ref,
     cot_ref,
     fetched_ref,
     out_ref,
@@ -273,7 +277,7 @@
     coef_ref,
     sums_ref,
 ):
-    tiles = rank_ref.shape[0]
+    tiles = pair_ref.shape[0]
     owners = fetched_ref.shape[0] // 9
     unrolls = [math.gcd(tiles, n) for n in unrolls]
     half = owners // 2
@@ -291,20 +295,15 @@
     dots_ref[0:K] = before
     dots_ref[K : 2 * K] = after
 
-    def owner_row(t):
-        row = owner_ref[:, pl.ds(pl.multiple_of(t * K, K), K)]
-        return jnp.where(lane_iota(1, K) < counts_ref[0, t], row, -1)
-
     def hot_place(t):
-        row = owner_row(t)
-        return hot16(2 * LANES, rank_ref[pl.ds(t, 1), :] + (row & 1) * LANES)
+        return hot16(2 * LANES, place_ref[pl.ds(t, 1), :])
 
     def fetch(g, _):
         several = [unrolls[0] * g + i for i in range(unrolls[0])]
         hots = [hot_place(t) for t in several]
         spreads = [dot_nn(table_ref[...], jnp.concatenate([hot, hot], 0)) for hot in hots]
         for t, spread in zip(several, spreads):
-            named = row_iota(half, K) == (owner_row(t) >> 1)
+            named = row_iota(half, K) == pair_ref[pl.ds(t, 1), :]
             for c in range(9):
                 kept = jnp.where(named, spread[c * half : (c + 1) * half], 0.0)
                 entry_ref[c, pl.ds(t, 1), :] = jnp.sum(kept, axis=0, keepdims=True)
@@ -314,8 +313,6 @@
     cx, cy = entry_ref[0] - 0.5, entry_ref[1] - 0.5
     a, b, c2 = entry_ref[2], entry_ref[3], entry_ref[4]
     opacity = 1.0 / (1.0 + jnp.exp(-entry_ref[8]))
-    spots = lane_iota(1, K)
-    left = jnp.concatenate([counts_ref[0, t] - spots for t in range(tiles)], 0)
     ax, ay = a * cx + b * cy, b * cx + c2 * cy
     base = jnp.log(0.99 * opacity) * LOG2E - (0.5 * LOG2E) * (ax * cx + ay * cy)
     coefs = [
@@ -324,7 +321,7 @@
         (-0.5 * LOG2E) * c2,
         LOG2E * ax,
         LOG2E * ay,
-        jnp.where(left > 0, base, -400.0),
+        jnp.where(pair_ref[...] >= 0, base, -400.0),
     ]
     for i, coef in enumerate(coefs):
         coef_ref[:, i, :] = coef
@@ -387,7 +384,7 @@
         for i in range(unrolls[2]):
             t = unrolls[2] * g + i
             hot = hot_place(t)
-            hits = hits16(half, owner_row(t) >> 1)
+            hits = hits16(half, pair_ref[pl.ds(t, 1), :])
             placed = []
             for c in range(9):
                 high, low = split2(entry_ref[c, pl.ds(t, 1), :])
@@ -505,18 +502,20 @@
     gauss = geometry.shape[2]
     rows = gauss // LANES
     target = list_owner.reshape(1, tiles * K)
-    requests, ranks = pl.pallas_call(
+    requests, pairs, places = pl.pallas_call(
         plan_kernel,
         out_shape=(
             jax.ShapeDtypeStruct((owners, LANES), jnp.int32),
             jax.ShapeDtypeStruct((tiles, K), jnp.int32),
+            jax.ShapeDtypeStruct((tiles, K), jnp.int32),
         ),
-        in_specs=[SMEM, HBM, HBM],
-        out_specs=(VMEM, VMEM),
+        in_specs=[HBM, HBM, HBM],
+        out_specs=(VMEM, VMEM, VMEM),
         scratch_shapes=[
+            pltpu.SMEM((1, tiles), jnp.int32),
             pltpu.VMEM((1, tiles * K), jnp.int32),
             pltpu.VMEM((1, tiles * K), jnp.int32),
-            pltpu.SemaphoreType.DMA((2,)),
+            pltpu.SemaphoreType.DMA((3,)),
         ],
         compiler_params=pltpu.CompilerParams(vmem_limit_bytes=60 * 1024 * 1024),
     )(counts, target, list_local)
@@ -550,7 +549,7 @@
     outgoing = pl.pallas_call(
         functools.partial(tile_kernel, (16, 8, 16)),
         out_shape=jax.ShapeDtypeStruct((owners * 9, LANES), F32),
-        in_specs=[SMEM, VMEM, VMEM, VMEM, VMEM],
+        in_specs=[VMEM, VMEM, VMEM, VMEM],
         out_specs=VMEM,
         scratch_shapes=[
             pltpu.VMEM((9 * owners // 2, 4 * LANES), BF16),
@@ -561,7 +560,7 @@
             pltpu.VMEM((tiles, 16, K), F32),
         ],
         compiler_params=LIMIT,
-    )(counts, target, ranks, cotangent[0], fetched)
+    )(pairs, places, cotangent[0], fetched)
     returned = exchange(outgoing, owners)
     ends = packed[owners + 1 :]
     look_vals = pl.pallas_call(

time: 96.3 us -> 94.6 us (0.982)
  Pallas kernels: 29 us -> 26.7 us
where the time goes in v5:
time: 94.6 us; the launch traced here: 94.3 us
  waiting for transfers between devices  32.9 us (35%)
  starting transfers between devices  32.8 us (35%)
  Pallas kernels  26.7 us (28%)
  local copies, waits for them, and re-layouts  1.14 us (1%)
    all_to_all x3, waiting for transfers between devices, exchange(): got = lax.all_to_all(sent, axis, split_axis=0, concat_axis=0, tiled=True)  28.6 us
    all_to_all x3, starting transfers between devices, exchange(): got = lax.all_to_all(sent, axis, split_axis=0, concat_axis=0, tiled=True)  24.2 us
    pallas_call x1, Pallas kernels, shards(): pl.pallas_call(functools.partial(tile_kernel, (16, 8, 16)), out_shape=jax...  9.56 us
    ppermute x3, starting transfers between devices, shards(): other_ids = [lax.ppermute(packed, 'view', shift) for shift in shifts]  4.9 us
    pallas_call x1, Pallas kernels, shards(): pl.pallas_call(gather_kernel, out_shape=(jax.ShapeDtypeStruct((owners * 9...  4.66 us
    pallas_call x3, Pallas kernels, shards(): pl.pallas_call(finish_kernel if last else add_view, out_shape=jax.ShapeDt...  4.05 us
    pallas_call x1, Pallas kernels, shards(): pl.pallas_call(scatter_kernel, out_shape=(jax.ShapeDtypeStruct((5, rows,...  3.97 us
    ppermute x3, starting transfers between devices, shards(): other_vals = [lax.ppermute(look_vals, 'view', shift) for shift in shifts]  3.69 us
  transfers between devices with their start and end apart: 9, of which 7 were waited for; matrix products, arithmetic and copies ran while one was open for 1% of the time, Pallas kernels for 7%

profile of v5, /device:TPU:1, one launch (start us, length us, event | category | flops | bytes accessed | tf_op | source)
XLA Modules:
  0.0 94.3 jit_solution(16150747522206444500)
XLA Ops:
  0.6 0.0 copy-start
  0.6 2.7 %shard_map.77 = (s32[64,128]{1,0:T(8,128)}, s32[16,256]{1,0:T(8,128)}, s32[16,256]{1,0:T(8,128)}) custom-call(s32[1,16]{1,0:T(1,128)} %counts_hbm.1, s32[1,4096]{1,0:T(1,128)} %bitcast.31, s32[1,4096]{1,0:T(1,128)} %local_hbm.1), custom_call_target="tpu_custom_call" | custom-call | tf_op jit(solution)/shard_map/pallas_call | solution.py:505
  3.3 13.2 %all-to-all-start = ((s32[64,1,128]{2,1,0:T(1,128)}), s32[64,1,128]{2,1,0:T(1,128)S(1)}, u32[]{:S(2)}, u32[]{:S(2)}) async-start(s32[64,1,128]{2,1,0:T(1,128)} %bitcast.30), calls=%async_computation | async-start | bytes 65536 | tf_op jit(solution)/shard_map/all_to_all | solution.py:494
  16.5 1.1 %copy.20 = f32[1,4,256,128]{3,2,1,0:T(8,128)S(1)} copy(f32[1,4,256,128]{3,1,2,0:T(4,128)} %bitcast.29) | data formatting | bytes 1048576
  17.6 0.0 copy-done
  17.6 0.4 shard_map.78.table_ref
  17.9 0.0 copy-start.3
  18.0 0.0 copy-start.1
  18.0 0.0 copy-start.2
  18.0 7.8 %all-to-all-done = s32[64,1,128]{2,1,0:T(1,128)S(1)} async-done(((s32[64,1,128]{2,1,0:T(1,128)}), s32[64,1,128]{2,1,0:T(1,128)S(1)}, u32[]{:S(2)}, u32[]{:S(2)}) %all-to-all-start) | async-done | bytes 32800 | tf_op jit(solution)/shard_map/all_to_all | solution.py:494
  25.8 4.7 %shard_map.79 = (f32[576,128]{1,0:T(8,128)}, s32[72,128]{1,0:T(8,128)S(1)}) custom-call(s32[64,128]{1,0:T(8,128)S(1)} %bitcast.27, bf16[2,576,512]{2,1,0:T(8,128)(2,1)S(1)} %shard_map.78.table_ref), custom_call_target="tpu_custom_call" | custom-call | tf_op jit(solution)/shard_map/pallas_call | solution.py:530
  30.4 6.2 %all-to-all-start.1 = ((f32[64,1,1152]{2,1,0:T(1,128)}), f32[64,1,1152]{2,1,0:T(1,128)S(1)}, u32[]{:S(2)}, u32[]{:S(2)}) async-start(f32[64,1,1152]{2,1,0:T(1,128)} %bitcast.6), calls=%async_computation.1 | async-start | bytes 589824 | tf_op jit(solution)/shard_map/all_to_all | solution.py:494
  36.6 1.0 %collective-permute-start = (s32[72,128]{1,0:T(8,128)S(1)}, s32[72,128]{1,0:T(8,128)S(1)}, u32[]{:S(2)}, u32[]{:S(2)}) collective-permute-start(s32[72,128]{1,0:T(8,128)S(1)} %get-tuple-element.14.ids_ref), channel_id=1, source_target_pairs={{0,1},{1,2},{2,3},{3,0},{4,5},{5,6},{6,7},{7,4},{8,9},{9,10},{10,1... | collective-permute-start | bytes 110600 | tf_op jit(solution)/shard_map/ppermute | solution.py:547
  37.6 2.4 %collective-permute-start.1 = (s32[72,128]{1,0:T(8,128)S(1)}, s32[72,128]{1,0:T(8,128)S(1)}, u32[]{:S(2)}, u32[]{:S(2)}) collective-permute-start(s32[72,128]{1,0:T(8,128)S(1)} %get-tuple-element.14.ids_ref), channel_id=1, source_target_pairs={{0,2},{1,3},{2,0},{3,1},{4,6},{5,7},{6,4},{7,5},{8,10},{9,11},{10,... | collective-permute-start | bytes 110600 | tf_op jit(solution)/shard_map/ppermute | solution.py:547
  40.0 1.5 %collective-permute-start.2 = (s32[72,128]{1,0:T(8,128)S(1)}, s32[72,128]{1,0:T(8,128)S(1)}, u32[]{:S(2)}, u32[]{:S(2)}) collective-permute-start(s32[72,128]{1,0:T(8,128)S(1)} %get-tuple-element.14.ids_ref), channel_id=1, source_target_pairs={{0,3},{1,0},{2,1},{3,2},{4,7},{5,4},{6,5},{7,6},{8,11},{9,8},{10,9... | collective-permute-start | bytes 110600 | tf_op jit(solution)/shard_map/ppermute | solution.py:547
  41.5 0.0 copy-done.3
  41.5 0.0 collective-permute-done.ids_ref
  41.6 0.7 collective-permute-done.1.ids_ref
  42.3 1.0 %collective-permute-done.2.ids_ref = s32[72,128]{1,0:T(8,128)S(1)} collective-permute-done((s32[72,128]{1,0:T(8,128)S(1)}, s32[72,128]{1,0:T(8,128)S(1)}, u32[]{:S(2)}, u32[]{:S(2)}) %collective-permute-start.2) | collective-permute-done | bytes 36896 | tf_op jit(solution)/shard_map/ppermute | solution.py:547
  43.3 7.1 %all-to-all-done.1 = f32[64,1,1152]{2,1,0:T(1,128)S(1)} async-done(((f32[64,1,1152]{2,1,0:T(1,128)}), f32[64,1,1152]{2,1,0:T(1,128)S(1)}, u32[]{:S(2)}, u32[]{:S(2)}) %all-to-all-start.1) | async-done | bytes 294944 | tf_op jit(solution)/shard_map/all_to_all | solution.py:494
  50.4 0.0 copy-done.1
  50.4 0.0 copy-done.2
  50.4 9.6 %shard_map.80 = f32[576,128]{1,0:T(8,128)} custom-call(s32[16,256]{1,0:T(8,128)S(1)} %copy-done.1, s32[16,256]{1,0:T(8,128)S(1)} %copy-done.2, f32[16,3,256]{2,1,0:T(4,128)S(1)} %bitcast.26, f32[576,128]{1,0:T(8,128)S(1)} %bitcast.24), custom_call_target="tpu_custom_call" | custom-call | tf_op jit(solution)/shard_map/pallas_call | solution.py:549
  60.0 4.9 %all-to-all-start.2 = ((f32[64,1,1152]{2,1,0:T(1,128)}), f32[64,1,1152]{2,1,0:T(1,128)S(1)}, u32[]{:S(2)}, u32[]{:S(2)}) async-start(f32[64,1,1152]{2,1,0:T(1,128)} %bitcast.8), calls=%async_computation.2 | async-start | bytes 589824 | tf_op jit(solution)/shard_map/all_to_all | solution.py:494
  64.9 13.7 %all-to-all-done.2 = f32[64,1,1152]{2,1,0:T(1,128)S(1)} async-done(((f32[64,1,1152]{2,1,0:T(1,128)}), f32[64,1,1152]{2,1,0:T(1,128)S(1)}, u32[]{:S(2)}, u32[]{:S(2)}) %all-to-all-start.2) | async-done | bytes 294944 | tf_op jit(solution)/shard_map/all_to_all | solution.py:494
  78.6 1.4 %shard_map.81.look_vals_ref = f32[65,4,128]{2,1,0:T(4,128)S(1)} custom-call(s32[7,128]{1,0:T(8,128)S(1)} %slice.3.ends_ref, f32[576,128]{1,0:T(8,128)S(1)} %bitcast.21), custom_call_target="tpu_custom_call" | custom-call | tf_op jit(solution)/shard_map/pallas_call | solution.py:566
  80.0 2.4 %collective-permute-start.5 = (f32[65,4,128]{2,1,0:T(4,128)S(1)}, f32[65,4,128]{2,1,0:T(4,128)S(1)}, u32[]{:S(2)}, u32[]{:S(2)}) collective-permute-start(f32[65,4,128]{2,1,0:T(4,128)S(1)} %shard_map.81.look_vals_ref), channel_id=1, source_target_pairs={{0,3},{1,0},{2,1},{3,2},{4,7},{5,4},{6,5},{7,6},{8,11},{9,8},{10,9... | collective-permute-start | bytes 399368 | tf_op jit(solution)/shard_map/ppermute | solution.py:574
  82.5 0.5 collective-permute-start.4
  82.9 0.8 collective-permute-start.3
  83.7 4.0 %shard_map.82 = (f32[5,256,128]{2,1,0:T(8,128)}, f32[2,256,256]{2,1,0:T(8,128)S(1)}) custom-call(s32[7,128]{1,0:T(8,128)S(1)} %slice.3.ends_ref, s32[72,128]{1,0:T(8,128)S(1)} %get-tuple-element.14.ids_ref, f32[576,128]{1,0:T(8,128)S(1)} %bitcast.22, f32[65,4,128]{2,1,0:T(4,128)S(1)} %shard_map.81.look_vals_ref), custom_call_target="tpu_custom_call" | custom-call | tf_op jit(solution)/shard_map/pallas_call | solution.py:576
  87.7 0.3 collective-permute-done.5.vals_ref
  88.0 1.1 %shard_map.83.start_ref = f32[2,256,256]{2,1,0:T(8,128)S(1)} custom-call(s32[72,128]{1,0:T(8,128)S(1)} %collective-permute-done.2.ids_ref, f32[65,4,128]{2,1,0:T(4,128)S(1)} %collective-permute-done.5.vals_ref, f32[2,256,256]{2,1,0:T(8,128)S(1)} %get-tuple-element.23.start_ref), custom_call_target="tpu_custom_call" | custom-call | tf_op jit(solution)/shard_map/pallas_call | solution.py:589
  89.1 0.0 collective-permute-done.4.vals_ref
  89.1 0.9 shard_map.84.start_ref
  90.0 2.3 %collective-permute-done.3.vals_ref = f32[65,4,128]{2,1,0:T(4,128)S(1)} collective-permute-done((f32[65,4,128]{2,1,0:T(4,128)S(1)}, f32[65,4,128]{2,1,0:T(4,128)S(1)}, u32[]{:S(2)}, u32[]{:S(2)}) %collective-permute-start.3) | collective-permute-done | bytes 133152 | tf_op jit(solution)/shard_map/ppermute | solution.py:574
  92.3 2.0 %shard_map.85 = f32[256,4,128]{2,1,0:T(4,128)} custom-call(s32[72,128]{1,0:T(8,128)S(1)} %collective-permute-done.ids_ref, f32[65,4,128]{2,1,0:T(4,128)S(1)} %collective-permute-done.3.vals_ref, f32[2,256,256]{2,1,0:T(8,128)S(1)} %shard_map.84.start_ref), custom_call_target="tpu_custom_call" | custom-call | tf_op jit(solution)/shard_map/pallas_call | solution.py:589
  (2 shorter events, 0.0 us)
Async XLA Ops:
  0.6 16.9 %copy-start = (f32[1,5,32768]{2,0,1:T(1,128)S(1)}, f32[1,5,32768]{2,0,1:T(1,128)}, u32[]{:S(2)}) copy-start(f32[1,5,32768]{2,0,1:T(1,128)} %param.6) | copy-start | bytes 1966084
  3.3 22.5 %all-to-all-start = ((s32[64,1,128]{2,1,0:T(1,128)}), s32[64,1,128]{2,1,0:T(1,128)S(1)}, u32[]{:S(2)}, u32[]{:S(2)}) async-start(s32[64,1,128]{2,1,0:T(1,128)} %bitcast.30), calls=%async_computation | async-start | bytes 65536 | tf_op jit(solution)/shard_map/all_to_all | solution.py:494
  17.9 23.6 %copy-start.3 = (f32[1,16,3,256]{3,1,2,0:T(8,128)S(1)}, f32[1,16,3,256]{3,1,2,0:T(8,128)}, u32[]{:S(2)}) copy-start(f32[1,16,3,256]{3,1,2,0:T(8,128)} %param.11) | copy-start | bytes 147460
  18.0 32.4 %copy-start.1 = (s32[16,256]{1,0:T(8,128)S(1)}, s32[16,256]{1,0:T(8,128)}, u32[]{:S(2)}) copy-start(s32[16,256]{1,0:T(8,128)} %get-tuple-element.15.pair_ref) | copy-start | bytes 49156
  18.0 32.4 %copy-start.2 = (s32[16,256]{1,0:T(8,128)S(1)}, s32[16,256]{1,0:T(8,128)}, u32[]{:S(2)}) copy-start(s32[16,256]{1,0:T(8,128)} %get-tuple-element.16.place_ref) | copy-start | bytes 49156
  30.4 20.0 %all-to-all-start.1 = ((f32[64,1,1152]{2,1,0:T(1,128)}), f32[64,1,1152]{2,1,0:T(1,128)S(1)}, u32[]{:S(2)}, u32[]{:S(2)}) async-start(f32[64,1,1152]{2,1,0:T(1,128)} %bitcast.6), calls=%async_computation.1 | async-start | bytes 589824 | tf_op jit(solution)/shard_map/all_to_all | solution.py:494
  36.6 4.9 %collective-permute-start = (s32[72,128]{1,0:T(8,128)S(1)}, s32[72,128]{1,0:T(8,128)S(1)}, u32[]{:S(2)}, u32[]{:S(2)}) collective-permute-start(s32[72,128]{1,0:T(8,128)S(1)} %get-tuple-element.14.ids_ref), channel_id=1, source_target_pairs={{0,1},{1,2},{2,3},{3,0},{4,5},{5,6},{6,7},{7,4},{8,9},{9,10},{10,1... | collective-permute-start | bytes 110600 | tf_op jit(solution)/shard_map/ppermute | solution.py:547
  37.6 4.7 %collective-permute-start.1 = (s32[72,128]{1,0:T(8,128)S(1)}, s32[72,128]{1,0:T(8,128)S(1)}, u32[]{:S(2)}, u32[]{:S(2)}) collective-permute-start(s32[72,128]{1,0:T(8,128)S(1)} %get-tuple-element.14.ids_ref), channel_id=1, source_target_pairs={{0,2},{1,3},{2,0},{3,1},{4,6},{5,7},{6,4},{7,5},{8,10},{9,11},{10,... | collective-permute-start | bytes 110600 | tf_op jit(solution)/shard_map/ppermute | solution.py:547
  40.0 3.3 %collective-permute-start.2 = (s32[72,128]{1,0:T(8,128)S(1)}, s32[72,128]{1,0:T(8,128)S(1)}, u32[]{:S(2)}, u32[]{:S(2)}) collective-permute-start(s32[72,128]{1,0:T(8,128)S(1)} %get-tuple-element.14.ids_ref), channel_id=1, source_target_pairs={{0,3},{1,0},{2,1},{3,2},{4,7},{5,4},{6,5},{7,6},{8,11},{9,8},{10,9... | collective-permute-start | bytes 110600 | tf_op jit(solution)/shard_map/ppermute | solution.py:547
  60.0 18.6 %all-to-all-start.2 = ((f32[64,1,1152]{2,1,0:T(1,128)}), f32[64,1,1152]{2,1,0:T(1,128)S(1)}, u32[]{:S(2)}, u32[]{:S(2)}) async-start(f32[64,1,1152]{2,1,0:T(1,128)} %bitcast.8), calls=%async_computation.2 | async-start | bytes 589824 | tf_op jit(solution)/shard_map/all_to_all | solution.py:494
  80.0 8.0 %collective-permute-start.5 = (f32[65,4,128]{2,1,0:T(4,128)S(1)}, f32[65,4,128]{2,1,0:T(4,128)S(1)}, u32[]{:S(2)}, u32[]{:S(2)}) collective-permute-start(f32[65,4,128]{2,1,0:T(4,128)S(1)} %shard_map.81.look_vals_ref), channel_id=1, source_target_pairs={{0,3},{1,0},{2,1},{3,2},{4,7},{5,4},{6,5},{7,6},{8,11},{9,8},{10,9... | collective-permute-start | bytes 399368 | tf_op jit(solution)/shard_map/ppermute | solution.py:574
  82.5 6.6 %collective-permute-start.4 = (f32[65,4,128]{2,1,0:T(4,128)S(1)}, f32[65,4,128]{2,1,0:T(4,128)S(1)}, u32[]{:S(2)}, u32[]{:S(2)}) collective-permute-start(f32[65,4,128]{2,1,0:T(4,128)S(1)} %shard_map.81.look_vals_ref), channel_id=1, source_target_pairs={{0,2},{1,3},{2,0},{3,1},{4,6},{5,7},{6,4},{7,5},{8,10},{9,11},{10,... | collective-permute-start | bytes 399368 | tf_op jit(solution)/shard_map/ppermute | solution.py:574
  82.9 9.3 %collective-permute-start.3 = (f32[65,4,128]{2,1,0:T(4,128)S(1)}, f32[65,4,128]{2,1,0:T(4,128)S(1)}, u32[]{:S(2)}, u32[]{:S(2)}) collective-permute-start(f32[65,4,128]{2,1,0:T(4,128)S(1)} %shard_map.81.look_vals_ref), channel_id=1, source_target_pairs={{0,1},{1,2},{2,3},{3,0},{4,5},{5,6},{6,7},{7,4},{8,9},{9,10},{10,1... | collective-permute-start | bytes 399368 | tf_op jit(solution)/shard_map/ppermute | solution.py:574

commit v6 on v5

--- a/solution.py
+++ b/solution.py
@@ -187,6 +187,13 @@
         store(bucket, offset >> 7, now)
 
 
+def to_scalars(ends, ends_ref):
+    amount = ends.shape[1]
+    for s in range(amount):
+        ends_ref[0, s] = ends[0, s]
+    return ends[0, amount // 2 - 1], ends[0, amount - 1]
+
+
 def gather_kernel(asked_ref, table_ref, out_ref, packed_ref, ends_ref, held_ref, found_ref):
     owners = asked_ref.shape[0]
     asked = asked_ref[...]
@@ -197,10 +204,8 @@
     sides = ((lane_iota(8, 2 * LANES) >> 7) == row_iota(8, 2 * LANES)).astype(F32).astype(BF16)
     ends = dot_nt(sides, dot_nn(upto, valid).astype(BF16)).astype(jnp.int32)
     held_ref[...] = jnp.zeros_like(held_ref)
-    for s in range(owners):
-        ends_ref[0, s] = ends[0, s]
-        ends_ref[0, owners + s] = ends[1, s]
-    totals = ends[0, owners - 1], ends[1, owners - 1]
+    ends = jnp.concatenate([ends[0:1], ends[1:2]], 1)
+    totals = to_scalars(ends, ends_ref)
     base = owners * LANES - totals[1]
 
     def row_at(g, j):
@@ -211,9 +216,7 @@
 
     compact(owners, ends_ref, base, row_at, store)
     packed_ref[...] = held_ref[0] + held_ref[1]
-    packed_ref[owners + 1 : owners + 2, 0 : 2 * owners] = jnp.concatenate(
-        [ends[0:1], ends[1:2]], 1
-    )
+    packed_ref[owners + 1 : owners + 2, 0 : 2 * owners] = ends
 
     def chunk(row, bucket, wide):
         for at in range(0, wide, 2):
@@ -401,9 +404,10 @@
         out_ref[pl.ds(9 + c, half, stride=18), :] = part[:, LANES:]
 
 
-def collect(ends_ref, vals_ref, first, number, held_ref):
+def collect(packed_ref, ends_ref, vals_ref, first, number, held_ref):
     owners = vals_ref.shape[0] // 9
-    base = owners * LANES - ends_ref[0, 2 * owners - 1]
+    totals = to_scalars(packed_ref[owners + 1 : owners + 2, 0 : 2 * owners], ends_ref)
+    base = owners * LANES - totals[1]
     held_ref[...] = jnp.zeros_like(held_ref)
     blank = jnp.zeros((8 - number, LANES), F32)
 
@@ -416,10 +420,11 @@
         held_ref[bucket, pl.ds(at, 1), :, :] = block[None]
 
     compact(owners, ends_ref, base, row_at, store)
-
-
-def collect_kernel(ends_ref, vals_ref, look_ref, held_ref):
-    collect(ends_ref, vals_ref, 5, 4, held_ref)
+    return totals
+
+
+def collect_kernel(packed_ref, vals_ref, look_ref, held_ref, ends_ref):
+    collect(packed_ref, ends_ref, vals_ref, 5, 4, held_ref)
     look_ref[...] = held_ref[0, :, 0:4, :] + held_ref[1, :, 0:4, :]
 
 
@@ -453,11 +458,10 @@
 
 
 def scatter_kernel(
-    ends_ref, ids_ref, vals_ref, look_vals_ref, geo_ref, look_acc_ref, acc_ref, held_ref
+    ids_ref, vals_ref, look_vals_ref, geo_ref, look_acc_ref, acc_ref, held_ref, ends_ref
 ):
     owners = vals_ref.shape[0] // 9
-    totals = ends_ref[0, owners - 1], ends_ref[0, 2 * owners - 1]
-    collect(ends_ref, vals_ref, 0, 5, held_ref)
+    totals = collect(ids_ref, ends_ref, vals_ref, 0, 5, held_ref)
     acc_ref[...] = jnp.zeros_like(acc_ref)
     values = [[(held_ref.at[bucket], 5), (look_vals_ref, 4)] for bucket in range(2)]
     add_chunks(ids_ref, values, totals, owners, acc_ref)
@@ -562,28 +566,31 @@
         compiler_params=LIMIT,
     )(pairs, places, cotangent[0], fetched)
     returned = exchange(outgoing, owners)
-    ends = packed[owners + 1 :]
     look_vals = pl.pallas_call(
         collect_kernel,
         out_shape=jax.ShapeDtypeStruct((owners + 1, 4, LANES), F32),
-        in_specs=[SMEM, VMEM],
+        in_specs=[VMEM, VMEM],
         out_specs=VMEM,
-        scratch_shapes=[pltpu.VMEM((2, owners + 1, 8, LANES), F32)],
+        scratch_shapes=[
+            pltpu.VMEM((2, owners + 1, 8, LANES), F32),
+            pltpu.SMEM((8, LANES), jnp.int32),
+        ],
         compiler_params=LIMIT,
-    )(ends, returned)
+    )(packed, returned)
     other_vals = [lax.ppermute(look_vals, "view", shift) for shift in shifts]
     sums = jax.ShapeDtypeStruct((2, 256, 4 * LOW), F32)
     geo, look = pl.pallas_call(
         scatter_kernel,
         out_shape=(jax.ShapeDtypeStruct((5, rows, LANES), F32), sums),
-        in_specs=[SMEM, VMEM, VMEM, VMEM],
+        in_specs=[VMEM, VMEM, VMEM],
         out_specs=(VMEM, VMEM),
         scratch_shapes=[
             pltpu.VMEM((2, 9 * LOW, 256), F32),
             pltpu.VMEM((2, owners + 1, 8, LANES), F32),
+            pltpu.SMEM((8, LANES), jnp.int32),
         ],
         compiler_params=LIMIT,
-    )(ends, packed, returned, look_vals)
+    )(packed, returned, look_vals)
     for i in reversed(range(views - 1)):
         last = i == 0
         look = pl.pallas_call(

time: 94.6 us -> 93.6 us (0.989)
  blocking collectives: 0 us -> 18.4 us
  waiting for transfers between devices: 32.9 us -> 15.7 us
  starting transfers between devices: 32.8 us -> 25.9 us
  Pallas kernels: 26.7 us -> 32.1 us
    all_to_all x0 -> x1, blocking collectives: none -> 18.4 us  [exchange(): got = lax.all_to_all(sent, axis, split_axis=0, concat_axis=0, tiled=True)]
    all_to_all x3 -> x2, waiting for transfers between devices: 28.6 us -> 13.8 us  [exchange(): got = lax.all_to_all(sent, axis, split_axis=0, concat_axis=0, tiled=True)]
    all_to_all x3 -> x2, starting transfers between devices: 24.2 us -> 17.4 us  [exchange(): got = lax.all_to_all(sent, axis, split_axis=0, concat_axis=0, tiled=True)]
    pallas_call x3, Pallas kernels: 4.05 us -> 7.01 us  [shards(): pl.pallas_call(finish_kernel if last else add_view, out_shape=jax.ShapeDt...]
    ppermute x3, waiting for transfers between devices: 2.59 us -> 0.01 us  [shards(): other_vals = [lax.ppermute(look_vals, 'view', shift) for shift in shifts]]
    pallas_call x1, Pallas kernels: 4.66 us -> 6.52 us  [shards(): pl.pallas_call(gather_kernel, out_shape=(jax.ShapeDtypeStruct((owners * 9...]
    pallas_call x1, Pallas kernels: 3.97 us -> 5.57 us  [shards(): pl.pallas_call(scatter_kernel, out_shape=(jax.ShapeDtypeStruct((5, rows,...]
  transfers between devices with their start and end apart: 9 -> 8, of which waited for: 7 -> 4; matrix products, arithmetic and copies ran while one was open for 1% -> 1% of each run, Pallas kernels for 7% -> 10%
where the time goes in v6:
time: 93.6 us; the launch traced here: 93.9 us
  Pallas kernels  32.1 us (34%)
  starting transfers between devices  25.9 us (28%)
  blocking collectives  18.4 us (20%)
  waiting for transfers between devices  15.7 us (17%)
  local copies, waits for them, and re-layouts  1.14 us (1%)
    all_to_all x1, blocking collectives, exchange(): got = lax.all_to_all(sent, axis, split_axis=0, concat_axis=0, tiled=True)  18.4 us
    all_to_all x2, starting transfers between devices, exchange(): got = lax.all_to_all(sent, axis, split_axis=0, concat_axis=0, tiled=True)  17.4 us
    all_to_all x2, waiting for transfers between devices, exchange(): got = lax.all_to_all(sent, axis, split_axis=0, concat_axis=0, tiled=True)  13.8 us
    pallas_call x1, Pallas kernels, shards(): pl.pallas_call(functools.partial(tile_kernel, (16, 8, 16)), out_shape=jax...  8.85 us
    pallas_call x3, Pallas kernels, shards(): pl.pallas_call(finish_kernel if last else add_view, out_shape=jax.ShapeDt...  7.01 us
    pallas_call x1, Pallas kernels, shards(): pl.pallas_call(gather_kernel, out_shape=(jax.ShapeDtypeStruct((owners * 9...  6.52 us
    pallas_call x1, Pallas kernels, shards(): pl.pallas_call(scatter_kernel, out_shape=(jax.ShapeDtypeStruct((5, rows,...  5.57 us
    ppermute x3, starting transfers between devices, shards(): other_ids = [lax.ppermute(packed, 'view', shift) for shift in shifts]  4.9 us
  transfers between devices with their start and end apart: 8, of which 4 were waited for; matrix products, arithmetic and copies ran while one was open for 1% of the time, Pallas kernels for 10%

profile of v6, /device:TPU:1, one launch (start us, length us, event | category | flops | bytes accessed | tf_op | source)
XLA Modules:
  0.0 93.9 jit_solution(4248643912119946124)
XLA Ops:
  0.6 0.0 copy-start
  0.6 2.7 %shard_map.77 = (s32[64,128]{1,0:T(8,128)}, s32[16,256]{1,0:T(8,128)}, s32[16,256]{1,0:T(8,128)}) custom-call(s32[1,16]{1,0:T(1,128)} %counts_hbm.1, s32[1,4096]{1,0:T(1,128)} %bitcast.32, s32[1,4096]{1,0:T(1,128)} %local_hbm.1), custom_call_target="tpu_custom_call" | custom-call | tf_op jit(solution)/shard_map/pallas_call | solution.py:509
  3.3 13.2 %all-to-all-start = ((s32[64,1,128]{2,1,0:T(1,128)}), s32[64,1,128]{2,1,0:T(1,128)S(1)}, u32[]{:S(2)}, u32[]{:S(2)}) async-start(s32[64,1,128]{2,1,0:T(1,128)} %bitcast.31), calls=%async_computation | async-start | bytes 65536 | tf_op jit(solution)/shard_map/all_to_all | solution.py:498
  16.5 1.1 %copy.20 = f32[1,4,256,128]{3,2,1,0:T(8,128)S(1)} copy(f32[1,4,256,128]{3,1,2,0:T(4,128)} %bitcast.30) | data formatting | bytes 1048576
  17.6 0.0 copy-done
  17.6 0.4 shard_map.78.table_ref
  17.9 0.0 copy-start.3
  18.0 0.0 copy-start.1
  18.0 0.0 copy-start.2
  18.0 7.8 %all-to-all-done = s32[64,1,128]{2,1,0:T(1,128)S(1)} async-done(((s32[64,1,128]{2,1,0:T(1,128)}), s32[64,1,128]{2,1,0:T(1,128)S(1)}, u32[]{:S(2)}, u32[]{:S(2)}) %all-to-all-start) | async-done | bytes 32800 | tf_op jit(solution)/shard_map/all_to_all | solution.py:498
  25.8 6.5 %shard_map.79 = (f32[576,128]{1,0:T(8,128)}, s32[72,128]{1,0:T(8,128)S(1)}) custom-call(s32[64,128]{1,0:T(8,128)S(1)} %bitcast.28, bf16[2,576,512]{2,1,0:T(8,128)(2,1)S(1)} %shard_map.78.table_ref), custom_call_target="tpu_custom_call" | custom-call | tf_op jit(solution)/shard_map/pallas_call | solution.py:534
  32.3 4.2 %all-to-all-start.1 = ((f32[64,1,1152]{2,1,0:T(1,128)}), f32[64,1,1152]{2,1,0:T(1,128)S(1)}, u32[]{:S(2)}, u32[]{:S(2)}) async-start(f32[64,1,1152]{2,1,0:T(1,128)} %bitcast.6), calls=%async_computation.1 | async-start | bytes 589824 | tf_op jit(solution)/shard_map/all_to_all | solution.py:498
  36.5 0.8 collective-permute-start
  37.3 2.9 %collective-permute-start.1 = (s32[72,128]{1,0:T(8,128)S(1)}, s32[72,128]{1,0:T(8,128)S(1)}, u32[]{:S(2)}, u32[]{:S(2)}) collective-permute-start(s32[72,128]{1,0:T(8,128)S(1)} %get-tuple-element.14.packed_ref.ids_ref), channel_id=1, source_target_pairs={{0,2},{1,3},{2,0},{3,1},{4,6},{5,7},{6,4},{7,5},{8,10},{9,11},{10,... | collective-permute-start | bytes 110600 | tf_op jit(solution)/shard_map/ppermute | solution.py:551
  40.2 1.2 %collective-permute-start.2 = (s32[72,128]{1,0:T(8,128)S(1)}, s32[72,128]{1,0:T(8,128)S(1)}, u32[]{:S(2)}, u32[]{:S(2)}) collective-permute-start(s32[72,128]{1,0:T(8,128)S(1)} %get-tuple-element.14.packed_ref.ids_ref), channel_id=1, source_target_pairs={{0,3},{1,0},{2,1},{3,2},{4,7},{5,4},{6,5},{7,6},{8,11},{9,8},{10,9... | collective-permute-start | bytes 110600 | tf_op jit(solution)/shard_map/ppermute | solution.py:551
  41.4 0.0 copy-done.3
  41.4 0.0 collective-permute-done.ids_ref
  41.5 1.6 %collective-permute-done.1.ids_ref = s32[72,128]{1,0:T(8,128)S(1)} collective-permute-done((s32[72,128]{1,0:T(8,128)S(1)}, s32[72,128]{1,0:T(8,128)S(1)}, u32[]{:S(2)}, u32[]{:S(2)}) %collective-permute-start.1) | collective-permute-done | bytes 36896 | tf_op jit(solution)/shard_map/ppermute | solution.py:551
  43.0 0.3 collective-permute-done.2.ids_ref
  43.3 6.0 %all-to-all-done.1 = f32[64,1,1152]{2,1,0:T(1,128)S(1)} async-done(((f32[64,1,1152]{2,1,0:T(1,128)}), f32[64,1,1152]{2,1,0:T(1,128)S(1)}, u32[]{:S(2)}, u32[]{:S(2)}) %all-to-all-start.1) | async-done | bytes 294944 | tf_op jit(solution)/shard_map/all_to_all | solution.py:498
  49.3 0.0 copy-done.1
  49.3 0.0 copy-done.2
  49.3 8.8 %shard_map.80 = f32[576,128]{1,0:T(8,128)S(1)} custom-call(s32[16,256]{1,0:T(8,128)S(1)} %copy-done.1, s32[16,256]{1,0:T(8,128)S(1)} %copy-done.2, f32[16,3,256]{2,1,0:T(4,128)S(1)} %bitcast.27, f32[576,128]{1,0:T(8,128)S(1)} %bitcast.24), custom_call_target="tpu_custom_call" | custom-call | tf_op jit(solution)/shard_map/pallas_call | solution.py:553
  58.2 18.4 %all_to_all.15 = f32[64,1,1152]{2,1,0:T(1,128)S(1)} all-to-all(f32[64,1,1152]{2,1,0:T(1,128)S(1)} %bitcast.25), channel_id=1, replica_groups=mesh['owner'=64,'view'=4] {'owner'}, dimensions={0} | all-to-all | bytes 589824 | tf_op jit(solution)/shard_map/all_to_all | solution.py:498
  76.6 1.1 %shard_map.81.look_vals_ref = f32[65,4,128]{2,1,0:T(4,128)S(1)} custom-call(s32[72,128]{1,0:T(8,128)S(1)} %get-tuple-element.14.packed_ref.ids_ref, f32[576,128]{1,0:T(8,128)S(1)} %bitcast.21), custom_call_target="tpu_custom_call" | custom-call | tf_op jit(solution)/shard_map/pallas_call | solution.py:569
  77.6 2.6 %collective-permute-start.5 = (f32[65,4,128]{2,1,0:T(4,128)S(1)}, f32[65,4,128]{2,1,0:T(4,128)S(1)}, u32[]{:S(2)}, u32[]{:S(2)}) collective-permute-start(f32[65,4,128]{2,1,0:T(4,128)S(1)} %shard_map.81.look_vals_ref), channel_id=1, source_target_pairs={{0,3},{1,0},{2,1},{3,2},{4,7},{5,4},{6,5},{7,6},{8,11},{9,8},{10,9... | collective-permute-start | bytes 399368 | tf_op jit(solution)/shard_map/ppermute | solution.py:580
  80.2 0.5 collective-permute-start.4
  80.7 0.6 collective-permute-start.3
  81.3 5.6 %shard_map.82 = (f32[5,256,128]{2,1,0:T(8,128)}, f32[2,256,256]{2,1,0:T(8,128)S(1)}) custom-call(s32[72,128]{1,0:T(8,128)S(1)} %get-tuple-element.14.packed_ref.ids_ref, f32[576,128]{1,0:T(8,128)S(1)} %bitcast.22, f32[65,4,128]{2,1,0:T(4,128)S(1)} %shard_map.81.look_vals_ref), custom_call_target="tpu_custom_call" | custom-call | tf_op jit(solution)/shard_map/pallas_call | solution.py:582
  86.9 0.0 collective-permute-done.5.vals_ref
  86.9 1.9 %shard_map.83.start_ref = f32[2,256,256]{2,1,0:T(8,128)S(1)} custom-call(s32[72,128]{1,0:T(8,128)S(1)} %collective-permute-done.2.ids_ref, f32[65,4,128]{2,1,0:T(4,128)S(1)} %collective-permute-done.5.vals_ref, f32[2,256,256]{2,1,0:T(8,128)S(1)} %get-tuple-element.23.start_ref), custom_call_target="tpu_custom_call" | custom-call | tf_op jit(solution)/shard_map/pallas_call | solution.py:596
  88.8 0.0 collective-permute-done.4.vals_ref
  88.8 2.0 %shard_map.84.start_ref = f32[2,256,256]{2,1,0:T(8,128)S(1)} custom-call(s32[72,128]{1,0:T(8,128)S(1)} %collective-permute-done.1.ids_ref, f32[65,4,128]{2,1,0:T(4,128)S(1)} %collective-permute-done.4.vals_ref, f32[2,256,256]{2,1,0:T(8,128)S(1)} %shard_map.83.start_ref), custom_call_target="tpu_custom_call" | custom-call | tf_op jit(solution)/shard_map/pallas_call | solution.py:596
  90.8 0.0 collective-permute-done.3.vals_ref
  90.8 3.2 %shard_map.85 = f32[256,4,128]{2,1,0:T(4,128)} custom-call(s32[72,128]{1,0:T(8,128)S(1)} %collective-permute-done.ids_ref, f32[65,4,128]{2,1,0:T(4,128)S(1)} %collective-permute-done.3.vals_ref, f32[2,256,256]{2,1,0:T(8,128)S(1)} %shard_map.84.start_ref), custom_call_target="tpu_custom_call" | custom-call | tf_op jit(solution)/shard_map/pallas_call | solution.py:596
  (1 shorter events, 0.0 us)
Async XLA Ops:
  0.6 16.9 %copy-start = (f32[1,5,32768]{2,0,1:T(1,128)S(1)}, f32[1,5,32768]{2,0,1:T(1,128)}, u32[]{:S(2)}) copy-start(f32[1,5,32768]{2,0,1:T(1,128)} %param.6) | copy-start | bytes 1966084
  3.3 22.5 %all-to-all-start = ((s32[64,1,128]{2,1,0:T(1,128)}), s32[64,1,128]{2,1,0:T(1,128)S(1)}, u32[]{:S(2)}, u32[]{:S(2)}) async-start(s32[64,1,128]{2,1,0:T(1,128)} %bitcast.31), calls=%async_computation | async-start | bytes 65536 | tf_op jit(solution)/shard_map/all_to_all | solution.py:498
  17.9 23.5 %copy-start.3 = (f32[1,16,3,256]{3,1,2,0:T(8,128)S(1)}, f32[1,16,3,256]{3,1,2,0:T(8,128)}, u32[]{:S(2)}) copy-start(f32[1,16,3,256]{3,1,2,0:T(8,128)} %param.11) | copy-start | bytes 147460
  18.0 31.4 %copy-start.1 = (s32[16,256]{1,0:T(8,128)S(1)}, s32[16,256]{1,0:T(8,128)}, u32[]{:S(2)}) copy-start(s32[16,256]{1,0:T(8,128)} %get-tuple-element.15.pair_ref) | copy-start | bytes 49156
  18.0 31.4 %copy-start.2 = (s32[16,256]{1,0:T(8,128)S(1)}, s32[16,256]{1,0:T(8,128)}, u32[]{:S(2)}) copy-start(s32[16,256]{1,0:T(8,128)} %get-tuple-element.16.place_ref) | copy-start | bytes 49156
  32.3 17.0 %all-to-all-start.1 = ((f32[64,1,1152]{2,1,0:T(1,128)}), f32[64,1,1152]{2,1,0:T(1,128)S(1)}, u32[]{:S(2)}, u32[]{:S(2)}) async-start(f32[64,1,1152]{2,1,0:T(1,128)} %bitcast.6), calls=%async_computation.1 | async-start | bytes 589824 | tf_op jit(solution)/shard_map/all_to_all | solution.py:498
  36.5 4.9 %collective-permute-start = (s32[72,128]{1,0:T(8,128)S(1)}, s32[72,128]{1,0:T(8,128)S(1)}, u32[]{:S(2)}, u32[]{:S(2)}) collective-permute-start(s32[72,128]{1,0:T(8,128)S(1)} %get-tuple-element.14.packed_ref.ids_ref), channel_id=1, source_target_pairs={{0,1},{1,2},{2,3},{3,0},{4,5},{5,6},{6,7},{7,4},{8,9},{9,10},{10,1... | collective-permute-start | bytes 110600 | tf_op jit(solution)/shard_map/ppermute | solution.py:551
  37.3 5.7 %collective-permute-start.1 = (s32[72,128]{1,0:T(8,128)S(1)}, s32[72,128]{1,0:T(8,128)S(1)}, u32[]{:S(2)}, u32[]{:S(2)}) collective-permute-start(s32[72,128]{1,0:T(8,128)S(1)} %get-tuple-element.14.packed_ref.ids_ref), channel_id=1, source_target_pairs={{0,2},{1,3},{2,0},{3,1},{4,6},{5,7},{6,4},{7,5},{8,10},{9,11},{10,... | collective-permute-start | bytes 110600 | tf_op jit(solution)/shard_map/ppermute | solution.py:551
  40.2 3.1 %collective-permute-start.2 = (s32[72,128]{1,0:T(8,128)S(1)}, s32[72,128]{1,0:T(8,128)S(1)}, u32[]{:S(2)}, u32[]{:S(2)}) collective-permute-start(s32[72,128]{1,0:T(8,128)S(1)} %get-tuple-element.14.packed_ref.ids_ref), channel_id=1, source_target_pairs={{0,3},{1,0},{2,1},{3,2},{4,7},{5,4},{6,5},{7,6},{8,11},{9,8},{10,9... | collective-permute-start | bytes 110600 | tf_op jit(solution)/shard_map/ppermute | solution.py:551
  77.6 9.3 %collective-permute-start.5 = (f32[65,4,128]{2,1,0:T(4,128)S(1)}, f32[65,4,128]{2,1,0:T(4,128)S(1)}, u32[]{:S(2)}, u32[]{:S(2)}) collective-permute-start(f32[65,4,128]{2,1,0:T(4,128)S(1)} %shard_map.81.look_vals_ref), channel_id=1, source_target_pairs={{0,3},{1,0},{2,1},{3,2},{4,7},{5,4},{6,5},{7,6},{8,11},{9,8},{10,9... | collective-permute-start | bytes 399368 | tf_op jit(solution)/shard_map/ppermute | solution.py:580
  80.2 8.6 %collective-permute-start.4 = (f32[65,4,128]{2,1,0:T(4,128)S(1)}, f32[65,4,128]{2,1,0:T(4,128)S(1)}, u32[]{:S(2)}, u32[]{:S(2)}) collective-permute-start(f32[65,4,128]{2,1,0:T(4,128)S(1)} %shard_map.81.look_vals_ref), channel_id=1, source_target_pairs={{0,2},{1,3},{2,0},{3,1},{4,6},{5,7},{6,4},{7,5},{8,10},{9,11},{10,... | collective-permute-start | bytes 399368 | tf_op jit(solution)/shard_map/ppermute | solution.py:580
  80.7 10.1 %collective-permute-start.3 = (f32[65,4,128]{2,1,0:T(4,128)S(1)}, f32[65,4,128]{2,1,0:T(4,128)S(1)}, u32[]{:S(2)}, u32[]{:S(2)}) collective-permute-start(f32[65,4,128]{2,1,0:T(4,128)S(1)} %shard_map.81.look_vals_ref), channel_id=1, source_target_pairs={{0,1},{1,2},{2,3},{3,0},{4,5},{5,6},{6,7},{7,4},{8,9},{9,10},{10,1... | collective-permute-start | bytes 399368 | tf_op jit(solution)/shard_map/ppermute | solution.py:580
